TPU v7x, 32 devices: a whole 2x2x4 slice. The times are simulated.
32 devices in a mesh: seq: 16 (over z, x, core), head: 2 (over y).
Axes of the slice: x: 2, y: 2, z: 4, core: 2. Of those that a mesh axis runs over, the one named last changes fastest.
Arguments:
- tokens: bfloat16 [8192, 1024], P(('seq', 'head')), may hold values from -6 to 6
- w_query: bfloat16 [1024, 1024], P(None, 'head'), may hold values from -0.1875 to 0.1875
- w_key: bfloat16 [1024, 1024], P(None, 'head'), may hold values from -0.1875 to 0.1875
- w_value: bfloat16 [1024, 1024], P(None, 'head'), may hold values from -0.1875 to 0.1875
- w_beta: bfloat16 [1024, 8], P(None, 'head'), may hold values from -0.09375 to 0.09375
- beta_bias: float32 [8], P('head'), may hold values from -1 to 3, as said below
- conv_weight: float32 [3, 4, 1024], P(None, None, 'head'), may hold values from -3 to 3
- norm_gain: float32 [1024], P('head'), may hold values from 0.1 to 1.9
- w_out: bfloat16 [1024, 1024], P('head'), may hold values from -0.1875 to 0.1875
Outputs:
- mixed: bfloat16 [8192, 1024], P(('seq', 'head'))
Inputs may be any that keep to these rules, and one draw needn't show every extreme that they name: `beta_bias`: one logit offset per head.
All inputs are finite; a program needn't handle non-finite values.
Results may differ from a plain program's by a relative error of at most 0.015.
The roundings to bfloat16 on the way count: a program that leaves them out, or rounds other values in their place, can miss the bound.
Values may be sent and summed in bfloat16 or wider, within the bound.
No kernel may reach another device: no remote copies, remote signals or barrier semaphores. Data moves between devices by JAX's collectives and lax.ppermute only.
A program may use at most 64 MiB of HBM per device.

v0:
```python
import jax
import jax.numpy as jnp
from jax import lax
from jax.sharding import PartitionSpec as P

SPAN = 64


precise = lax.Precision.HIGHEST


def from_behind(shard, axis, by):
    length = lax.axis_size(axis)
    pairs = [(i, i + by) for i in range(length) if 0 <= i + by < length]
    return lax.ppermute(shard, axis, pairs)


def compose(earlier_pair, later_pair):
    first_part = jnp.einsum("hij,hjk->hik", earlier_pair[0], later_pair[0], precision=precise)
    second = (
        jnp.einsum("hij,hjk->hik", earlier_pair[1], later_pair[0], precision=precise)
        + later_pair[1]
    )
    return (first_part, second)


def absorb(pair_sofar, block_in):
    return (compose(pair_sofar, block_in), None)


def local(tokens, w_query, w_key, w_value, w_beta, beta_bias, conv_weight, norm_gain, w_out):
    gathered = lax.all_gather(tokens, "head", axis=0, tiled=True)
    length = gathered.shape[0]
    heads_here = beta_bias.shape[0]
    head_width = w_query.shape[1]
    head_dim = head_width // heads_here
    tap_count = conv_weight.shape[1]
    joined = jnp.concatenate([w_query, w_key, w_value], 1)
    projected = jnp.dot(gathered, joined, preferred_element_type=jnp.float32).astype(jnp.bfloat16)
    logits = jnp.dot(gathered, w_beta, preferred_element_type=jnp.float32) + beta_bias
    beta_rate = 2.0 * jax.nn.sigmoid(logits)
    earlier = from_behind(projected[length - (tap_count - 1) :], "seq", 1)
    padded = jnp.concatenate([earlier, projected], 0).astype(jnp.float32)
    taps_weight = jnp.transpose(conv_weight, (1, 0, 2)).reshape(tap_count, 3 * head_width)
    mixed_conv = padded[0:length] * taps_weight[0]
    for offset in range(1, tap_count):
        mixed_conv = mixed_conv + padded[offset : offset + length] * taps_weight[offset]
    activated = jax.nn.silu(mixed_conv).astype(jnp.bfloat16)
    blocks = length // SPAN

    def arrange(columns_in):
        shaped = columns_in.reshape(blocks, SPAN, heads_here, head_dim)
        return jnp.transpose(shaped, (0, 2, 1, 3)).astype(jnp.float32)

    queries = arrange(activated[:, :head_width])
    keys_raw = arrange(activated[:, head_width : 2 * head_width])
    values_in = arrange(activated[:, 2 * head_width :])
    keys_unit = keys_raw / jnp.sqrt(jnp.sum(keys_raw * keys_raw, -1, keepdims=True) + 1e-06)
    block_rates = jnp.transpose(beta_rate.reshape(blocks, SPAN, heads_here), (0, 2, 1))
    key_gram = jnp.einsum("nhcd,nhed->nhce", keys_unit, keys_unit, precision=precise)
    query_gram = jnp.einsum("nhcd,nhed->nhce", queries, keys_unit, precision=precise)
    row_index = lax.broadcasted_iota(jnp.int32, (SPAN, SPAN), 0)
    col_index = lax.broadcasted_iota(jnp.int32, (SPAN, SPAN), 1)
    strict_lower = (row_index > col_index).astype(jnp.float32)
    lower_incl = (row_index >= col_index).astype(jnp.float32)
    system = jnp.eye(SPAN, dtype=jnp.float32) + block_rates[..., :, None] * key_gram * strict_lower
    right_sides = block_rates[..., None] * jnp.concatenate([keys_unit, values_in], -1)
    solved = lax.linalg.triangular_solve(
        system, right_sides, left_side=True, lower=True, unit_diagonal=True
    )
    weights_k = solved[..., :head_dim]
    fresh_values = solved[..., head_dim:]
    transit = jnp.eye(head_dim, dtype=jnp.float32) - jnp.einsum(
        "nhca,nhcb->nhab", weights_k, keys_unit, precision=precise
    )
    landed = jnp.einsum("nhcv,nhcb->nhvb", fresh_values, keys_unit, precision=precise)
    eye_heads = jnp.broadcast_to(
        jnp.eye(head_dim, dtype=jnp.float32), (heads_here, head_dim, head_dim)
    )
    empty_state = jnp.zeros((heads_here, head_dim, head_dim), jnp.float32)
    shard_pair = lax.scan(absorb, (eye_heads, empty_state), (transit, landed))[0]
    every_pair = (
        lax.all_gather(shard_pair[0][None], "seq", axis=0, tiled=True),
        lax.all_gather(shard_pair[1][None], "seq", axis=0, tiled=True),
    )

    def step_over(position, carried):
        moved = lax.dynamic_index_in_dim(every_pair[0], position, 0, keepdims=False)
        placed = lax.dynamic_index_in_dim(every_pair[1], position, 0, keepdims=False)
        return jnp.einsum("hij,hjk->hik", carried, moved, precision=precise) + placed

    entering = lax.fori_loop(0, lax.axis_index("seq"), step_over, empty_state)

    def emit_block(carried, block_in):
        query_b, key_b, weight_b, fresh_b, qgram_b = block_in
        update = fresh_b - jnp.einsum("hca,hva->hcv", weight_b, carried, precision=precise)
        output = jnp.einsum("hca,hva->hcv", query_b, carried, precision=precise)
        output = output + jnp.einsum(
            "hce,hev->hcv", qgram_b * lower_incl, update, precision=precise
        )
        carried = carried + jnp.einsum("hcv,hcb->hvb", update, key_b, precision=precise)
        return (carried, output)

    outputs = lax.scan(
        emit_block, entering, (queries, keys_unit, weights_k, fresh_values, query_gram)
    )[1]
    ordered = jnp.transpose(outputs, (0, 2, 1, 3)).reshape(length, heads_here, head_dim)
    gain_rows = norm_gain.reshape(heads_here, head_dim)
    scaled = ordered * lax.rsqrt(jnp.mean(ordered * ordered, -1, keepdims=True) + 1e-05) * gain_rows
    normed = scaled.astype(jnp.bfloat16).reshape(length, head_width)
    product = jnp.dot(normed, w_out, preferred_element_type=jnp.float32)
    return lax.psum_scatter(
        lax.optimization_barrier(product.astype(jnp.bfloat16))
        .astype(jnp.float32)
        .astype(jnp.bfloat16),
        "head",
        scatter_dimension=0,
        tiled=True,
    )


def solution(mesh):
    in_specs = (
        P(("seq", "head"), None),
        P(None, "head"),
        P(None, "head"),
        P(None, "head"),
        P(None, "head"),
        P("head"),
        P(None, None, "head"),
        P("head"),
        P("head", None),
    )
    out_specs = P(("seq", "head"), None)
    return jax.shard_map(local, mesh=mesh, in_specs=in_specs, out_specs=out_specs, check_vma=False)
```

profile of v0, /device:TPU:0, one launch (start us, length us, event | category | flops | bytes accessed | tf_op | source)
XLA Modules:
  0.0 470.6 jit_solution(5248688421887342080)
XLA Ops:
  9.8 23.2 %all-gather.6.cloned.1.call-done = bf16[512,1024]{1,0:T(8,128)(2,1)} async-done(((bf16[256,1024]{1,0:T(8,128)(2,1)}), bf16[512,1024]{1,0:T(8,128)(2,1)}) %all-gather.6.cloned.1.call-update) | async-done | bytes 1048592 | tf_op jit(solution)/shard_map/all_gather | solution.py:32
  32.9 4.0 fusion.45
  38.2 1.7 collective-permute-start
  40.7 1.9 maximum_convert_fusion
  42.6 1.9 multiply_convert_fusion
  47.2 1.8 fusion.55
  49.0 158.0 %custom-call.3 = f32[8,4,1,64,64]{3,4,2,1,0:T(8,128)} custom-call(f32[8,4,1,64,64]{4,3,2,1,0:T(8,128)S(1)} %fusion.55), custom_call_target="InvertDiagBlocksLowerTriangular" | custom-call | tf_op jit(solution)/shard_map/triangular_solve | solution.py:68
  207.0 1.6 reshape.89
  208.7 3.5 fusion.48
  212.2 4.8 %fusion.79 = f32[8,4,128,128]{2,3,1,0:T(8,128)} fusion(f32[8,4,64,128]{3,2,1,0:T(8,128)S(1)} %bitcast_divide_fusion, f32[8,4,64,256]{3,2,1,0:T(8,128)S(1)} %fusion.48), kind=kOutput, calls=%fused_computation.114 | convolution fusion | flops 402653184 | bytes 4194304 | tf_op jit(solution)/shard_map/nhcv,nhcb->nhvb/dot_general | solution.py:76
  217.0 4.9 %convolution_subtract_fusion.1 = f32[8,4,128,128]{3,2,1,0:T(8,128)} fusion(f32[8,4,64,128]{3,2,1,0:T(8,128)S(1)} %bitcast_divide_fusion, f32[128,128]{1,0:T(8,128)S(1)} %fusion.71, f32[8,4,64,256]{3,2,1,0:T(8,128)S(1)} %fusion.48), kind=kOutput, calls=%fused_computation.61 | convolution fusion | flops 403177472 | bytes 4259840 | tf_op jit(solution)/shard_map/nhca,nhcb->nhab/dot_general | solution.py:73
  221.9 26.3 %while.38 = (s32[]{:T(128)}, f32[4,128,128]{1,2,0:T(8,128)S(1)}, f32[4,128,128]{1,2,0:T(8,128)S(1)}, f32[8,4,128,128]{3,2,1,0:T(8,128)}, f32[8,4,128,128]{2,3,1,0:T(8,128)}, /*index=5*/s32[]{:T(128)}, s32[]{:T(128)}) while((s32[]{:T(128)}, f32[4,128,128]{1,2,0:T(8,128)S(1)}, f32[4,128,128]{1,2,0:T(8,128)S(1)}, ...), condition=%wide.region_2.3_spmd.clone, body=%wide.region_1.2_spmd.clone.sunk | while | flops 201457664 | bytes 2885207 | solution.py:81
  221.9 1.7 fusion.134
  223.7 1.6 convolution_bitcast_fusion.4
  225.3 1.6 fusion.134
  226.9 1.6 convolution_bitcast_fusion.4
  228.5 1.6 fusion.134
  230.2 1.6 convolution_bitcast_fusion.4
  231.8 1.6 fusion.134
  235.1 1.6 fusion.134
  238.4 1.6 fusion.134
  241.6 1.6 fusion.134
  244.9 1.6 fusion.134
  251.5 2.0 fusion.67
  253.4 1.6 fusion.82
  255.1 47.1 %all-gather.8.cloned.1.call-done = f32[64,128,128]{2,1,0:T(8,128)} async-done(((f32[4,128,128]{2,1,0:T(8,128)}), f32[64,128,128]{2,1,0:T(8,128)}) %all-gather.8.cloned.1.call-update) | async-done | bytes 4194320 | tf_op jit(solution)/shard_map/all_gather | solution.py:83
  302.2 51.3 %all-gather.10.cloned.1.call-done = f32[64,128,128]{2,1,0:T(8,128)} async-done(((f32[4,128,128]{2,1,0:T(8,128)}), f32[64,128,128]{2,1,0:T(8,128)}) %all-gather.10.cloned.1.call-update) | async-done | bytes 4194320 | tf_op jit(solution)/shard_map/all_gather | solution.py:84
  353.6 44.7 %while.37 = (s32[]{:T(128)}, f32[4,128,128]{2,1,0:T(8,128)S(1)}, f32[8,4,64,128]{3,2,1,0:T(8,128)}, f32[8,4,64,128]{3,2,1,0:T(8,128)}, f32[8,4,64,128]{3,2,1,0:T...) while((s32[]{:T(128)}, f32[4,128,128]{2,1,0:T(8,128)S(1)}, ...), condition=%wide.region_6.7_spmd.clone, body=%wide.region_5.6_spmd.clone.sunk | while | flops 176316416 | bytes 2525793 | solution.py:104
  353.6 1.6 convolution_subtract_fusion.3
  356.4 2.2 fusion.129
  359.2 1.6 convolution_subtract_fusion.3
  362.0 2.2 fusion.129
  364.8 1.6 convolution_subtract_fusion.3
  367.6 2.2 fusion.129
  370.4 1.6 convolution_subtract_fusion.3
  373.2 2.2 fusion.129
  376.0 1.6 convolution_subtract_fusion.3
  378.7 2.2 fusion.129
  381.5 1.6 convolution_subtract_fusion.3
  384.3 2.2 fusion.129
  387.1 1.6 convolution_subtract_fusion.3
  389.9 2.2 fusion.129
  392.7 1.6 convolution_subtract_fusion.3
  395.5 2.2 fusion.129
  398.3 1.6 multiply_reduce_fusion
  400.0 1.9 copy.87
  402.6 1.7 convolution_convert_fusion
  404.3 59.8 %reduce-scatter.2.cloned.1.call-done = bf16[256,1024]{1,0:T(8,128)(2,1)} async-done(((bf16[512,1024]{1,0:T(8,128)(2,1)}), bf16[256,1024]{1,0:T(8,128)(2,1)}) %reduce-scatter.2.cloned.1.call-update) | async-done | bytes 524304 | tf_op jit(solution)/shard_map/reduce_scatter | solution.py:112
  (113 shorter events, 34.4 us)
Async XLA Ops:
  6.5 396.0 %copy-start = (bf16[512,1024]{1,0:T(8,128)(2,1)S(1)}, bf16[512,1024]{1,0:T(8,128)(2,1)}, u32[]{:S(2)}) copy-start(bf16[512,1024]{1,0:T(8,128)(2,1)} %param.23) | copy-start | bytes 3145732
  6.5 26.4 %all-gather.6.cloned.1.call-start = ((), (), s32[]{:S(2)}) async-start(), calls=%async_computation.1 | async-start | bytes 1572864 | tf_op jit(solution)/shard_map/all_gather | solution.py:32
  7.3 294.9 %all-gather.8.cloned.1.call-start = ((), (), s32[]{:S(2)}) async-start(), calls=%async_computation.3 | async-start | bytes 4456448 | tf_op jit(solution)/shard_map/all_gather | solution.py:83
  9.8 30.2 %copy-start.10 = (bf16[1024,4]{0,1:T(4,128)(2,1)S(1)}, bf16[1024,4]{0,1:T(4,128)(2,1)}, u32[]{:S(2)}) copy-start(bf16[1024,4]{0,1:T(4,128)(2,1)} %param.19) | copy-start | bytes 24580
  9.8 30.2 %copy-start.12 = (f32[4]{0:T(128)S(1)}, f32[4]{0:T(128)}, u32[]{:S(2)}) copy-start(f32[4]{0:T(128)} %param.20) | copy-start | bytes 52
  32.9 7.0 %copy-start.5 = (bf16[512,1024]{1,0:T(8,128)(2,1)S(1)}, bf16[512,1024]{1,0:T(8,128)(2,1)}, u32[]{:S(2)}) copy-start(bf16[512,1024]{1,0:T(8,128)(2,1)} %all-gather.6.cloned.1.call-done) | copy-start | bytes 3145732
  37.0 1.2 copy-start.4
  38.2 2.6 collective-permute-start
  46.4 0.8 copy-start.6
  46.4 0.8 copy-start.7
  46.4 0.8 copy-start.8
  46.4 0.8 copy-start.9
  212.2 9.6 %copy-start.1 = (f32[8,4,64,256]{3,2,1,0:T(8,128)}, f32[8,4,64,256]{3,2,1,0:T(8,128)S(1)}, u32[]{:S(2)}) copy-start(f32[8,4,64,256]{3,2,1,0:T(8,128)S(1)} %fusion.48) | copy-start | bytes 6291460
  221.9 28.3 %copy-start.3 = (bf16[512,512]{1,0:T(8,128)(2,1)S(1)}, bf16[512,512]{1,0:T(8,128)(2,1)}, u32[]{:S(2)}) copy-start(bf16[512,512]{1,0:T(8,128)(2,1)} %get-tuple-element.270) | copy-start | bytes 1572868
  249.0 104.4 %all-gather.10.cloned.1.call-start = ((), (), s32[]{:S(2)}) async-start(), calls=%async_computation.4 | async-start | bytes 4456448 | tf_op jit(solution)/shard_map/all_gather | solution.py:84
  249.9 214.2 %reduce-scatter.2.cloned.1.call-start = ((), (), s32[]{:S(2)}) async-start(), calls=%async_computation.2 | async-start | bytes 1572864 | tf_op jit(solution)/shard_map/reduce_scatter | solution.py:112
  250.4 3.1 copy-start.2
  398.3 4.3 copy-start.11
Sparse Core Ops, SparseCore 0:
  8.9 23.9 all-gather.5
  249.1 52.9 all-gather.7
  304.3 49.0 all-gather.9
  404.4 59.6 reduce-scatter.1
where the time goes:
time: 473 us; the launch traced here: 471 us
  waiting for transfers between devices  182 us (38%)
  other arithmetic  168 us (36%)
  matrix products  92.8 us (20%)
  between operations  13.5 us (3%)
  local copies, waits for them, and re-layouts  11 us (2%)
    another operation x3, other arithmetic, local(): lax.linalg.triangular_solve(system, right_sides, left_side=True, lower=Tr...  159 us
    reduce_scatter x1, waiting for transfers between devices, local(): lax.psum_scatter(lax.optimization_barrier(product.astype(jnp.bfloat16)).a...  59.8 us
    all_gather x1, waiting for transfers between devices, local(): lax.all_gather(shard_pair[1][None], 'seq', axis=0, tiled=True)  51.3 us
    all_gather x1, waiting for transfers between devices, local(): lax.all_gather(shard_pair[0][None], 'seq', axis=0, tiled=True)  47.1 us
    all_gather x1, waiting for transfers between devices, local(): gathered = lax.all_gather(tokens, 'head', axis=0, tiled=True)  23.2 us
    dot_general x8, matrix products, emit_block(): output = jnp.einsum('hca,hva->hcv', query_b, carried, precision=precise)  17.4 us
    dot_general x8, matrix products, compose(): jnp.einsum('hij,hjk->hik', earlier_pair[1], later_pair[0], precision=prec...  13.1 us
    dot_general x8, matrix products, emit_block(): jnp.einsum('hca,hva->hcv', weight_b, carried, precision=precise)  12.6 us
  transfers between devices with their start and end apart: 5, of which 5 were waited for; matrix products, arithmetic and copies ran while one was open for 2% of the time, Pallas kernels for 0%

commit v1 on v0

v1 whole, which is shorter than its diff:
```python
import functools

import jax
import jax.numpy as jnp
from jax import lax
from jax.experimental import pallas as pl
from jax.experimental.pallas import tpu as pltpu
from jax.sharding import PartitionSpec as P

BASE = 32
HALO = 16
F32 = jnp.float32
BF16 = jnp.bfloat16
VMEM = pl.BlockSpec(memory_space=pltpu.VMEM)
NN = ((1,), (0,))
NT = ((1,), (1,))
TN = ((0,), (0,))


def dot(left, right, dims=NN):
    return lax.dot_general(left, right, (dims, ((), ())), preferred_element_type=F32)


def split(wide):
    top = wide.astype(BF16)
    return top, (wide - top.astype(F32)).astype(BF16)


def dot_wide(left, right, dims=NN):
    left_top, left_rest = split(left)
    right_top, right_rest = split(right)
    return (
        dot(left_top, right_top, dims)
        + dot(left_rest, right_top, dims)
        + dot(left_top, right_rest, dims)
    )


def dot_half(left, right, dims=NN):
    left_top, left_rest = split(left)
    return dot(left_top, right, dims) + dot(left_rest, right, dims)


def invert(lower):
    size = lower.shape[0]
    lanes = 128
    row = lax.broadcasted_iota(jnp.int32, (BASE, lanes), 0)
    lane = lax.broadcasted_iota(jnp.int32, (BASE, lanes), 1)
    group = lane // BASE
    parts = []
    for start in range(0, size, lanes):
        window = lower[start : start + lanes, start : start + lanes]
        packed = jnp.zeros((BASE, lanes), F32)
        for index in range(lanes // BASE):
            packed = jnp.where(group == index, window[index * BASE : (index + 1) * BASE], packed)
        solved = (row == lane - group * BASE).astype(F32)
        for step in range(BASE - 1):
            column = jnp.take_along_axis(packed, group * BASE + step, axis=1)
            solved = solved - column * solved[step : step + 1, :]
        inverse = jnp.concatenate(
            [jnp.where(group == index, solved, 0.0) for index in range(lanes // BASE)], 0
        )
        row_full = lax.broadcasted_iota(jnp.int32, (lanes, lanes), 0)
        lane_full = lax.broadcasted_iota(jnp.int32, (lanes, lanes), 1)
        width = BASE
        while width < lanes:
            coupling = jnp.where(
                (row_full // (2 * width) == lane_full // (2 * width))
                & (row_full // width != lane_full // width),
                window,
                0.0,
            )
            inverse = inverse - dot_wide(inverse, dot_wide(coupling, inverse))
            width *= 2
        parts.append(inverse)
    width = lanes
    while width < size:
        joined = []
        for index in range(0, len(parts), 2):
            first, second = parts[index], parts[index + 1]
            start = index * width
            below = lower[start + width : start + 2 * width, start : start + width]
            corner = -dot_wide(second, dot_wide(below, first))
            joined.append(
                jnp.concatenate(
                    [
                        jnp.concatenate([first, jnp.zeros_like(first)], 1),
                        jnp.concatenate([corner, second], 1),
                    ],
                    0,
                )
            )
        parts = joined
        width *= 2
    return parts[0]


def part_kernel(
    x_ref,
    halo_ref,
    wq_ref,
    wk_ref,
    wv_ref,
    wb_ref,
    bias_ref,
    conv_ref,
    pair_ref,
    local_ref,
    reach_ref,
    proj_ref,
):
    rows = x_ref.shape[0]
    heads = pair_ref.shape[0]
    dim = pair_ref.shape[2]
    taps = conv_ref.shape[1]
    x = x_ref[...]
    active = []
    for index, w_ref in enumerate((wq_ref, wk_ref, wv_ref)):
        proj_ref[index, :HALO] = dot(halo_ref[...], w_ref[...]).astype(BF16).astype(F32)
        proj_ref[index, HALO:] = dot(x, w_ref[...]).astype(BF16).astype(F32)
        first = HALO - (taps - 1)
        total = proj_ref[index, first : first + rows] * conv_ref[index, 0:1]
        for tap in range(1, taps):
            total = total + proj_ref[index, first + tap : first + tap + rows] * conv_ref[
                index, tap : tap + 1
            ]
        active.append((total / (1.0 + jnp.exp(-total))).astype(BF16))
    logits = dot(x, wb_ref[...]) + bias_ref[...]
    rates = 2.0 / (1.0 + jnp.exp(-logits))
    row = lax.broadcasted_iota(jnp.int32, (rows, rows), 0)
    lane = lax.broadcasted_iota(jnp.int32, (rows, rows), 1)
    for head in range(heads):
        span = slice(head * dim, (head + 1) * dim)
        query, key, value = (each[:, span] for each in active)
        rate = rates[:, head : head + 1]
        wide_key = key.astype(F32)
        norm = lax.rsqrt(jnp.sum(wide_key * wide_key, 1, keepdims=True) + 1e-6)
        norm_row = jnp.sum(jnp.where(row == lane, norm, 0.0), 0, keepdims=True)
        rate_row = jnp.sum(jnp.where(row == lane, rate, 0.0), 0, keepdims=True)
        gram = dot(key, key, NT)
        lower = jnp.where(row > lane, gram * (rate * norm) * norm_row, 0.0)
        inverse = invert(lower) * rate_row
        fresh = dot_half(inverse, value)
        weight = dot_half(inverse * norm_row, key)
        moved = dot_half(jnp.concatenate([weight * norm, fresh * norm], 1), key, TN)
        eye = (row[:dim, :dim] == lane[:dim, :dim]).astype(F32)
        pair_ref[head, :dim] = eye - moved[:dim]
        pair_ref[head, dim:] = moved[dim:]
        attend = jnp.where(row >= lane, dot(query, key, NT) * norm_row, 0.0)
        seen = dot_wide(attend, jnp.concatenate([fresh, weight], 1))
        local_ref[:, span] = seen[:, :dim]
        reach_ref[:, span] = query.astype(F32) - seen[:, dim:]


def compose(low, high):
    dim = low.shape[1]
    joined = dot_wide(low, high[:dim])
    return jnp.concatenate([joined[:dim], joined[dim:] + high[dim:]], 0)


def shard_kernel(flags_ref, own_ref, other_ref, first_ref, keep_ref, send_ref):
    heads = own_ref.shape[0]
    swapped = flags_ref[0] == 1
    kept = keep_ref.shape[0]
    bit = flags_ref[1]
    for head in range(heads):
        own, other = own_ref[head], other_ref[head]
        low = jnp.where(swapped, other, own)
        high = jnp.where(swapped, own, other)
        first_ref[head] = low
        whole = compose(low, high)
        if kept == heads:
            keep_ref[head] = whole
            send_ref[head] = whole.astype(BF16)
        else:
            side = head // kept

            @pl.when(bit == side)
            def _():
                keep_ref[head % kept] = whole

            @pl.when(bit != side)
            def _():
                send_ref[head % kept] = whole.astype(BF16)


def join_kernel(flags_ref, own_ref, other_ref, low_ref, total_ref, send_ref):
    later = flags_ref[0] == 1
    for head in range(own_ref.shape[0]):
        own, other = own_ref[head], other_ref[head].astype(F32)
        low = jnp.where(later, other, own)
        high = jnp.where(later, own, other)
        whole = compose(low, high)
        low_ref[head] = low
        total_ref[head] = whole
        start = whole.shape[0] - send_ref.shape[1]
        send_ref[head] = whole[start:].astype(BF16)


def enter_kernel(flags_ref, state_ref, *refs):
    levels = len(refs) - 2
    keep_ref, send_ref = refs[levels:]
    count = keep_ref.shape[0]
    dim = keep_ref.shape[1]
    for head in range(count):
        state = jnp.where(flags_ref[levels] == 1, state_ref[head].astype(F32), 0.0)
        for level in range(levels - 1, 0, -1):
            low = refs[level][head]
            after = dot_wide(state, low[:dim]) + low[dim:]
            state = jnp.where(flags_ref[level] == 1, after, state)
        low = refs[0][head]
        after = dot_wide(state, low[:dim]) + low[dim:]
        later = flags_ref[0] == 1
        keep_ref[head] = jnp.where(later, after, state)
        send_ref[head] = jnp.where(later, state, after).astype(BF16)


def finish_kernel(
    flags_ref, keep_ref, came_ref, first_ref, local0, local1, reach0, reach1, gain_ref, own_ref, other_ref
):
    heads = first_ref.shape[0]
    dim = first_ref.shape[2]
    count = keep_ref.shape[0]
    swapped = flags_ref[0] == 1
    bit = flags_ref[1]
    for head in range(heads):
        span = slice(head * dim, (head + 1) * dim)
        state = keep_ref[head % count]
        if count < heads:
            state = jnp.where(bit == head // count, state, came_ref[head % count].astype(F32))
        first = first_ref[head]
        middle = dot_wide(state, first[:dim]) + first[dim:]
        for local, reach, out, late in (
            (local0, reach0, own_ref, swapped),
            (local1, reach1, other_ref, jnp.logical_not(swapped)),
        ):
            entering = jnp.where(late, middle, state)
            rows = local[:, span] + dot_wide(reach[:, span], entering, NT)
            scale = lax.rsqrt(jnp.mean(rows * rows, 1, keepdims=True) + 1e-5)
            out[:, span] = (rows * scale * gain_ref[:, span]).astype(BF16)


def output_kernel(mine_ref, theirs_ref, w_mine_ref, w_theirs_ref, out_ref):
    mine = dot(mine_ref[...], w_mine_ref[...]).astype(BF16).astype(F32)
    theirs = dot(theirs_ref[...], w_theirs_ref[...]).astype(BF16).astype(F32)
    out_ref[...] = (mine + theirs).astype(BF16)


def call(kernel, outs, inputs, flags=None, scratch=(), flops=0, moved=0):
    specs = [VMEM] * len(inputs)
    if flags is not None:
        inputs = [flags] + list(inputs)
        specs = [pl.BlockSpec(memory_space=pltpu.SMEM)] + specs
    return pl.pallas_call(
        kernel,
        out_shape=[jax.ShapeDtypeStruct(shape, dtype) for shape, dtype in outs],
        in_specs=specs,
        out_specs=[VMEM] * len(outs),
        scratch_shapes=list(scratch),
        compiler_params=pltpu.CompilerParams(vmem_limit_bytes=48 * 1024 * 1024),
        cost_estimate=pl.CostEstimate(flops=flops, bytes_accessed=moved, transcendentals=0),
    )(*inputs)


def shift(block, axes, pairs):
    return lax.ppermute(block, axes, pairs)


def local(tokens, w_query, w_key, w_value, w_beta, beta_bias, conv_weight, norm_gain, w_out):
    groups = lax.axis_size("head")
    shards = lax.axis_size("seq")
    heads = beta_bias.shape[0]
    columns = w_query.shape[1]
    dim = columns // heads
    width = tokens.shape[1]
    me_head = lax.axis_index("head")
    me_seq = lax.axis_index("seq")
    ahead = [(i, i + 1) for i in range(shards - 1)]

    if groups == 2:
        rows = tokens.shape[0]
        swap = [(0, 1), (1, 0)]
        tail = tokens[rows - HALO :]
        other = shift(tokens, "head", swap)
        flat = [(i, i + 1) for i in range(shards * groups - 1)]
        own_halo = shift(tail, ("seq", "head"), flat)
        behind = shift(tail, "seq", ahead)
        other_halo = jnp.where(me_head == 0, tail, behind)
        halves = [(tokens, own_halo), (other, other_halo)]
        swapped = me_head
    else:
        gathered = lax.all_gather(tokens, "head", axis=0, tiled=True)
        rows = gathered.shape[0] // 2
        behind = shift(gathered[2 * rows - HALO :], "seq", ahead)
        halves = [(gathered[:rows], behind), (gathered[rows:], gathered[rows - HALO : rows])]
        swapped = jnp.zeros((), jnp.int32)

    bias = beta_bias.reshape(1, heads)
    gain = norm_gain.reshape(1, columns)
    pair_shape = (heads, 2 * dim, dim)
    results = []
    for block, halo in halves:
        results.append(
            call(
                part_kernel,
                [(pair_shape, F32), ((rows, columns), F32), ((rows, columns), F32)],
                [block, halo, w_query, w_key, w_value, w_beta, bias, conv_weight],
                scratch=[pltpu.VMEM((3, rows + HALO, columns), F32)],
                flops=8 * 10**9,
                moved=5 * 10**6,
            )
        )
    (pair0, local0, reach0), (pair1, local1, reach1) = results

    levels = shards.bit_length() - 1
    bits = [(me_seq >> level) & 1 for level in range(levels)]
    kept = heads // 2 if heads % 2 == 0 else heads
    flags = jnp.stack([swapped, bits[0]]).astype(jnp.int32)
    first, keep, send = call(
        shard_kernel,
        [(pair_shape, F32), ((kept,) + pair_shape[1:], F32), ((kept,) + pair_shape[1:], BF16)],
        [pair0, pair1],
        flags=flags,
    )
    lows = []
    for level in range(levels):
        partner = [(i, i ^ (1 << level)) for i in range(shards)]
        if level == levels - 1:
            lows.append(shift(send, "seq", [(i, j) for i, j in partner if j > i]))
            break
        came = shift(send, "seq", partner)
        last = level == levels - 2
        low, keep, send = call(
            join_kernel,
            [
                (keep.shape, F32),
                (keep.shape, F32),
                ((kept, dim if last else 2 * dim, dim), BF16),
            ],
            [keep, came],
            flags=bits[level].reshape(1).astype(jnp.int32),
        )
        lows.append(low)
    state_in = lows.pop()
    keep, send = call(
        enter_kernel,
        [((kept, dim, dim), F32), ((kept, dim, dim), BF16)],
        [state_in] + lows,
        flags=jnp.stack(bits).astype(jnp.int32),
    )
    if kept < heads:
        came = shift(send, "seq", [(i, i ^ 1) for i in range(shards)])
    else:
        came = send
    normed0, normed1 = call(
        finish_kernel,
        [((rows, columns), BF16), ((rows, columns), BF16)],
        [keep, came, first, local0, local1, reach0, reach1, gain],
        flags=flags,
    )
    if groups == 2:
        w_other = shift(w_out, "head", swap)
        theirs = shift(normed1, "head", swap)
        return call(
            output_kernel,
            [((rows, width), BF16)],
            [normed0, theirs, w_out, w_other],
        )[0]
    normed = jnp.concatenate([normed0, normed1], 0)
    mine = jnp.dot(normed, w_out, preferred_element_type=F32).astype(BF16)
    return lax.psum_scatter(mine, "head", scatter_dimension=0, tiled=True)


def solution(mesh):
    in_specs = (
        P(("seq", "head"), None),
        P(None, "head"),
        P(None, "head"),
        P(None, "head"),
        P(None, "head"),
        P("head"),
        P(None, None, "head"),
        P("head"),
        P("head", None),
    )
    out_specs = P(("seq", "head"), None)
    return jax.shard_map(local, mesh=mesh, in_specs=in_specs, out_specs=out_specs, check_vma=False)
```

time: 473 us -> 90.4 us (0.19)
  other arithmetic: 168 us -> 0.92 us
  waiting for transfers between devices: 182 us -> 22.6 us
  matrix products: 92.8 us -> 0 us
  Pallas kernels: 0 us -> 33.7 us
  starting transfers between devices: 2.08 us -> 20.5 us
  between operations: 13.5 us -> 0.16 us
    another operation x3 -> x2, other arithmetic: 159 us -> 0.15 us  [the longest x1 0.08 us: local(): jnp.stack(bits).astype(jnp.int32)]
    all_gather x3 -> x0, waiting for transfers between devices: 122 us -> none  [the longest x1 51.3 us: local(): lax.all_gather(shard_pair[1][None], 'seq', axis=0, tiled=True)]
    dot_general x55 -> x0, matrix products: 89.3 us -> none  [the longest x8 17.4 us: emit_block(): output = jnp.einsum('hca,hva->hcv', query_b, carried, precision=precise)]
    reduce_scatter x1 -> x0, waiting for transfers between devices: 59.8 us -> none  [local(): lax.psum_scatter(lax.optimization_barrier(product.astype(jnp.bfloat16)).a...]
    pallas_call x0 -> x9, Pallas kernels: none -> 33.7 us  [call(): pl.pallas_call(kernel, out_shape=[jax.ShapeDtypeStruct(shape, dtype) for...]
    ppermute x1 -> x10, waiting for transfers between devices: 0.29 us -> 22.6 us  [shift(): return lax.ppermute(block, axes, pairs)]
    ppermute x1 -> x10, starting transfers between devices: 1.74 us -> 20.5 us  [shift(): return lax.ppermute(block, axes, pairs)]
    unnamed x27 -> x41, local copies, waits for them, and re-layouts: 1.33 us -> 11 us
  transfers between devices with their start and end apart: 5 -> 10, of which waited for: 5 -> 7; matrix products, arithmetic and copies ran while one was open for 2% -> 2% of each run, Pallas kernels for 0% -> 36%
where the time goes in v1:
time: 90.4 us; the launch traced here: 89.8 us
  Pallas kernels  33.7 us (37%)
  waiting for transfers between devices  22.6 us (25%)
  starting transfers between devices  20.5 us (23%)
  local copies, waits for them, and re-layouts  11.8 us (13%)
  other arithmetic  0.92 us (1%)
    pallas_call x9, Pallas kernels, call(): pl.pallas_call(kernel, out_shape=[jax.ShapeDtypeStruct(shape, dtype) for...  33.7 us
    ppermute x10, waiting for transfers between devices, shift(): return lax.ppermute(block, axes, pairs)  22.6 us
    ppermute x10, starting transfers between devices, shift(): return lax.ppermute(block, axes, pairs)  20.5 us
    unnamed x41, local copies, waits for them, and re-layouts  11 us
  transfers between devices with their start and end apart: 10, of which 7 were waited for; matrix products, arithmetic and copies ran while one was open for 2% of the time, Pallas kernels for 36%

profile of v1, /device:TPU:0, one launch (start us, length us, event | category | flops | bytes accessed | tf_op | source)
XLA Modules:
  0.0 89.8 jit_solution(2314542535021936974)
XLA Ops:
  0.0 3.0 %collective-permute-start.1 = (bf16[256,1024]{1,0:T(8,128)(2,1)}, bf16[256,1024]{1,0:T(8,128)(2,1)}, u32[]{:S(2)}, u32[]{:S(2)}) collective-permute-start(bf16[256,1024]{1,0:T(8,128)(2,1)} %x_ref.1), channel_id=1, source_target_pairs={{0,1},{1,0},{2,3},{3,2},{4,5},{5,4},{6,7},{7,6},{8,9},{9,8},{10,11... | collective-permute-start | bytes 1572872 | tf_op jit(solution)/shard_map/ppermute | solution.py:266
  3.0 0.8 slice.3
  3.8 1.9 %collective-permute-start = (bf16[16,1024]{1,0:T(8,128)(2,1)S(1)}, bf16[16,1024]{1,0:T(8,128)(2,1)S(1)}, u32[]{:S(2)}, u32[]{:S(2)}) collective-permute-start(bf16[16,1024]{1,0:T(8,128)(2,1)S(1)} %slice.3), channel_id=1, source_target_pairs={{0,1},{1,2},{2,3},{3,4},{4,5},{5,6},{6,7},{7,8},{8,9},{9,10},{10,1... | collective-permute-start | bytes 98312 | tf_op jit(solution)/shard_map/ppermute | solution.py:266
  5.7 1.5 %collective-permute-start.2 = (bf16[16,1024]{1,0:T(8,128)(2,1)S(1)}, bf16[16,1024]{1,0:T(8,128)(2,1)S(1)}, u32[]{:S(2)}, u32[]{:S(2)}) collective-permute-start(bf16[16,1024]{1,0:T(8,128)(2,1)S(1)} %slice.3), channel_id=1, source_target_pairs={{0,2},{2,4},{4,6},{6,8},{8,10},{10,12},{12,14},{14,16},{16,18},{18... | collective-permute-start | bytes 98312 | tf_op jit(solution)/shard_map/ppermute | solution.py:266
  7.1 3.6 %collective-permute-start.9 = (bf16[512,1024]{1,0:T(8,128)(2,1)}, bf16[512,1024]{1,0:T(8,128)(2,1)S(1)}, u32[]{:S(2)}, u32[]{:S(2)}) collective-permute-start(bf16[512,1024]{1,0:T(8,128)(2,1)} %w_mine_ref.1), channel_id=1, source_target_pairs={{0,1},{1,0},{2,3},{3,2},{4,5},{5,4},{6,7},{7,6},{8,9},{9,8},{10,11... | collective-permute-start | bytes 3145736 | tf_op jit(solution)/shard_map/ppermute | solution.py:266
  10.7 0.1 pad_add_fusion.flags_ref
  10.8 0.6 copy-done.19
  11.4 0.2 copy.10.wb_ref
  11.6 0.0 copy-start.17
  11.6 0.0 collective-permute-done.2
  11.6 0.8 broadcast_select_fusion.halo_ref
  12.4 3.8 %collective-permute-done.halo_ref = bf16[16,1024]{1,0:T(8,128)(2,1)S(1)} collective-permute-done((bf16[16,1024]{1,0:T(8,128)(2,1)S(1)}, bf16[16,1024]{1,0:T(8,128)(2,1)S(1)}, u32[]{:S(2)}, u32[]{:S(2)}) %collective-permute-start) | collective-permute-done | bytes 32800 | tf_op jit(solution)/shard_map/ppermute | solution.py:266
  16.2 1.0 %copy-done.9 = bf16[256,1024]{1,0:T(8,128)(2,1)S(1)} copy-done((bf16[256,1024]{1,0:T(8,128)(2,1)S(1)}, bf16[256,1024]{1,0:T(8,128)(2,1)}, u32[]{:S(2)}) %copy-start.9) | copy-done | bytes 524312
  17.3 1.2 %copy-done.11 = bf16[1024,512]{1,0:T(8,128)(2,1)S(1)} copy-done((bf16[1024,512]{1,0:T(8,128)(2,1)S(1)}, bf16[1024,512]{1,0:T(8,128)(2,1)}, u32[]{:S(2)}) %copy-start.11) | copy-done | bytes 1048600
  18.5 1.2 %copy-done.13 = bf16[1024,512]{1,0:T(8,128)(2,1)S(1)} copy-done((bf16[1024,512]{1,0:T(8,128)(2,1)S(1)}, bf16[1024,512]{1,0:T(8,128)(2,1)}, u32[]{:S(2)}) %copy-start.13) | copy-done | bytes 1048600
  19.7 1.2 %copy-done.15 = bf16[1024,512]{1,0:T(8,128)(2,1)S(1)} copy-done((bf16[1024,512]{1,0:T(8,128)(2,1)S(1)}, bf16[1024,512]{1,0:T(8,128)(2,1)}, u32[]{:S(2)}) %copy-start.15) | copy-done | bytes 1048600
  20.9 11.7 %shard_map.91 = (f32[4,256,128]{2,1,0:T(8,128)S(1)}, f32[256,512]{1,0:T(8,128)S(1)}, f32[256,512]{1,0:T(8,128)S(1)}) custom-call(bf16[256,1024]{1,0:T(8,128)(2,1)S(1)} %copy-done.9, bf16[16,1024]{1,0:T(8,128)(2,1)S(1)} %collective-permute-done.halo_ref, bf16[1024,512]{1,0:T(8,128)(2,1)S(1)} %copy-done.11, bf16[1024,512]{1,0:T(8,128)(2,1)S(1)} %copy-done.13, ...), custom_call_target="tpu_custom_call" | custom-call | flops 8000000000 | bytes 5000000 | tf_op jit(solution)/shard_map/pallas_call | solution.py:254
  32.6 0.0 collective-permute-done.1.x_ref
  32.7 12.9 %shard_map.92 = (f32[4,256,128]{2,1,0:T(8,128)S(1)}, f32[256,512]{1,0:T(8,128)S(1)}, f32[256,512]{1,0:T(8,128)S(1)}) custom-call(bf16[256,1024]{1,0:T(8,128)(2,1)} %collective-permute-done.1.x_ref, bf16[16,1024]{1,0:T(8,128)(2,1)S(1)} %broadcast_select_fusion.halo_ref, bf16[1024,512]{1,0:T(8,128)(2,1)S(1)} %copy-done.12, bf16[1024,512]{1,0:T(8,128)(2,1)S(1)} %copy-done.14, ...), custom_call_target="tpu_custom_call" | custom-call | flops 8000000000 | bytes 5000000 | tf_op jit(solution)/shard_map/pallas_call | solution.py:254
  45.6 1.5 %shard_map.93 = (f32[4,256,128]{2,1,0:T(8,128)S(1)}, f32[2,256,128]{2,1,0:T(8,128)S(1)}, bf16[2,256,128]{2,1,0:T(8,128)(2,1)S(1)}) custom-call(s32[2]{0:T(128)S(1)} %pad_add_fusion.flags_ref, f32[4,256,128]{2,1,0:T(8,128)S(1)} %get-tuple-element.26.own_ref, f32[4,256,128]{2,1,0:T(8,128)S(1)} %get-tuple-element.27.other_ref), custom_call_target="tpu_custom_call" | custom-call | tf_op jit(solution)/shard_map/pallas_call | solution.py:254
  47.1 0.0 copy-start.1
  47.1 0.8 copy-done.1
  47.9 0.2 collective-permute-start.3
  48.1 1.1 %collective-permute-done.3.other_ref = bf16[2,256,128]{2,1,0:T(8,128)(2,1)S(1)} collective-permute-done((bf16[2,256,128]{2,1,0:T(8,128)(2,1)S(1)}, bf16[2,256,128]{2,1,0:T(8,128)(2,1)S(1)}, u32[]{:S(2)}, u32[]{:S(2)}) %collective-permute-start.3) | collective-permute-done | bytes 131104 | tf_op jit(solution)/shard_map/ppermute | solution.py:266
  49.2 0.9 %shard_map.94 = (f32[2,256,128]{2,1,0:T(8,128)S(1)}, f32[2,256,128]{2,1,0:T(8,128)S(1)}, bf16[2,256,128]{2,1,0:T(8,128)(2,1)}) custom-call(s32[1]{0:T(128)} %bitcast.1.flags_ref, f32[2,256,128]{2,1,0:T(8,128)S(1)} %get-tuple-element.28.own_ref, bf16[2,256,128]{2,1,0:T(8,128)(2,1)S(1)} %collective-permute-done.3.other_ref), custom_call_target="tpu_custom_call" | custom-call | tf_op jit(solution)/shard_map/pallas_call | solution.py:254
  50.2 0.7 copy-done.7
  50.9 2.3 %collective-permute-start.4 = (bf16[2,256,128]{2,1,0:T(8,128)(2,1)}, bf16[2,256,128]{2,1,0:T(8,128)(2,1)S(1)}, u32[]{:S(2)}, u32[]{:S(2)}) collective-permute-start(bf16[2,256,128]{2,1,0:T(8,128)(2,1)} %get-tuple-element.31), channel_id=1, source_target_pairs={{0,4},{2,6},{4,0},{6,2},{8,12},{10,14},{12,8},{14,10},{16,20},{18,... | collective-permute-start | bytes 393224 | tf_op jit(solution)/shard_map/ppermute | solution.py:266
  53.1 4.2 %collective-permute-done.4.other_ref = bf16[2,256,128]{2,1,0:T(8,128)(2,1)S(1)} collective-permute-done((bf16[2,256,128]{2,1,0:T(8,128)(2,1)}, bf16[2,256,128]{2,1,0:T(8,128)(2,1)S(1)}, u32[]{:S(2)}, u32[]{:S(2)}) %collective-permute-start.4) | collective-permute-done | bytes 131104 | tf_op jit(solution)/shard_map/ppermute | solution.py:266
  57.4 0.9 %copy-done.8 = f32[2,256,128]{2,1,0:T(8,128)S(1)} copy-done((f32[2,256,128]{2,1,0:T(8,128)S(1)}, f32[2,256,128]{2,1,0:T(8,128)}, u32[]{:S(2)}) %copy-start.8) | copy-done | bytes 262168
  58.3 0.9 %shard_map.95 = (f32[2,256,128]{2,1,0:T(8,128)S(1)}, f32[2,256,128]{2,1,0:T(8,128)S(1)}, bf16[2,256,128]{2,1,0:T(8,128)(2,1)}) custom-call(s32[1]{0:T(128)} %bitcast.2.flags_ref, f32[2,256,128]{2,1,0:T(8,128)S(1)} %copy-done.8, bf16[2,256,128]{2,1,0:T(8,128)(2,1)S(1)} %collective-permute-done.4.other_ref), custom_call_target="tpu_custom_call" | custom-call | tf_op jit(solution)/shard_map/pallas_call | solution.py:254
  59.2 0.7 copy-done.3
  59.9 0.7 copy-done.5
  60.6 1.8 %collective-permute-start.5 = (bf16[2,256,128]{2,1,0:T(8,128)(2,1)}, bf16[2,256,128]{2,1,0:T(8,128)(2,1)S(1)}, u32[]{:S(2)}, u32[]{:S(2)}) collective-permute-start(bf16[2,256,128]{2,1,0:T(8,128)(2,1)} %get-tuple-element.33), channel_id=1, source_target_pairs={{0,8},{2,10},{4,12},{6,14},{8,0},{10,2},{12,4},{14,6},{16,24},{18,... | collective-permute-start | bytes 393224 | tf_op jit(solution)/shard_map/ppermute | solution.py:266
  62.5 3.6 %collective-permute-done.5.other_ref = bf16[2,256,128]{2,1,0:T(8,128)(2,1)S(1)} collective-permute-done((bf16[2,256,128]{2,1,0:T(8,128)(2,1)}, bf16[2,256,128]{2,1,0:T(8,128)(2,1)S(1)}, u32[]{:S(2)}, u32[]{:S(2)}) %collective-permute-start.5) | collective-permute-done | bytes 131104 | tf_op jit(solution)/shard_map/ppermute | solution.py:266
  66.0 0.9 %copy-done.6 = f32[2,256,128]{2,1,0:T(8,128)S(1)} copy-done((f32[2,256,128]{2,1,0:T(8,128)S(1)}, f32[2,256,128]{2,1,0:T(8,128)}, u32[]{:S(2)}) %copy-start.6) | copy-done | bytes 262168
  67.0 1.0 %shard_map.96 = (f32[2,256,128]{2,1,0:T(8,128)S(1)}, f32[2,256,128]{2,1,0:T(8,128)}, bf16[2,128,128]{2,1,0:T(8,128)(2,1)S(1)}) custom-call(s32[1]{0:T(128)} %bitcast.3.flags_ref, f32[2,256,128]{2,1,0:T(8,128)S(1)} %copy-done.6, bf16[2,256,128]{2,1,0:T(8,128)(2,1)S(1)} %collective-permute-done.5.other_ref), custom_call_target="tpu_custom_call" | custom-call | tf_op jit(solution)/shard_map/pallas_call | solution.py:254
  68.0 4.6 %collective-permute-start.6 = (bf16[2,128,128]{2,1,0:T(8,128)(2,1)S(1)}, bf16[2,128,128]{2,1,0:T(8,128)(2,1)S(1)}, u32[]{:S(2)}, u32[]{:S(2)}) collective-permute-start(bf16[2,128,128]{2,1,0:T(8,128)(2,1)S(1)} %get-tuple-element.34), channel_id=1, source_target_pairs={{0,16},{2,18},{4,20},{6,22},{8,24},{10,26},{12,28},{14,30},{1,17},... | collective-permute-start | bytes 196616 | tf_op jit(solution)/shard_map/ppermute | solution.py:266
  72.6 0.1 pad_add_fusion.1.flags_ref
  72.7 1.8 %collective-permute-done.6.state_ref = bf16[2,128,128]{2,1,0:T(8,128)(2,1)S(1)} collective-permute-done((bf16[2,128,128]{2,1,0:T(8,128)(2,1)S(1)}, bf16[2,128,128]{2,1,0:T(8,128)(2,1)S(1)}, u32[]{:S(2)}, u32[]{:S(2)}) %collective-permute-start.6) | collective-permute-done | bytes 65568 | tf_op jit(solution)/shard_map/ppermute | solution.py:266
  74.5 1.2 %shard_map.97 = (f32[2,128,128]{2,1,0:T(8,128)S(1)}, bf16[2,128,128]{2,1,0:T(8,128)(2,1)S(1)}) custom-call(s32[4]{0:T(128)S(1)} %pad_add_fusion.1.flags_ref, bf16[2,128,128]{2,1,0:T(8,128)(2,1)S(1)} %collective-permute-done.6.state_ref, f32[2,256,128]{2,1,0:T(8,128)S(1)} %get-tuple-element.35.refs_0_, f32[2,256,128]{2,1,0:T(8,128)S(1)} %copy-done.4, ...), custom_call_target="tpu_custom_call" | custom-call | tf_op jit(solution)/shard_map/pallas_call | solution.py:254
  75.8 0.1 collective-permute-start.7
  75.8 1.2 %collective-permute-done.7.came_ref = bf16[2,128,128]{2,1,0:T(8,128)(2,1)S(1)} collective-permute-done((bf16[2,128,128]{2,1,0:T(8,128)(2,1)S(1)}, bf16[2,128,128]{2,1,0:T(8,128)(2,1)S(1)}, u32[]{:S(2)}, u32[]{:S(2)}) %collective-permute-start.7) | collective-permute-done | bytes 65568 | tf_op jit(solution)/shard_map/ppermute | solution.py:266
  77.1 0.7 copy-done.10
  77.8 2.0 %shard_map.98 = (bf16[256,512]{1,0:T(8,128)(2,1)S(1)}, bf16[256,512]{1,0:T(8,128)(2,1)S(1)}) custom-call(s32[2]{0:T(128)S(1)} %pad_add_fusion.flags_ref, f32[2,128,128]{2,1,0:T(8,128)S(1)} %get-tuple-element.38.keep_ref, bf16[2,128,128]{2,1,0:T(8,128)(2,1)S(1)} %collective-permute-done.7.came_ref, f32[4,256,128]{2,1,0:T(8,128)S(1)} %copy-done.2, ...), custom_call_target="tpu_custom_call" | custom-call | tf_op jit(solution)/shard_map/pallas_call | solution.py:254
  79.8 1.6 %collective-permute-start.8 = (bf16[256,512]{1,0:T(8,128)(2,1)S(1)}, bf16[256,512]{1,0:T(8,128)(2,1)S(1)}, u32[]{:S(2)}, u32[]{:S(2)}) collective-permute-start(bf16[256,512]{1,0:T(8,128)(2,1)S(1)} %get-tuple-element.46), channel_id=1, source_target_pairs={{0,1},{1,0},{2,3},{3,2},{4,5},{5,4},{6,7},{7,6},{8,9},{9,8},{10,11... | collective-permute-start | bytes 786440 | tf_op jit(solution)/shard_map/ppermute | solution.py:266
  81.4 0.0 collective-permute-done.9.w_theirs_ref
  81.4 6.9 %collective-permute-done.8.theirs_ref = bf16[256,512]{1,0:T(8,128)(2,1)S(1)} collective-permute-done((bf16[256,512]{1,0:T(8,128)(2,1)S(1)}, bf16[256,512]{1,0:T(8,128)(2,1)S(1)}, u32[]{:S(2)}, u32[]{:S(2)}) %collective-permute-start.8) | collective-permute-done | bytes 262176 | tf_op jit(solution)/shard_map/ppermute | solution.py:266
  88.2 1.5 %shard_map.99 = bf16[256,1024]{1,0:T(8,128)(2,1)} custom-call(bf16[256,512]{1,0:T(8,128)(2,1)S(1)} %get-tuple-element.45.mine_ref, bf16[256,512]{1,0:T(8,128)(2,1)S(1)} %collective-permute-done.8.theirs_ref, bf16[512,1024]{1,0:T(8,128)(2,1)S(1)} %copy-done, bf16[512,1024]{1,0:T(8,128)(2,1)S(1)} %collective-permute-done.9.w_theirs_ref), custom_call_target="tpu_custom_call" | custom-call | tf_op jit(solution)/shard_map/pallas_call | solution.py:254
  (26 shorter events, 0.0 us)
Async XLA Ops:
  0.0 32.6 %collective-permute-start.1 = (bf16[256,1024]{1,0:T(8,128)(2,1)}, bf16[256,1024]{1,0:T(8,128)(2,1)}, u32[]{:S(2)}, u32[]{:S(2)}) collective-permute-start(bf16[256,1024]{1,0:T(8,128)(2,1)} %x_ref.1), channel_id=1, source_target_pairs={{0,1},{1,0},{2,3},{3,2},{4,5},{5,4},{6,7},{7,6},{8,9},{9,8},{10,11... | collective-permute-start | bytes 1572872 | tf_op jit(solution)/shard_map/ppermute | solution.py:266
  3.8 12.4 %collective-permute-start = (bf16[16,1024]{1,0:T(8,128)(2,1)S(1)}, bf16[16,1024]{1,0:T(8,128)(2,1)S(1)}, u32[]{:S(2)}, u32[]{:S(2)}) collective-permute-start(bf16[16,1024]{1,0:T(8,128)(2,1)S(1)} %slice.3), channel_id=1, source_target_pairs={{0,1},{1,2},{2,3},{3,4},{4,5},{5,6},{6,7},{7,8},{8,9},{9,10},{10,1... | collective-permute-start | bytes 98312 | tf_op jit(solution)/shard_map/ppermute | solution.py:266
  5.7 6.0 %collective-permute-start.2 = (bf16[16,1024]{1,0:T(8,128)(2,1)S(1)}, bf16[16,1024]{1,0:T(8,128)(2,1)S(1)}, u32[]{:S(2)}, u32[]{:S(2)}) collective-permute-start(bf16[16,1024]{1,0:T(8,128)(2,1)S(1)} %slice.3), channel_id=1, source_target_pairs={{0,2},{2,4},{4,6},{6,8},{8,10},{10,12},{12,14},{14,16},{16,18},{18... | collective-permute-start | bytes 98312 | tf_op jit(solution)/shard_map/ppermute | solution.py:266
  7.1 74.2 %collective-permute-start.9 = (bf16[512,1024]{1,0:T(8,128)(2,1)}, bf16[512,1024]{1,0:T(8,128)(2,1)S(1)}, u32[]{:S(2)}, u32[]{:S(2)}) collective-permute-start(bf16[512,1024]{1,0:T(8,128)(2,1)} %w_mine_ref.1), channel_id=1, source_target_pairs={{0,1},{1,0},{2,3},{3,2},{4,5},{5,4},{6,7},{7,6},{8,9},{9,8},{10,11... | collective-permute-start | bytes 3145736 | tf_op jit(solution)/shard_map/ppermute | solution.py:266
  10.7 0.7 copy-start.19
  11.6 4.6 %copy-start.17 = (f32[3,4,512]{2,1,0:T(4,128)S(1)}, f32[3,4,512]{2,1,0:T(4,128)}, u32[]{:S(2)}) copy-start(f32[3,4,512]{2,1,0:T(4,128)} %conv_ref.3) | copy-start | bytes 73732
  12.4 3.8 %copy-start.18 = (f32[4]{0:T(128)S(1)}, f32[4]{0:T(128)}, u32[]{:S(2)}) copy-start(f32[4]{0:T(128)} %param.14) | copy-start | bytes 52
  16.2 1.0 %copy-start.9 = (bf16[256,1024]{1,0:T(8,128)(2,1)S(1)}, bf16[256,1024]{1,0:T(8,128)(2,1)}, u32[]{:S(2)}) copy-start(bf16[256,1024]{1,0:T(8,128)(2,1)} %x_ref.1) | copy-start | bytes 1572868
  17.3 1.2 %copy-start.11 = (bf16[1024,512]{1,0:T(8,128)(2,1)S(1)}, bf16[1024,512]{1,0:T(8,128)(2,1)}, u32[]{:S(2)}) copy-start(bf16[1024,512]{1,0:T(8,128)(2,1)} %wq_ref.3) | copy-start | bytes 3145732
  18.5 1.2 %copy-start.13 = (bf16[1024,512]{1,0:T(8,128)(2,1)S(1)}, bf16[1024,512]{1,0:T(8,128)(2,1)}, u32[]{:S(2)}) copy-start(bf16[1024,512]{1,0:T(8,128)(2,1)} %wk_ref.3) | copy-start | bytes 3145732
  19.7 1.2 %copy-start.15 = (bf16[1024,512]{1,0:T(8,128)(2,1)S(1)}, bf16[1024,512]{1,0:T(8,128)(2,1)}, u32[]{:S(2)}) copy-start(bf16[1024,512]{1,0:T(8,128)(2,1)} %wv_ref.3) | copy-start | bytes 3145732
  20.9 11.7 %copy-start.12 = (bf16[1024,512]{1,0:T(8,128)(2,1)S(1)}, bf16[1024,512]{1,0:T(8,128)(2,1)}, u32[]{:S(2)}) copy-start(bf16[1024,512]{1,0:T(8,128)(2,1)} %wq_ref.3) | copy-start | bytes 3145732
  20.9 11.7 %copy-start.14 = (bf16[1024,512]{1,0:T(8,128)(2,1)S(1)}, bf16[1024,512]{1,0:T(8,128)(2,1)}, u32[]{:S(2)}) copy-start(bf16[1024,512]{1,0:T(8,128)(2,1)} %wk_ref.3) | copy-start | bytes 3145732
  20.9 11.7 %copy-start.16 = (bf16[1024,512]{1,0:T(8,128)(2,1)S(1)}, bf16[1024,512]{1,0:T(8,128)(2,1)}, u32[]{:S(2)}) copy-start(bf16[1024,512]{1,0:T(8,128)(2,1)} %wv_ref.3) | copy-start | bytes 3145732
  47.1 0.8 copy-start.1
  47.9 1.3 %collective-permute-start.3 = (bf16[2,256,128]{2,1,0:T(8,128)(2,1)S(1)}, bf16[2,256,128]{2,1,0:T(8,128)(2,1)S(1)}, u32[]{:S(2)}, u32[]{:S(2)}) collective-permute-start(bf16[2,256,128]{2,1,0:T(8,128)(2,1)S(1)} %get-tuple-element.29), channel_id=1, source_target_pairs={{0,2},{2,0},{4,6},{6,4},{8,10},{10,8},{12,14},{14,12},{16,18},{18,... | collective-permute-start | bytes 393224 | tf_op jit(solution)/shard_map/ppermute | solution.py:266
  50.2 0.7 copy-start.7
  50.9 6.5 %collective-permute-start.4 = (bf16[2,256,128]{2,1,0:T(8,128)(2,1)}, bf16[2,256,128]{2,1,0:T(8,128)(2,1)S(1)}, u32[]{:S(2)}, u32[]{:S(2)}) collective-permute-start(bf16[2,256,128]{2,1,0:T(8,128)(2,1)} %get-tuple-element.31), channel_id=1, source_target_pairs={{0,4},{2,6},{4,0},{6,2},{8,12},{10,14},{12,8},{14,10},{16,20},{18,... | collective-permute-start | bytes 393224 | tf_op jit(solution)/shard_map/ppermute | solution.py:266
  57.4 1.0 %copy-start.8 = (f32[2,256,128]{2,1,0:T(8,128)S(1)}, f32[2,256,128]{2,1,0:T(8,128)}, u32[]{:S(2)}) copy-start(f32[2,256,128]{2,1,0:T(8,128)} %copy-done.7) | copy-start | bytes 786436
  59.2 0.7 copy-start.3
  59.9 0.7 copy-start.5
  60.6 5.4 %collective-permute-start.5 = (bf16[2,256,128]{2,1,0:T(8,128)(2,1)}, bf16[2,256,128]{2,1,0:T(8,128)(2,1)S(1)}, u32[]{:S(2)}, u32[]{:S(2)}) collective-permute-start(bf16[2,256,128]{2,1,0:T(8,128)(2,1)} %get-tuple-element.33), channel_id=1, source_target_pairs={{0,8},{2,10},{4,12},{6,14},{8,0},{10,2},{12,4},{14,6},{16,24},{18,... | collective-permute-start | bytes 393224 | tf_op jit(solution)/shard_map/ppermute | solution.py:266
  62.5 12.0 %copy-start.4 = (f32[2,256,128]{2,1,0:T(8,128)S(1)}, f32[2,256,128]{2,1,0:T(8,128)}, u32[]{:S(2)}) copy-start(f32[2,256,128]{2,1,0:T(8,128)} %copy-done.3) | copy-start | bytes 786436
  66.0 1.0 %copy-start.6 = (f32[2,256,128]{2,1,0:T(8,128)S(1)}, f32[2,256,128]{2,1,0:T(8,128)}, u32[]{:S(2)}) copy-start(f32[2,256,128]{2,1,0:T(8,128)} %copy-done.5) | copy-start | bytes 786436
  68.0 9.1 %copy-start.2 = (f32[4,256,128]{2,1,0:T(8,128)S(1)}, f32[4,256,128]{2,1,0:T(8,128)}, u32[]{:S(2)}) copy-start(f32[4,256,128]{2,1,0:T(8,128)} %copy-done.1) | copy-start | bytes 1572868
  68.0 6.5 %collective-permute-start.6 = (bf16[2,128,128]{2,1,0:T(8,128)(2,1)S(1)}, bf16[2,128,128]{2,1,0:T(8,128)(2,1)S(1)}, u32[]{:S(2)}, u32[]{:S(2)}) collective-permute-start(bf16[2,128,128]{2,1,0:T(8,128)(2,1)S(1)} %get-tuple-element.34), channel_id=1, source_target_pairs={{0,16},{2,18},{4,20},{6,22},{8,24},{10,26},{12,28},{14,30},{1,17},... | collective-permute-start | bytes 196616 | tf_op jit(solution)/shard_map/ppermute | solution.py:266
  75.8 1.3 %collective-permute-start.7 = (bf16[2,128,128]{2,1,0:T(8,128)(2,1)S(1)}, bf16[2,128,128]{2,1,0:T(8,128)(2,1)S(1)}, u32[]{:S(2)}, u32[]{:S(2)}) collective-permute-start(bf16[2,128,128]{2,1,0:T(8,128)(2,1)S(1)} %get-tuple-element.39), channel_id=1, source_target_pairs={{0,2},{2,0},{4,6},{6,4},{8,10},{10,8},{12,14},{14,12},{16,18},{18,... | collective-permute-start | bytes 196616 | tf_op jit(solution)/shard_map/ppermute | solution.py:266
  77.1 0.7 copy-start.10
  77.8 10.5 %copy-start = (bf16[512,1024]{1,0:T(8,128)(2,1)S(1)}, bf16[512,1024]{1,0:T(8,128)(2,1)}, u32[]{:S(2)}) copy-start(bf16[512,1024]{1,0:T(8,128)(2,1)} %w_mine_ref.1) | copy-start | bytes 3145732
  79.8 8.4 %collective-permute-start.8 = (bf16[256,512]{1,0:T(8,128)(2,1)S(1)}, bf16[256,512]{1,0:T(8,128)(2,1)S(1)}, u32[]{:S(2)}, u32[]{:S(2)}) collective-permute-start(bf16[256,512]{1,0:T(8,128)(2,1)S(1)} %get-tuple-element.46), channel_id=1, source_target_pairs={{0,1},{1,0},{2,3},{3,2},{4,5},{5,4},{6,7},{7,6},{8,9},{9,8},{10,11... | collective-permute-start | bytes 786440 | tf_op jit(solution)/shard_map/ppermute | solution.py:266

commit v2 on v0

v2 whole, which is shorter than its diff:
```python
import functools

import jax
import jax.numpy as jnp
from jax import lax
from jax.experimental import pallas as pl
from jax.experimental.pallas import tpu as pltpu
from jax.sharding import PartitionSpec as P

BASE = 16
HALO = 16
F32 = jnp.float32
BF16 = jnp.bfloat16
VMEM = pl.BlockSpec(memory_space=pltpu.VMEM)
NN = ((1,), (0,))
NT = ((1,), (1,))
TN = ((0,), (0,))


def dot(left, right, dims=NN):
    return lax.dot_general(left, right, (dims, ((), ())), preferred_element_type=F32)


def split(wide):
    top = wide.astype(BF16)
    return top, (wide - top.astype(F32)).astype(BF16)


def dot_wide(left, right, dims=NN):
    left_top, left_rest = split(left)
    right_top, right_rest = split(right)
    return (
        dot(left_top, right_top, dims)
        + dot(left_rest, right_top, dims)
        + dot(left_top, right_rest, dims)
    )


def dot_half(left, right, dims=NN):
    left_top, left_rest = split(left)
    return dot(left_top, right, dims) + dot(left_rest, right, dims)


def substitute(windows):
    lanes = windows[0].shape[0]
    row = lax.broadcasted_iota(jnp.int32, (8, lanes), 0)
    lane = lax.broadcasted_iota(jnp.int32, (8, lanes), 1)
    group = lane // BASE
    bands = BASE // 8
    packed, solved = [], []
    for window in windows:
        rows = []
        for band in range(bands):
            piece = window[band * 8 : band * 8 + 8]
            for index in range(1, lanes // BASE):
                start = index * BASE + band * 8
                piece = jnp.where(group == index, window[start : start + 8], piece)
            rows.append(piece)
        packed.append(rows)
        solved.append(
            [(row + band * 8 == lane - group * BASE).astype(F32) for band in range(bands)]
        )
    for step in range(BASE - 1):
        at = step // 8
        place = group * BASE + step
        for rows, found in zip(packed, solved):
            pivot = found[at][step % 8 : step % 8 + 1]
            for band in range(at, bands):
                if band > at or step % 8 < 7:
                    column = jnp.take_along_axis(rows[band], place, axis=1)
                    found[band] = found[band] - column * pivot
    return [
        jnp.concatenate(
            [jnp.where(group == index, piece, 0.0) for index in range(lanes // BASE) for piece in found],
            0,
        )
        for found in solved
    ]


def invert(lowers):
    size = lowers[0].shape[0]
    lanes = 128
    starts = range(0, size, lanes)
    windows = [low[at : at + lanes, at : at + lanes] for low in lowers for at in starts]
    inverses = substitute(windows)
    row = lax.broadcasted_iota(jnp.int32, (lanes, lanes), 0)
    lane = lax.broadcasted_iota(jnp.int32, (lanes, lanes), 1)
    width = BASE
    while width < lanes:
        mask = (row // (2 * width) == lane // (2 * width)) & (row // width != lane // width)
        inner = [
            dot_wide(jnp.where(mask, window, 0.0), inverse)
            for window, inverse in zip(windows, inverses)
        ]
        inverses = [inverse - dot_wide(inverse, each) for inverse, each in zip(inverses, inner)]
        width *= 2
    count = len(starts)
    groups = [inverses[at : at + count] for at in range(0, len(inverses), count)]
    while width < size:
        joined = []
        below = [
            [
                dot_wide(
                    low[(at + 1) * width : (at + 2) * width, at * width : (at + 1) * width], parts[at]
                )
                for at in range(0, len(parts), 2)
            ]
            for low, parts in zip(lowers, groups)
        ]
        for inner, parts in zip(below, groups):
            merged = []
            for at in range(0, len(parts), 2):
                first, second = parts[at], parts[at + 1]
                corner = -dot_wide(second, inner[at // 2])
                merged.append(
                    jnp.concatenate(
                        [
                            jnp.concatenate([first, jnp.zeros_like(first)], 1),
                            jnp.concatenate([corner, second], 1),
                        ],
                        0,
                    )
                )
            joined.append(merged)
        groups = joined
        width *= 2
    return [parts[0] for parts in groups]


def activate(x, weights, conv_ref, proj_ref, blocks):
    taps = conv_ref.shape[1]
    active = [[] for _ in blocks]
    for index, w_ref in enumerate(weights):
        proj_ref[index] = dot(x, w_ref[...]).astype(BF16).astype(F32)
        for (start, rows), outs in zip(blocks, active):
            first = start - (taps - 1)
            total = proj_ref[index, first : first + rows] * conv_ref[index, 0:1]
            for tap in range(1, taps):
                total = total + proj_ref[index, first + tap : first + tap + rows] * conv_ref[
                    index, tap : tap + 1
                ]
            outs.append((total / (1.0 + jnp.exp(-total))).astype(BF16))
    return active


def invert_few(count, lowers):
    inverses = []
    for lower in lowers:
        eye = jnp.eye(lower.shape[0], dtype=F32)
        inverse = eye - lower
        for _ in range(count - 2):
            inverse = eye - dot_wide(lower, inverse)
        inverses.append(inverse)
    return inverses


def transitions(keys, values, rates, invert=invert):
    rows, dim = keys[0].shape
    row = lax.broadcasted_iota(jnp.int32, (rows, rows), 0)
    lane = lax.broadcasted_iota(jnp.int32, (rows, rows), 1)
    norms, norm_rows, rate_rows, lowers = [], [], [], []
    for key, rate_row in zip(keys, rates):
        rate = jnp.sum(jnp.where(row == lane, rate_row, 0.0), 1, keepdims=True)
        wide_key = key.astype(F32)
        norm = lax.rsqrt(jnp.sum(wide_key * wide_key, 1, keepdims=True) + 1e-6)
        norm_row = jnp.sum(jnp.where(row == lane, norm, 0.0), 0, keepdims=True)
        norms.append(norm)
        norm_rows.append(norm_row)
        rate_rows.append(rate_row)
        gram = dot(key, key, NT)
        lowers.append(jnp.where(row > lane, gram * (rate * norm) * norm_row, 0.0))
    inverses = [each * rate for each, rate in zip(invert(lowers), rate_rows)]
    eye = jnp.eye(dim, dtype=F32)
    solved = []
    for key, value, inverse, norm_row in zip(keys, values, inverses, norm_rows):
        fresh = dot_half(inverse, value)
        weight = dot_half(inverse * norm_row, key)
        solved.append(jnp.concatenate([fresh, weight], 1))
    pairs = []
    for key, each, norm in zip(keys, solved, norms):
        moved = dot_half(each * norm, key, TN)
        pairs.append(jnp.concatenate([eye - moved[dim:], moved[:dim]], 0))
    return pairs, solved, norm_rows


def look(query, key, norm_row, solved):
    rows, dim = query.shape
    row = lax.broadcasted_iota(jnp.int32, (rows, rows), 0)
    lane = lax.broadcasted_iota(jnp.int32, (rows, rows), 1)
    attend = jnp.where(row >= lane, dot(query, key, NT) * norm_row, 0.0)
    seen = dot(attend.astype(BF16), solved)
    return jnp.concatenate([seen[:, :dim], query.astype(F32) - seen[:, dim:]], 1)


def spans_of(count, width):
    dim = width // count
    return [slice(head * dim, (head + 1) * dim) for head in range(count)]


def write_rates(x, wb, bias_ref):
    logits = dot(wb, x, NT)
    return [
        2.0 / (1.0 + jnp.exp(-(logits[head : head + 1] + bias_ref[head])))
        for head in range(wb.shape[0])
    ]


def edge_kernel(x_ref, head_ref, tail_ref):
    head_ref[...] = x_ref[: head_ref.shape[0]]
    tail_ref[...] = x_ref[x_ref.shape[0] - tail_ref.shape[0] :]


def early_kernel(
    bias_ref, x_ref, wq_ref, wk_ref, wv_ref, wb_ref, conv_ref, pair_ref, look_ref, proj_ref
):
    rows, width = x_ref.shape
    x = jnp.concatenate([jnp.zeros((HALO, width), BF16), x_ref[...]], 0)
    active = activate(x, (wq_ref, wk_ref, wv_ref), conv_ref, proj_ref, [(HALO, rows)])[0]
    spans = spans_of(pair_ref.shape[0], active[0].shape[1])
    queries, keys, values = ([each[:, span] for span in spans] for each in active)
    lane = lax.broadcasted_iota(jnp.int32, (1, rows), 1)
    rates = [
        jnp.where(lane < conv_ref.shape[1] - 1, 0.0, each)
        for each in write_rates(x_ref[...], wb_ref[...], bias_ref)
    ]
    pairs, solved, norm_rows = transitions(keys, values, rates)
    for head in range(len(spans)):
        pair_ref[head] = pairs[head]
        look_ref[head] = look(
            queries[head], keys[head], norm_rows[head], solved[head].astype(BF16)
        )


def late_kernel(
    flags_ref,
    bias_ref,
    x_ref,
    wq_ref,
    wk_ref,
    wv_ref,
    wb_ref,
    conv_ref,
    head_ref,
    tail_ref,
    halo_ref,
    behind_ref,
    early_ref,
    keep_ref,
    send_ref,
    norm_ref,
    held_ref,
    mini_ref,
    proj_ref,
):
    heads = early_ref.shape[0]
    kept = keep_ref.shape[0]
    rows = x_ref.shape[0]
    swapped = flags_ref[0] == 1
    halo = jnp.where(swapped, behind_ref[...], tail_ref[...])
    x = jnp.concatenate([halo, x_ref[...], halo_ref[...], head_ref[...]], 0)
    active, few = activate(
        x,
        (wq_ref, wk_ref, wv_ref),
        conv_ref,
        proj_ref,
        [(HALO, rows), (2 * HALO + rows, HALO)],
    )
    spans = spans_of(heads, active[0].shape[1])
    queries, keys, values = ([each[:, span] for span in spans] for each in active)
    rates = write_rates(x_ref[...], wb_ref[...], bias_ref)
    lane = lax.broadcasted_iota(jnp.int32, (1, HALO), 1)
    few_rates = [
        jnp.where(lane < conv_ref.shape[1] - 1, each, 0.0)
        for each in write_rates(head_ref[...], wb_ref[...], bias_ref)
    ]
    few_queries, few_keys, few_values = ([each[:, span] for span in spans] for each in few)
    few_pairs, few_solved, few_norm_rows = transitions(
        few_keys, few_values, few_rates, functools.partial(invert_few, conv_ref.shape[1] - 1)
    )
    early = []
    for head in range(heads):
        mini_ref[head] = look(
            few_queries[head], few_keys[head], few_norm_rows[head], few_solved[head].astype(BF16)
        )
        early.append(compose(few_pairs[head], early_ref[head]))
    pairs, solved, norm_rows = transitions(keys, values, rates)
    bit = flags_ref[1]
    wholes = []
    for head, late in enumerate(pairs):
        norm_ref[head : head + 1] = norm_rows[head]
        low = jnp.where(swapped, late, early[head])
        held_ref[head] = jnp.concatenate(
            [
                solved[head].astype(BF16),
                queries[head],
                keys[head],
                low.astype(BF16),
                few_pairs[head].astype(BF16),
            ],
            1,
        )
        wholes.append(compose(low, jnp.where(swapped, early[head], late)).astype(BF16))
    for head in range(kept):
        if kept == heads:
            keep_ref[head] = wholes[head]
            send_ref[head] = wholes[head]
        else:
            one, two = wholes[head], wholes[head + kept]
            keep_ref[head] = jnp.where(bit == 1, two, one)
            send_ref[head] = jnp.where(bit == 1, one, two)


def look_kernel(taps, flags_ref, norm_ref, held_ref, mini_ref, early_ref, both_ref):
    swapped = flags_ref[0] == 1
    heads = held_ref.shape[0]
    rows = held_ref.shape[1]
    dim = held_ref.shape[2] // 6
    row = lax.broadcasted_iota(jnp.int32, (HALO, 2 * dim), 0)
    for head in range(heads):
        late = look(
            held_ref[head, :, 2 * dim : 3 * dim],
            held_ref[head, :, 3 * dim : 4 * dim],
            norm_ref[head : head + 1],
            held_ref[head, :, : 2 * dim],
        )
        early = early_ref[head]
        few = held_ref[head, :, 5 * dim :]
        through = dot(early[:, dim:].astype(BF16), few, NT)
        early = jnp.concatenate([early[:, :dim] + through[:, dim:], through[:, :dim]], 1)
        top = jnp.where(row < taps - 1, mini_ref[head], early[:HALO])
        early = jnp.concatenate([top, early[HALO:]], 0)
        first = held_ref[head, :, 4 * dim : 5 * dim]
        later = jnp.where(swapped, early, late)
        through = dot(later[:, dim:].astype(BF16), first, NT)
        later = jnp.concatenate([later[:, :dim] + through[:, dim:], through[:, :dim]], 1)
        both_ref[0, head] = jnp.where(swapped, later, early)
        both_ref[1, head] = jnp.where(swapped, late, later)


def compose(low, high):
    dim = low.shape[1]
    joined = dot_wide(low, high[:dim])
    return jnp.concatenate([joined[:dim], joined[dim:] + high[dim:]], 0)


def join_kernel(flags_ref, own_ref, other_ref, send_ref):
    later = flags_ref[0] == 1
    for head in range(own_ref.shape[0]):
        own, other = own_ref[head], other_ref[head]
        low = jnp.where(later, other, own)
        high = jnp.where(later, own, other)
        dim = low.shape[1]
        joined = dot(low, high[:dim])
        start = 2 * dim - send_ref.shape[1]
        if start < dim:
            send_ref[head, : dim - start] = joined[start:dim].astype(BF16)
        send_ref[head, dim - start :] = (joined[dim:] + high[dim:].astype(F32)).astype(BF16)


def open_kernel(flags_ref, own_ref, other_ref, path_ref):
    dim = own_ref.shape[2]
    row = lax.broadcasted_iota(jnp.int32, (2 * dim, dim), 0)
    lane = lax.broadcasted_iota(jnp.int32, (2 * dim, dim), 1)
    for head in range(own_ref.shape[0]):
        path_ref[head, :, :dim] = (row == lane).astype(F32)
        low = jnp.where(flags_ref[0] == 1, other_ref[head], own_ref[head])
        path_ref[head, :, dim:] = low.astype(F32)


def path_kernel(flags_ref, path_ref, came_ref, out_ref):
    dim = came_ref.shape[2]
    for head in range(came_ref.shape[0]):
        path = path_ref[head]
        through = dot_wide(came_ref[head].astype(F32), path[:dim])
        longer = jnp.concatenate([through[:dim], through[dim:] + path[dim:]], 0)
        out_ref[head] = jnp.where(flags_ref[0] == 1, longer, path)


def enter_kernel(flags_ref, state_ref, path_ref, keep_ref, send_ref):
    dim = state_ref.shape[2]
    for head in range(keep_ref.shape[0]):
        state = jnp.where(flags_ref[1] == 1, state_ref[head], jnp.zeros_like(state_ref[head]))
        path = path_ref[head]
        both = (dot(state, path[:dim].astype(BF16)) + path[dim:]).astype(BF16)
        later = flags_ref[0] == 1
        keep_ref[head] = jnp.where(later, both[:, dim:], both[:, :dim])
        send_ref[head] = jnp.where(later, both[:, :dim], both[:, dim:])


def finish_kernel(place, flags_ref, keep_ref, came_ref, both_ref, gain_ref, out_ref):
    count, dim = keep_ref.shape[:2]
    heads = both_ref.shape[1]
    for head, span in enumerate(spans_of(heads, heads * dim)):
        state = keep_ref[head % count]
        if count < heads:
            state = jnp.where(flags_ref[0] == head // count, state, came_ref[head % count])
        reach = both_ref[place, head, :, dim:].astype(BF16)
        rows = both_ref[place, head, :, :dim] + dot(reach, state, NT)
        scale = lax.rsqrt(jnp.mean(rows * rows, 1, keepdims=True) + 1e-5)
        out_ref[:, span] = (rows * scale * gain_ref[:, span]).astype(BF16)


def finish_mine_kernel(flags_ref, keep_ref, came_ref, both_ref, gain_ref, w_ref, out_ref, normed_ref):
    finish_kernel(0, flags_ref, keep_ref, came_ref, both_ref, gain_ref, normed_ref)
    out_ref[...] = dot(normed_ref[...], w_ref[...]).astype(BF16)


def half_kernel(flags_ref, w_ref, part_ref):
    rows = part_ref.shape[0]
    part_ref[...] = w_ref[pl.ds(pl.multiple_of(flags_ref[0] * rows, rows), rows)]


def output_kernel(flags_ref, theirs_ref, part_ref, rest_ref, mine_ref, out_ref):
    rows = part_ref.shape[0]
    later = flags_ref[0] == 1
    low, high = theirs_ref[:, :rows], theirs_ref[:, rows:]
    total = dot(jnp.where(later, high, low), part_ref[...])
    total = total + dot(jnp.where(later, low, high), rest_ref[...])
    theirs = total.astype(BF16).astype(F32)
    out_ref[...] = (mine_ref[...].astype(F32) + theirs).astype(BF16)


def call(kernel, outs, inputs, scalars=(), scratch=(), flops=10**7, moved=10**5, grant=8):
    specs = [pl.BlockSpec(memory_space=pltpu.SMEM)] * len(scalars)
    specs += [VMEM] * len(inputs)
    return pl.pallas_call(
        kernel,
        out_shape=[jax.ShapeDtypeStruct(shape, dtype) for shape, dtype in outs],
        in_specs=specs,
        out_specs=[VMEM] * len(outs),
        scratch_shapes=list(scratch),
        compiler_params=pltpu.CompilerParams(vmem_limit_bytes=grant * 1024 * 1024),
        cost_estimate=pl.CostEstimate(flops=flops, bytes_accessed=moved, transcendentals=0),
    )(*scalars, *inputs)


def together(*arrays):
    return lax.optimization_barrier(arrays)


def shift(block, axes, pairs):
    return lax.ppermute(block, axes, pairs)


def local(tokens, w_query, w_key, w_value, w_beta, beta_bias, conv_weight, norm_gain, w_out):
    groups = lax.axis_size("head")
    shards = lax.axis_size("seq")
    heads = beta_bias.shape[0]
    columns = w_query.shape[1]
    dim = columns // heads
    width = tokens.shape[1]
    me_head = lax.axis_index("head")
    me_seq = lax.axis_index("seq")
    ahead = [(i, i + 1) for i in range(shards - 1)]

    if groups == 2:
        rows = tokens.shape[0]
        swap = [(0, 1), (1, 0)]
        early = tokens
        late = shift(tokens, "head", swap)
        head, tail = call(
            edge_kernel, [((HALO, width), BF16)] * 2, [tokens], flops=2 * 10**10, moved=10**6
        )
        flat = [(i, i + 1) for i in range(shards * groups - 1)]
        halo = shift(tail, ("seq", "head"), flat)
        behind = shift(tail, "seq", ahead)
        swapped = me_head
    else:
        gathered = lax.all_gather(tokens, "head", axis=0, tiled=True)
        rows = gathered.shape[0] // 2
        early, late = gathered[:rows], gathered[rows:]
        halo = behind = shift(late[rows - HALO :], "seq", ahead)
        head, tail = early[:HALO], early[rows - HALO :]
        swapped = jnp.zeros((), jnp.int32)

    gain = norm_gain.reshape(1, columns)
    pair_shape = (heads, 2 * dim, dim)
    kept = heads // 2 if heads % 2 == 0 else heads
    kept_shape = (kept,) + pair_shape[1:]
    levels = shards.bit_length() - 1
    bits = [((me_seq >> level) & 1).astype(jnp.int32).reshape(1) for level in range(levels)]
    flags = jnp.concatenate([swapped.astype(jnp.int32).reshape(1), bits[0]])
    weights = [w_query, w_key, w_value, w_beta.T, conv_weight]
    pair0, look0 = call(
        early_kernel,
        [(pair_shape, F32), ((heads, rows, 2 * dim), F32)],
        [early] + weights,
        scalars=[beta_bias],
        scratch=[pltpu.VMEM((3, rows + HALO, columns), F32)],
        grant=24,
    )
    keep, send, *held = call(
        late_kernel,
        [
            (kept_shape, BF16),
            (kept_shape, BF16),
            ((heads, rows), F32),
            ((heads, rows, 6 * dim), BF16),
            ((heads, HALO, 2 * dim), F32),
        ],
        [late] + weights + [head, tail, halo, behind, pair0],
        scalars=[flags, beta_bias],
        scratch=[pltpu.VMEM((3, rows + 3 * HALO, columns), F32)],
        grant=24,
    )
    own = keep
    for level in range(levels):
        partner = [(i, i ^ (1 << level)) for i in range(shards)]
        if level == levels - 1:
            partner = [(i, j) for i, j in partner if j > i]
        came = shift(send, "seq", partner)
        if level == 1:
            both = call(
                functools.partial(look_kernel, conv_weight.shape[1]),
                [((2, heads, rows, 2 * dim), F32)],
                held + [look0],
                scalars=[flags],
            )[0]
            came, path, both = together(came, path, both)
            if groups == 2:
                part = call(
                    half_kernel,
                    [((w_out.shape[0] // 2, width), BF16)],
                    [w_out],
                    scalars=[bits[0]],
                )[0]
        elif level > 1:
            came, path = together(came, path)
        if level == levels - 1:
            break
        send = call(
            join_kernel,
            [((kept, dim if level == levels - 2 else 2 * dim, dim), BF16)],
            [own, came],
            scalars=[bits[level]],
        )[0]
        if level == 0:
            own, came, send = together(own, came, send)
            path = call(
                open_kernel, [((kept, 2 * dim, 2 * dim), F32)], [own, came], scalars=[bits[0]]
            )[0]
        else:
            path, came, send = together(path, came, send)
            path = call(
                path_kernel, [((kept, 2 * dim, 2 * dim), F32)], [path, came], scalars=[bits[level]]
            )[0]
            if level == 1 and groups == 2:
                part, path = together(part, path)
                part = shift(part, "head", swap)
        own = send
    keep, send = call(
        enter_kernel,
        [((kept, dim, dim), BF16)] * 2,
        [came, path],
        scalars=[jnp.concatenate([bits[0], bits[levels - 1]])],
    )
    came = shift(send, "seq", [(i, i ^ 1) for i in range(shards)]) if kept < heads else send
    gone = call(
        functools.partial(finish_kernel, 1),
        [((rows, columns), BF16)],
        [keep, came, both, gain],
        scalars=[bits[0]],
    )[0]
    if groups == 2:
        theirs = shift(gone, "head", swap)
        mine = call(
            finish_mine_kernel,
            [((rows, width), BF16)],
            [keep, came, both, gain, w_out],
            scalars=[bits[0]],
            scratch=[pltpu.VMEM((rows, columns), BF16)],
        )[0]
        part, gone = together(part, gone)
        rest = shift(part, "seq", [(i, i ^ 1) for i in range(shards)])
        return call(
            output_kernel,
            [((rows, width), BF16)],
            [theirs, part, rest, mine],
            scalars=[bits[0]],
        )[0]
    normed = call(
        functools.partial(finish_kernel, 0),
        [((rows, columns), BF16)],
        [keep, came, both, gain],
        scalars=[bits[0]],
    )[0]
    product = jnp.dot(
        jnp.concatenate([normed, gone], 0), w_out, preferred_element_type=F32
    ).astype(BF16)
    return lax.psum_scatter(product, "head", scatter_dimension=0, tiled=True)


def solution(mesh):
    in_specs = (
        P(("seq", "head"), None),
        P(None, "head"),
        P(None, "head"),
        P(None, "head"),
        P(None, "head"),
        P("head"),
        P(None, None, "head"),
        P("head"),
        P("head", None),
    )
    out_specs = P(("seq", "head"), None)
    return jax.shard_map(local, mesh=mesh, in_specs=in_specs, out_specs=out_specs, check_vma=False)
```

time: 473 us -> 63.3 us (0.13)
  waiting for transfers between devices: 182 us -> 13.1 us
  other arithmetic: 168 us -> 0.15 us
  matrix products: 92.8 us -> 0 us
  Pallas kernels: 0 us -> 21 us
  starting transfers between devices: 2.08 us -> 19.4 us
  between operations: 13.5 us -> 0.28 us
    another operation x3 -> x0, other arithmetic: 159 us -> none  [local(): lax.linalg.triangular_solve(system, right_sides, left_side=True, lower=Tr...]
    all_gather x3 -> x0, waiting for transfers between devices: 122 us -> none  [the longest x1 51.3 us: local(): lax.all_gather(shard_pair[1][None], 'seq', axis=0, tiled=True)]
    dot_general x55 -> x0, matrix products: 89.3 us -> none  [the longest x8 17.4 us: emit_block(): output = jnp.einsum('hca,hva->hcv', query_b, carried, precision=precise)]
    reduce_scatter x1 -> x0, waiting for transfers between devices: 59.8 us -> none  [local(): lax.psum_scatter(lax.optimization_barrier(product.astype(jnp.bfloat16)).a...]
    pallas_call x0 -> x15, Pallas kernels: none -> 21 us  [call(): pl.pallas_call(kernel, out_shape=[jax.ShapeDtypeStruct(shape, dtype) for...]
    ppermute x1 -> x11, starting transfers between devices: 1.74 us -> 19.4 us  [shift(): return lax.ppermute(block, axes, pairs)]
    ppermute x1 -> x11, waiting for transfers between devices: 0.29 us -> 13.1 us  [shift(): return lax.ppermute(block, axes, pairs)]
    unnamed x27 -> x42, local copies, waits for them, and re-layouts: 1.33 us -> 8.71 us
  transfers between devices with their start and end apart: 5 -> 11, of which waited for: 5 -> 7; matrix products, arithmetic and copies ran while one was open for 2% -> 0% of each run, Pallas kernels for 0% -> 17%
where the time goes in v2:
time: 63.3 us; the launch traced here: 62.7 us
  Pallas kernels  21 us (33%)
  starting transfers between devices  19.4 us (31%)
  waiting for transfers between devices  13.1 us (21%)
  local copies, waits for them, and re-layouts  8.71 us (14%)
    pallas_call x15, Pallas kernels, call(): pl.pallas_call(kernel, out_shape=[jax.ShapeDtypeStruct(shape, dtype) for...  21 us
    ppermute x11, starting transfers between devices, shift(): return lax.ppermute(block, axes, pairs)  19.4 us
    ppermute x11, waiting for transfers between devices, shift(): return lax.ppermute(block, axes, pairs)  13.1 us
    unnamed x42, local copies, waits for them, and re-layouts  8.71 us
  transfers between devices with their start and end apart: 11, of which 7 were waited for; matrix products, arithmetic and copies ran while one was open for 0% of the time, Pallas kernels for 17%

profile of v2, /device:TPU:0, one launch (start us, length us, event | category | flops | bytes accessed | tf_op | source)
XLA Modules:
  0.0 62.7 jit_solution(7530177017788353867)
XLA Ops:
  0.0 3.0 %collective-permute-start = (bf16[256,1024]{1,0:T(8,128)(2,1)}, bf16[256,1024]{1,0:T(8,128)(2,1)}, u32[]{:S(2)}, u32[]{:S(2)}) collective-permute-start(bf16[256,1024]{1,0:T(8,128)(2,1)} %x_ref.3), channel_id=1, source_target_pairs={{0,1},{1,0},{2,3},{3,2},{4,5},{5,4},{6,7},{7,6},{8,9},{9,8},{10,11... | collective-permute-start | bytes 1572872 | tf_op jit(solution)/shard_map/ppermute | solution.py:443
  3.0 1.1 %copy-done.13 = bf16[256,1024]{1,0:T(8,128)(2,1)S(1)} copy-done((bf16[256,1024]{1,0:T(8,128)(2,1)S(1)}, bf16[256,1024]{1,0:T(8,128)(2,1)}, u32[]{:S(2)}) %copy-start.13) | copy-done | bytes 524312
  4.1 2.2 %collective-permute-start.1 = (bf16[16,1024]{1,0:T(8,128)(2,1)S(1)}, bf16[16,1024]{1,0:T(8,128)(2,1)S(1)}, u32[]{:S(2)}, u32[]{:S(2)}) collective-permute-start(bf16[16,1024]{1,0:T(8,128)(2,1)S(1)} %get-tuple-element.36.tail_ref), channel_id=1, source_target_pairs={{0,1},{1,2},{2,3},{3,4},{4,5},{5,6},{6,7},{7,8},{8,9},{9,10},{10,1... | collective-permute-start | bytes 98312 | tf_op jit(solution)/shard_map/ppermute | solution.py:443
  6.3 1.5 %collective-permute-start.2 = (bf16[16,1024]{1,0:T(8,128)(2,1)S(1)}, bf16[16,1024]{1,0:T(8,128)(2,1)S(1)}, u32[]{:S(2)}, u32[]{:S(2)}) collective-permute-start(bf16[16,1024]{1,0:T(8,128)(2,1)S(1)} %get-tuple-element.36.tail_ref), channel_id=1, source_target_pairs={{0,2},{2,4},{4,6},{6,8},{8,10},{10,12},{12,14},{14,16},{16,18},{18... | collective-permute-start | bytes 98312 | tf_op jit(solution)/shard_map/ppermute | solution.py:443
  7.8 0.0 copy-start.4
  7.8 0.1 pad_add_fusion.1.flags_ref
  7.9 0.0 copy-start.14
  7.9 1.1 %copy-done.14 = bf16[256,1024]{1,0:T(8,128)(2,1)S(1)} copy-done((bf16[256,1024]{1,0:T(8,128)(2,1)S(1)}, bf16[256,1024]{1,0:T(8,128)(2,1)}, u32[]{:S(2)}) %copy-start.14) | copy-done | bytes 524312
  9.0 5.9 %shard_map.92 = (f32[4,256,128]{2,1,0:T(8,128)S(1)}, f32[4,256,256]{2,1,0:T(8,128)S(1)}) custom-call(f32[4]{0:T(128)S(1)} %copy-done.20, bf16[256,1024]{1,0:T(8,128)(2,1)S(1)} %copy-done.14, bf16[1024,512]{1,0:T(8,128)(2,1)S(1)} %copy-done.1, bf16[1024,512]{1,0:T(8,128)(2,1)S(1)} %copy-done.2, bf16[1024,512]{1,0:T(8,128)(2,1)S(1)} %copy-done.3, ...), custom_call_target="tpu_custom_call" | custom-call | flops 10000000 | bytes 100000 | tf_op jit(solution)/shard_map/pallas_call | solution.py:427
  14.9 0.2 collective-permute-done.1.halo_ref
  15.1 0.0 collective-permute-done.2.behind_ref
  15.1 0.1 collective-permute-done.x_ref
  15.3 7.2 %shard_map.93 = (bf16[2,256,128]{2,1,0:T(8,128)(2,1)S(1)}, bf16[2,256,128]{2,1,0:T(8,128)(2,1)S(1)}, f32[4,256]{1,0:T(4,128)S(1)}, bf16[4,256,768]{2,1,0:T(8,128)(2,1)S(1)}, f32[4,16,256]{2,1,0:T(8,128)S(1)}) custom-call(s32[2]{0:T(128)S(1)} %pad_add_fusion.1.flags_ref, f32[4]{0:T(128)S(1)} %copy-done.20, bf16[256,1024]{1,0:T(8,128)(2,1)} %collective-permute-done.x_ref, ...), custom_call_target="tpu_custom_call" | custom-call | flops 10000000 | bytes 100000 | tf_op jit(solution)/shard_map/pallas_call | solution.py:427
  22.5 1.2 %copy-done.7 = bf16[4,256,768]{2,1,0:T(8,128)(2,1)} copy-done((bf16[4,256,768]{2,1,0:T(8,128)(2,1)}, bf16[4,256,768]{2,1,0:T(8,128)(2,1)S(1)}, u32[]{:S(2)}) %copy-start.7) | copy-done | bytes 1572888
  23.7 2.6 %collective-permute-start.3 = (bf16[2,256,128]{2,1,0:T(8,128)(2,1)S(1)}, bf16[2,256,128]{2,1,0:T(8,128)(2,1)S(1)}, u32[]{:S(2)}, u32[]{:S(2)}) collective-permute-start(bf16[2,256,128]{2,1,0:T(8,128)(2,1)S(1)} %get-tuple-element.39), channel_id=1, source_target_pairs={{0,2},{2,0},{4,6},{6,4},{8,10},{10,8},{12,14},{14,12},{16,18},{18,... | collective-permute-start | bytes 393224 | tf_op jit(solution)/shard_map/ppermute | solution.py:443
  26.3 1.0 %collective-permute-done.3.other_ref = bf16[2,256,128]{2,1,0:T(8,128)(2,1)S(1)} collective-permute-done((bf16[2,256,128]{2,1,0:T(8,128)(2,1)S(1)}, bf16[2,256,128]{2,1,0:T(8,128)(2,1)S(1)}, u32[]{:S(2)}, u32[]{:S(2)}) %collective-permute-start.3) | collective-permute-done | bytes 131104 | tf_op jit(solution)/shard_map/ppermute | solution.py:443
  27.2 0.2 shard_map.94.own_ref
  27.4 0.0 copy-start.11
  27.5 0.6 %copy-done.11 = bf16[2,256,128]{2,1,0:T(8,128)(2,1)} copy-done((bf16[2,256,128]{2,1,0:T(8,128)(2,1)}, bf16[2,256,128]{2,1,0:T(8,128)(2,1)S(1)}, u32[]{:S(2)}) %copy-start.11) | copy-done | bytes 131096
  28.1 1.6 %collective-permute-start.4 = (bf16[2,256,128]{2,1,0:T(8,128)(2,1)S(1)}, bf16[2,256,128]{2,1,0:T(8,128)(2,1)S(1)}, u32[]{:S(2)}, u32[]{:S(2)}) collective-permute-start(bf16[2,256,128]{2,1,0:T(8,128)(2,1)S(1)} %shard_map.94.own_ref), channel_id=1, source_target_pairs={{0,4},{2,6},{4,0},{6,2},{8,12},{10,14},{12,8},{14,10},{16,20},{18,... | collective-permute-start | bytes 393224 | tf_op jit(solution)/shard_map/ppermute | solution.py:443
  29.7 0.8 %shard_map.98 = bf16[256,1024]{1,0:T(8,128)(2,1)} custom-call(s32[1]{0:T(128)} %bitcast.flags_ref, bf16[512,1024]{1,0:T(8,128)(2,1)S(1)} %copy-done), custom_call_target="tpu_custom_call" | custom-call | flops 10000000 | bytes 100000 | tf_op jit(solution)/shard_map/pallas_call | solution.py:427
  30.5 0.8 %copy-done.8 = bf16[4,256,768]{2,1,0:T(8,128)(2,1)S(1)} copy-done((bf16[4,256,768]{2,1,0:T(8,128)(2,1)S(1)}, bf16[4,256,768]{2,1,0:T(8,128)(2,1)}, u32[]{:S(2)}) %copy-start.8) | copy-done | bytes 1572888
  31.3 1.2 %copy-done.10 = f32[4,256,256]{2,1,0:T(8,128)S(1)} copy-done((f32[4,256,256]{2,1,0:T(8,128)S(1)}, f32[4,256,256]{2,1,0:T(8,128)}, u32[]{:S(2)}) %copy-start.10) | copy-done | bytes 1048600
  32.5 0.8 %copy-done.17 = f32[4,16,256]{2,1,0:T(8,128)S(1)} copy-done((f32[4,16,256]{2,1,0:T(8,128)S(1)}, f32[4,16,256]{2,1,0:T(8,128)}, u32[]{:S(2)}) %copy-start.17) | copy-done | bytes 65560
  33.3 1.8 %shard_map.96.both_ref = f32[2,4,256,256]{3,2,1,0:T(8,128)S(1)} custom-call(s32[2]{0:T(128)S(1)} %pad_add_fusion.1.flags_ref, f32[4,256]{1,0:T(4,128)S(1)} %get-tuple-element.43.norm_ref, bf16[4,256,768]{2,1,0:T(8,128)(2,1)S(1)} %copy-done.8, f32[4,16,256]{2,1,0:T(8,128)S(1)} %copy-done.17, f32[4,256,256]{2,1,0:T(8,128)S(1)} %copy-done.10), custom_call_target="tpu_custom_call" | custom-call | flops 10000000 | bytes 100000 | tf_op jit(solution)/shard_map/pallas_call | solution.py:427
  35.2 0.0 copy-start.19
  35.2 0.2 shard_map.97.own_ref
  35.4 0.4 shard_map.99.path_ref
  35.8 0.0 copy-start.5
  35.8 0.8 %copy-done.5 = f32[2,256,256]{2,1,0:T(8,128)} copy-done((f32[2,256,256]{2,1,0:T(8,128)}, f32[2,256,256]{2,1,0:T(8,128)S(1)}, u32[]{:S(2)}) %copy-start.5) | copy-done | bytes 524312
  36.6 1.1 %collective-permute-start.9 = (bf16[256,1024]{1,0:T(8,128)(2,1)}, bf16[256,1024]{1,0:T(8,128)(2,1)}, u32[]{:S(2)}, u32[]{:S(2)}) collective-permute-start(bf16[256,1024]{1,0:T(8,128)(2,1)} %shard_map.98), channel_id=1, source_target_pairs={{0,1},{1,0},{2,3},{3,2},{4,5},{5,4},{6,7},{7,6},{8,9},{9,8},{10,11... | collective-permute-start | bytes 1572872 | tf_op jit(solution)/shard_map/ppermute | solution.py:443
  37.6 1.6 %collective-permute-start.5 = (bf16[2,256,128]{2,1,0:T(8,128)(2,1)S(1)}, bf16[2,256,128]{2,1,0:T(8,128)(2,1)S(1)}, u32[]{:S(2)}, u32[]{:S(2)}) collective-permute-start(bf16[2,256,128]{2,1,0:T(8,128)(2,1)S(1)} %shard_map.97.own_ref), channel_id=1, source_target_pairs={{0,8},{2,10},{4,12},{6,14},{8,0},{10,2},{12,4},{14,6},{16,24},{18,... | collective-permute-start | bytes 393224 | tf_op jit(solution)/shard_map/ppermute | solution.py:443
  39.2 3.4 %collective-permute-done.5.other_ref.came_ref = bf16[2,256,128]{2,1,0:T(8,128)(2,1)S(1)} collective-permute-done((bf16[2,256,128]{2,1,0:T(8,128)(2,1)S(1)}, bf16[2,256,128]{2,1,0:T(8,128)(2,1)S(1)}, u32[]{:S(2)}, u32[]{:S(2)}) %collective-permute-start.5) | collective-permute-done | bytes 131104 | tf_op jit(solution)/shard_map/ppermute | solution.py:443
  42.6 0.2 shard_map.100
  42.8 4.5 %collective-permute-start.6 = (bf16[2,128,128]{2,1,0:T(8,128)(2,1)S(1)}, bf16[2,128,128]{2,1,0:T(8,128)(2,1)S(1)}, u32[]{:S(2)}, u32[]{:S(2)}) collective-permute-start(bf16[2,128,128]{2,1,0:T(8,128)(2,1)S(1)} %shard_map.100), channel_id=1, source_target_pairs={{0,16},{2,18},{4,20},{6,22},{8,24},{10,26},{12,28},{14,30},{1,17},... | collective-permute-start | bytes 196616 | tf_op jit(solution)/shard_map/ppermute | solution.py:443
  47.3 0.1 pad_add_fusion.flags_ref
  47.4 1.0 %copy-done.6 = f32[2,256,256]{2,1,0:T(8,128)S(1)} copy-done((f32[2,256,256]{2,1,0:T(8,128)S(1)}, f32[2,256,256]{2,1,0:T(8,128)}, u32[]{:S(2)}) %copy-start.6) | copy-done | bytes 524312
  48.4 0.4 shard_map.101.path_ref
  48.8 0.4 collective-permute-done.6.state_ref
  49.2 0.7 %shard_map.102 = (bf16[2,128,128]{2,1,0:T(8,128)(2,1)S(1)}, bf16[2,128,128]{2,1,0:T(8,128)(2,1)S(1)}) custom-call(s32[2]{0:T(128)S(1)} %pad_add_fusion.flags_ref, bf16[2,128,128]{2,1,0:T(8,128)(2,1)S(1)} %collective-permute-done.6.state_ref, f32[2,256,256]{2,1,0:T(8,128)S(1)} %shard_map.101.path_ref), custom_call_target="tpu_custom_call" | custom-call | flops 10000000 | bytes 100000 | tf_op jit(solution)/shard_map/pallas_call | solution.py:427
  49.9 0.1 collective-permute-start.7
  50.0 1.2 %collective-permute-done.7.came_ref = bf16[2,128,128]{2,1,0:T(8,128)(2,1)S(1)} collective-permute-done((bf16[2,128,128]{2,1,0:T(8,128)(2,1)S(1)}, bf16[2,128,128]{2,1,0:T(8,128)(2,1)S(1)}, u32[]{:S(2)}, u32[]{:S(2)}) %collective-permute-start.7) | collective-permute-done | bytes 65568 | tf_op jit(solution)/shard_map/ppermute | solution.py:443
  51.3 0.4 shard_map.103
  51.7 0.2 collective-permute-start.10
  51.9 1.2 %collective-permute-start.8 = (bf16[256,512]{1,0:T(8,128)(2,1)S(1)}, bf16[256,512]{1,0:T(8,128)(2,1)S(1)}, u32[]{:S(2)}, u32[]{:S(2)}) collective-permute-start(bf16[256,512]{1,0:T(8,128)(2,1)S(1)} %shard_map.103), channel_id=1, source_target_pairs={{0,1},{1,0},{2,3},{3,2},{4,5},{5,4},{6,7},{7,6},{8,9},{9,8},{10,11... | collective-permute-start | bytes 786440 | tf_op jit(solution)/shard_map/ppermute | solution.py:443
  53.0 0.7 %shard_map.104.mine_ref = bf16[256,1024]{1,0:T(8,128)(2,1)S(1)} custom-call(s32[1]{0:T(128)} %bitcast.flags_ref, bf16[2,128,128]{2,1,0:T(8,128)(2,1)S(1)} %get-tuple-element.60.keep_ref, bf16[2,128,128]{2,1,0:T(8,128)(2,1)S(1)} %collective-permute-done.7.came_ref, f32[2,4,256,256]{3,2,1,0:T(8,128)S(1)} %shard_map.96.both_ref, f32[1,512]{1,0:T(1,128)S(1)} %bitcast.10, ...), custom_call_target="tpu_custom_call" | custom-call | flops 10000000 | bytes 100000 | tf_op jit(solution)/shard_map/pallas_call | solution.py:427
  53.8 6.7 %collective-permute-done.8.theirs_ref = bf16[256,512]{1,0:T(8,128)(2,1)S(1)} collective-permute-done((bf16[256,512]{1,0:T(8,128)(2,1)S(1)}, bf16[256,512]{1,0:T(8,128)(2,1)S(1)}, u32[]{:S(2)}, u32[]{:S(2)}) %collective-permute-start.8) | collective-permute-done | bytes 262176 | tf_op jit(solution)/shard_map/ppermute | solution.py:443
  60.5 2.3 %shard_map.105 = bf16[256,1024]{1,0:T(8,128)(2,1)} custom-call(s32[1]{0:T(128)} %bitcast.flags_ref, bf16[256,512]{1,0:T(8,128)(2,1)S(1)} %collective-permute-done.8.theirs_ref, bf16[256,1024]{1,0:T(8,128)(2,1)} %collective-permute-done.9.part_ref, bf16[256,1024]{1,0:T(8,128)(2,1)S(1)} %collective-permute-done.10.rest_ref, ...), custom_call_target="tpu_custom_call" | custom-call | flops 10000000 | bytes 100000 | tf_op jit(solution)/shard_map/pallas_call | solution.py:427
  (33 shorter events, 0.1 us)
Async XLA Ops:
  0.0 7.9 %copy-start.1 = (bf16[1024,512]{1,0:T(8,128)(2,1)S(1)}, bf16[1024,512]{1,0:T(8,128)(2,1)}, u32[]{:S(2)}) copy-start(bf16[1024,512]{1,0:T(8,128)(2,1)} %wq_ref.3) | copy-start | bytes 3145732
  0.0 7.9 %copy-start.2 = (bf16[1024,512]{1,0:T(8,128)(2,1)S(1)}, bf16[1024,512]{1,0:T(8,128)(2,1)}, u32[]{:S(2)}) copy-start(bf16[1024,512]{1,0:T(8,128)(2,1)} %wk_ref.3) | copy-start | bytes 3145732
  0.0 7.9 %copy-start.3 = (bf16[1024,512]{1,0:T(8,128)(2,1)S(1)}, bf16[1024,512]{1,0:T(8,128)(2,1)}, u32[]{:S(2)}) copy-start(bf16[1024,512]{1,0:T(8,128)(2,1)} %wv_ref.3) | copy-start | bytes 3145732
  0.0 15.3 %collective-permute-start = (bf16[256,1024]{1,0:T(8,128)(2,1)}, bf16[256,1024]{1,0:T(8,128)(2,1)}, u32[]{:S(2)}, u32[]{:S(2)}) collective-permute-start(bf16[256,1024]{1,0:T(8,128)(2,1)} %x_ref.3), channel_id=1, source_target_pairs={{0,1},{1,0},{2,3},{3,2},{4,5},{5,4},{6,7},{7,6},{8,9},{9,8},{10,11... | collective-permute-start | bytes 1572872 | tf_op jit(solution)/shard_map/ppermute | solution.py:443
  3.0 1.1 %copy-start.13 = (bf16[256,1024]{1,0:T(8,128)(2,1)S(1)}, bf16[256,1024]{1,0:T(8,128)(2,1)}, u32[]{:S(2)}) copy-start(bf16[256,1024]{1,0:T(8,128)(2,1)} %x_ref.3) | copy-start | bytes 1572868
  4.1 3.8 %copy-start.15 = (f32[3,4,512]{2,1,0:T(4,128)S(1)}, f32[3,4,512]{2,1,0:T(4,128)}, u32[]{:S(2)}) copy-start(f32[3,4,512]{2,1,0:T(4,128)} %conv_ref.3) | copy-start | bytes 73732
  4.1 3.8 %copy-start.18 = (bf16[1024,4]{0,1:T(4,128)(2,1)S(1)}, bf16[1024,4]{0,1:T(4,128)(2,1)}, u32[]{:S(2)}) copy-start(bf16[1024,4]{0,1:T(4,128)(2,1)} %param.13) | copy-start | bytes 24580
  4.1 3.8 %copy-start.20 = (f32[4]{0:T(128)S(1)}, f32[4]{0:T(128)}, u32[]{:S(2)}) copy-start(f32[4]{0:T(128)} %bias_ref.3) | copy-start | bytes 52
  4.1 11.0 %collective-permute-start.1 = (bf16[16,1024]{1,0:T(8,128)(2,1)S(1)}, bf16[16,1024]{1,0:T(8,128)(2,1)S(1)}, u32[]{:S(2)}, u32[]{:S(2)}) collective-permute-start(bf16[16,1024]{1,0:T(8,128)(2,1)S(1)} %get-tuple-element.36.tail_ref), channel_id=1, source_target_pairs={{0,1},{1,2},{2,3},{3,4},{4,5},{5,6},{6,7},{7,8},{8,9},{9,10},{10,1... | collective-permute-start | bytes 98312 | tf_op jit(solution)/shard_map/ppermute | solution.py:443
  6.3 8.8 %collective-permute-start.2 = (bf16[16,1024]{1,0:T(8,128)(2,1)S(1)}, bf16[16,1024]{1,0:T(8,128)(2,1)S(1)}, u32[]{:S(2)}, u32[]{:S(2)}) collective-permute-start(bf16[16,1024]{1,0:T(8,128)(2,1)S(1)} %get-tuple-element.36.tail_ref), channel_id=1, source_target_pairs={{0,2},{2,4},{4,6},{6,8},{8,10},{10,12},{12,14},{14,16},{16,18},{18... | collective-permute-start | bytes 98312 | tf_op jit(solution)/shard_map/ppermute | solution.py:443
  7.8 7.5 %copy-start.4 = (bf16[1024,512]{1,0:T(8,128)(2,1)S(1)}, bf16[1024,512]{1,0:T(8,128)(2,1)}, u32[]{:S(2)}) copy-start(bf16[1024,512]{1,0:T(8,128)(2,1)} %wv_ref.3) | copy-start | bytes 3145732
  7.9 1.1 %copy-start.14 = (bf16[256,1024]{1,0:T(8,128)(2,1)S(1)}, bf16[256,1024]{1,0:T(8,128)(2,1)}, u32[]{:S(2)}) copy-start(bf16[256,1024]{1,0:T(8,128)(2,1)} %x_ref.3) | copy-start | bytes 1572868
  14.9 7.6 %copy-start.9 = (f32[4,256,256]{2,1,0:T(8,128)}, f32[4,256,256]{2,1,0:T(8,128)S(1)}, u32[]{:S(2)}) copy-start(f32[4,256,256]{2,1,0:T(8,128)S(1)} %get-tuple-element.46.early_ref) | copy-start | bytes 3145732
  15.3 14.4 %copy-start = (bf16[512,1024]{1,0:T(8,128)(2,1)S(1)}, bf16[512,1024]{1,0:T(8,128)(2,1)}, u32[]{:S(2)}) copy-start(bf16[512,1024]{1,0:T(8,128)(2,1)} %w_ref.3) | copy-start | bytes 3145732
  22.5 1.2 %copy-start.7 = (bf16[4,256,768]{2,1,0:T(8,128)(2,1)}, bf16[4,256,768]{2,1,0:T(8,128)(2,1)S(1)}, u32[]{:S(2)}) copy-start(bf16[4,256,768]{2,1,0:T(8,128)(2,1)S(1)} %get-tuple-element.44.held_ref) | copy-start | bytes 4718596
  23.6 3.8 %copy-start.16 = (f32[4,16,256]{2,1,0:T(8,128)}, f32[4,16,256]{2,1,0:T(8,128)S(1)}, u32[]{:S(2)}) copy-start(f32[4,16,256]{2,1,0:T(8,128)S(1)} %get-tuple-element.45.mini_ref) | copy-start | bytes 196612
  23.7 3.6 %collective-permute-start.3 = (bf16[2,256,128]{2,1,0:T(8,128)(2,1)S(1)}, bf16[2,256,128]{2,1,0:T(8,128)(2,1)S(1)}, u32[]{:S(2)}, u32[]{:S(2)}) collective-permute-start(bf16[2,256,128]{2,1,0:T(8,128)(2,1)S(1)} %get-tuple-element.39), channel_id=1, source_target_pairs={{0,2},{2,0},{4,6},{6,4},{8,10},{10,8},{12,14},{14,12},{16,18},{18,... | collective-permute-start | bytes 393224 | tf_op jit(solution)/shard_map/ppermute | solution.py:443
  27.4 0.7 %copy-start.11 = (bf16[2,256,128]{2,1,0:T(8,128)(2,1)}, bf16[2,256,128]{2,1,0:T(8,128)(2,1)S(1)}, u32[]{:S(2)}) copy-start(bf16[2,256,128]{2,1,0:T(8,128)(2,1)S(1)} %collective-permute-done.3.other_ref) | copy-start | bytes 393220
  28.1 7.1 %collective-permute-start.4 = (bf16[2,256,128]{2,1,0:T(8,128)(2,1)S(1)}, bf16[2,256,128]{2,1,0:T(8,128)(2,1)S(1)}, u32[]{:S(2)}, u32[]{:S(2)}) collective-permute-start(bf16[2,256,128]{2,1,0:T(8,128)(2,1)S(1)} %shard_map.94.own_ref), channel_id=1, source_target_pairs={{0,4},{2,6},{4,0},{6,2},{8,12},{10,14},{12,8},{14,10},{16,20},{18,... | collective-permute-start | bytes 393224 | tf_op jit(solution)/shard_map/ppermute | solution.py:443
  29.7 1.6 %copy-start.8 = (bf16[4,256,768]{2,1,0:T(8,128)(2,1)S(1)}, bf16[4,256,768]{2,1,0:T(8,128)(2,1)}, u32[]{:S(2)}) copy-start(bf16[4,256,768]{2,1,0:T(8,128)(2,1)} %copy-done.7) | copy-start | bytes 4718596
  31.3 1.2 %copy-start.10 = (f32[4,256,256]{2,1,0:T(8,128)S(1)}, f32[4,256,256]{2,1,0:T(8,128)}, u32[]{:S(2)}) copy-start(f32[4,256,256]{2,1,0:T(8,128)} %copy-done.9) | copy-start | bytes 3145732
  32.5 0.8 %copy-start.17 = (f32[4,16,256]{2,1,0:T(8,128)S(1)}, f32[4,16,256]{2,1,0:T(8,128)}, u32[]{:S(2)}) copy-start(f32[4,16,256]{2,1,0:T(8,128)} %copy-done.16) | copy-start | bytes 196612
  33.3 1.8 %copy-start.12 = (bf16[2,256,128]{2,1,0:T(8,128)(2,1)S(1)}, bf16[2,256,128]{2,1,0:T(8,128)(2,1)}, u32[]{:S(2)}) copy-start(bf16[2,256,128]{2,1,0:T(8,128)(2,1)} %copy-done.11) | copy-start | bytes 393220
  35.2 16.1 %copy-start.19 = (f32[512]{0:T(512)S(1)}, f32[512]{0:T(512)}, u32[]{:S(2)}) copy-start(f32[512]{0:T(512)} %param.16) | copy-start | bytes 6148
  35.8 0.8 %copy-start.5 = (f32[2,256,256]{2,1,0:T(8,128)}, f32[2,256,256]{2,1,0:T(8,128)S(1)}, u32[]{:S(2)}) copy-start(f32[2,256,256]{2,1,0:T(8,128)S(1)} %shard_map.99.path_ref) | copy-start | bytes 1572868
  36.6 15.1 %collective-permute-start.9 = (bf16[256,1024]{1,0:T(8,128)(2,1)}, bf16[256,1024]{1,0:T(8,128)(2,1)}, u32[]{:S(2)}, u32[]{:S(2)}) collective-permute-start(bf16[256,1024]{1,0:T(8,128)(2,1)} %shard_map.98), channel_id=1, source_target_pairs={{0,1},{1,0},{2,3},{3,2},{4,5},{5,4},{6,7},{7,6},{8,9},{9,8},{10,11... | collective-permute-start | bytes 1572872 | tf_op jit(solution)/shard_map/ppermute | solution.py:443
  37.6 5.0 %collective-permute-start.5 = (bf16[2,256,128]{2,1,0:T(8,128)(2,1)S(1)}, bf16[2,256,128]{2,1,0:T(8,128)(2,1)S(1)}, u32[]{:S(2)}, u32[]{:S(2)}) collective-permute-start(bf16[2,256,128]{2,1,0:T(8,128)(2,1)S(1)} %shard_map.97.own_ref), channel_id=1, source_target_pairs={{0,8},{2,10},{4,12},{6,14},{8,0},{10,2},{12,4},{14,6},{16,24},{18,... | collective-permute-start | bytes 393224 | tf_op jit(solution)/shard_map/ppermute | solution.py:443
  42.8 6.4 %collective-permute-start.6 = (bf16[2,128,128]{2,1,0:T(8,128)(2,1)S(1)}, bf16[2,128,128]{2,1,0:T(8,128)(2,1)S(1)}, u32[]{:S(2)}, u32[]{:S(2)}) collective-permute-start(bf16[2,128,128]{2,1,0:T(8,128)(2,1)S(1)} %shard_map.100), channel_id=1, source_target_pairs={{0,16},{2,18},{4,20},{6,22},{8,24},{10,26},{12,28},{14,30},{1,17},... | collective-permute-start | bytes 196616 | tf_op jit(solution)/shard_map/ppermute | solution.py:443
  47.4 1.0 %copy-start.6 = (f32[2,256,256]{2,1,0:T(8,128)S(1)}, f32[2,256,256]{2,1,0:T(8,128)}, u32[]{:S(2)}) copy-start(f32[2,256,256]{2,1,0:T(8,128)} %copy-done.5) | copy-start | bytes 1572868
  49.9 1.3 %collective-permute-start.7 = (bf16[2,128,128]{2,1,0:T(8,128)(2,1)S(1)}, bf16[2,128,128]{2,1,0:T(8,128)(2,1)S(1)}, u32[]{:S(2)}, u32[]{:S(2)}) collective-permute-start(bf16[2,128,128]{2,1,0:T(8,128)(2,1)S(1)} %get-tuple-element.61), channel_id=1, source_target_pairs={{0,2},{2,0},{4,6},{6,4},{8,10},{10,8},{12,14},{14,12},{16,18},{18,... | collective-permute-start | bytes 196616 | tf_op jit(solution)/shard_map/ppermute | solution.py:443
  51.7 8.8 %collective-permute-start.10 = (bf16[256,1024]{1,0:T(8,128)(2,1)}, bf16[256,1024]{1,0:T(8,128)(2,1)S(1)}, u32[]{:S(2)}, u32[]{:S(2)}) collective-permute-start(bf16[256,1024]{1,0:T(8,128)(2,1)} %collective-permute-done.9.part_ref), channel_id=1, source_target_pairs={{0,2},{2,0},{4,6},{6,4},{8,10},{10,8},{12,14},{14,12},{16,18},{18,... | collective-permute-start | bytes 1572872 | tf_op jit(solution)/shard_map/ppermute | solution.py:443
  51.9 8.6 %collective-permute-start.8 = (bf16[256,512]{1,0:T(8,128)(2,1)S(1)}, bf16[256,512]{1,0:T(8,128)(2,1)S(1)}, u32[]{:S(2)}, u32[]{:S(2)}) collective-permute-start(bf16[256,512]{1,0:T(8,128)(2,1)S(1)} %shard_map.103), channel_id=1, source_target_pairs={{0,1},{1,0},{2,3},{3,2},{4,5},{5,4},{6,7},{7,6},{8,9},{9,8},{10,11... | collective-permute-start | bytes 786440 | tf_op jit(solution)/shard_map/ppermute | solution.py:443

commit v3 on v2

--- a/solution.py
+++ b/solution.py
@@ -89,11 +89,30 @@
     width = BASE
     while width < lanes:
         mask = (row // (2 * width) == lane // (2 * width)) & (row // width != lane // width)
+        picks = range(width, lanes, 2 * width)
+
+        def odd(full):
+            return jnp.concatenate([full[at : at + width] for at in picks], 0)
+
+        def spread(picked):
+            none = jnp.zeros((width, lanes), F32)
+            return jnp.concatenate(
+                [
+                    each
+                    for index in range(len(picks))
+                    for each in (none, picked[index * width : (index + 1) * width])
+                ],
+                0,
+            )
+
         inner = [
-            dot_wide(jnp.where(mask, window, 0.0), inverse)
+            dot_wide(odd(jnp.where(mask, window, 0.0)), inverse)
             for window, inverse in zip(windows, inverses)
         ]
-        inverses = [inverse - dot_wide(inverse, each) for inverse, each in zip(inverses, inner)]
+        inverses = [
+            inverse - spread(dot_wide(odd(inverse), spread(each)))
+            for inverse, each in zip(inverses, inner)
+        ]
         width *= 2
     count = len(starts)
     groups = [inverses[at : at + count] for at in range(0, len(inverses), count)]
@@ -176,11 +195,12 @@
     for key, value, inverse, norm_row in zip(keys, values, inverses, norm_rows):
         fresh = dot_half(inverse, value)
         weight = dot_half(inverse * norm_row, key)
-        solved.append(jnp.concatenate([fresh, weight], 1))
+        solved.append(jnp.concatenate([weight, fresh], 1))
     pairs = []
     for key, each, norm in zip(keys, solved, norms):
-        moved = dot_half(each * norm, key, TN)
-        pairs.append(jnp.concatenate([eye - moved[dim:], moved[:dim]], 0))
+        top, rest = split(each * norm)
+        moved = dot(key, top, TN) + dot(key, rest, TN)
+        pairs.append(jnp.concatenate([eye - moved[:, :dim], moved[:, dim:]], 1))
     return pairs, solved, norm_rows
 
 
@@ -189,8 +209,8 @@
     row = lax.broadcasted_iota(jnp.int32, (rows, rows), 0)
     lane = lax.broadcasted_iota(jnp.int32, (rows, rows), 1)
     attend = jnp.where(row >= lane, dot(query, key, NT) * norm_row, 0.0)
-    seen = dot(attend.astype(BF16), solved)
-    return jnp.concatenate([seen[:, :dim], query.astype(F32) - seen[:, dim:]], 1)
+    seen = dot_half(attend, solved)
+    return jnp.concatenate([query.astype(F32) - seen[:, :dim], seen[:, dim:]], 1)
 
 
 def spans_of(count, width):
@@ -293,12 +313,11 @@
         held_ref[head] = jnp.concatenate(
             [
                 solved[head].astype(BF16),
-                queries[head],
-                keys[head],
+                jnp.concatenate([queries[head], keys[head]], 1),
                 low.astype(BF16),
                 few_pairs[head].astype(BF16),
             ],
-            1,
+            0,
         )
         wholes.append(compose(low, jnp.where(swapped, early[head], late)).astype(BF16))
     for head in range(kept):
@@ -311,37 +330,38 @@
             send_ref[head] = jnp.where(bit == 1, one, two)
 
 
+def after(reads, pair):
+    dim = pair.shape[0]
+    through = dot(reads[:, :dim].astype(BF16), pair)
+    return jnp.concatenate([through[:, :dim], through[:, dim:] + reads[:, dim:]], 1)
+
+
 def look_kernel(taps, flags_ref, norm_ref, held_ref, mini_ref, early_ref, both_ref):
     swapped = flags_ref[0] == 1
     heads = held_ref.shape[0]
-    rows = held_ref.shape[1]
-    dim = held_ref.shape[2] // 6
+    dim = held_ref.shape[2] // 2
+    rows = (held_ref.shape[1] - 2 * dim) // 2
     row = lax.broadcasted_iota(jnp.int32, (HALO, 2 * dim), 0)
     for head in range(heads):
         late = look(
-            held_ref[head, :, 2 * dim : 3 * dim],
-            held_ref[head, :, 3 * dim : 4 * dim],
+            held_ref[head, rows : 2 * rows, :dim],
+            held_ref[head, rows : 2 * rows, dim:],
             norm_ref[head : head + 1],
-            held_ref[head, :, : 2 * dim],
+            held_ref[head, :rows],
         )
-        early = early_ref[head]
-        few = held_ref[head, :, 5 * dim :]
-        through = dot(early[:, dim:].astype(BF16), few, NT)
-        early = jnp.concatenate([early[:, :dim] + through[:, dim:], through[:, :dim]], 1)
+        first = held_ref[head, 2 * rows : 2 * rows + dim]
+        early = after(early_ref[head], held_ref[head, 2 * rows + dim :])
         top = jnp.where(row < taps - 1, mini_ref[head], early[:HALO])
         early = jnp.concatenate([top, early[HALO:]], 0)
-        first = held_ref[head, :, 4 * dim : 5 * dim]
-        later = jnp.where(swapped, early, late)
-        through = dot(later[:, dim:].astype(BF16), first, NT)
-        later = jnp.concatenate([later[:, :dim] + through[:, dim:], through[:, :dim]], 1)
+        later = after(jnp.where(swapped, early, late), first)
         both_ref[0, head] = jnp.where(swapped, later, early)
         both_ref[1, head] = jnp.where(swapped, late, later)
 
 
 def compose(low, high):
-    dim = low.shape[1]
-    joined = dot_wide(low, high[:dim])
-    return jnp.concatenate([joined[:dim], joined[dim:] + high[dim:]], 0)
+    dim = low.shape[0]
+    joined = dot_wide(high[:, :dim], low)
+    return jnp.concatenate([joined[:, :dim], joined[:, dim:] + high[:, dim:]], 1)
 
 
 def join_kernel(flags_ref, own_ref, other_ref, send_ref):
@@ -350,42 +370,42 @@
         own, other = own_ref[head], other_ref[head]
         low = jnp.where(later, other, own)
         high = jnp.where(later, own, other)
-        dim = low.shape[1]
-        joined = dot(low, high[:dim])
-        start = 2 * dim - send_ref.shape[1]
-        if start < dim:
-            send_ref[head, : dim - start] = joined[start:dim].astype(BF16)
-        send_ref[head, dim - start :] = (joined[dim:] + high[dim:].astype(F32)).astype(BF16)
+        dim = low.shape[0]
+        landed = send_ref.shape[2] - dim
+        joined = dot(high[:, :dim], low)
+        if landed > 0:
+            send_ref[head, :, :dim] = joined[:, :dim].astype(BF16)
+        send_ref[head, :, landed:] = (joined[:, dim:] + high[:, dim:].astype(F32)).astype(BF16)
 
 
 def open_kernel(flags_ref, own_ref, other_ref, path_ref):
-    dim = own_ref.shape[2]
-    row = lax.broadcasted_iota(jnp.int32, (2 * dim, dim), 0)
-    lane = lax.broadcasted_iota(jnp.int32, (2 * dim, dim), 1)
+    dim = own_ref.shape[1]
+    row = lax.broadcasted_iota(jnp.int32, (dim, 2 * dim), 0)
+    lane = lax.broadcasted_iota(jnp.int32, (dim, 2 * dim), 1)
     for head in range(own_ref.shape[0]):
-        path_ref[head, :, :dim] = (row == lane).astype(F32)
+        path_ref[head, :dim] = (row == lane).astype(F32)
         low = jnp.where(flags_ref[0] == 1, other_ref[head], own_ref[head])
-        path_ref[head, :, dim:] = low.astype(F32)
+        path_ref[head, dim:] = low.astype(F32)
 
 
 def path_kernel(flags_ref, path_ref, came_ref, out_ref):
-    dim = came_ref.shape[2]
+    dim = came_ref.shape[1]
     for head in range(came_ref.shape[0]):
         path = path_ref[head]
-        through = dot_wide(came_ref[head].astype(F32), path[:dim])
-        longer = jnp.concatenate([through[:dim], through[dim:] + path[dim:]], 0)
+        through = dot_half(path[:, :dim], came_ref[head])
+        longer = jnp.concatenate([through[:, :dim], through[:, dim:] + path[:, dim:]], 1)
         out_ref[head] = jnp.where(flags_ref[0] == 1, longer, path)
 
 
 def enter_kernel(flags_ref, state_ref, path_ref, keep_ref, send_ref):
-    dim = state_ref.shape[2]
+    dim = state_ref.shape[1]
     for head in range(keep_ref.shape[0]):
         state = jnp.where(flags_ref[1] == 1, state_ref[head], jnp.zeros_like(state_ref[head]))
         path = path_ref[head]
-        both = (dot(state, path[:dim].astype(BF16)) + path[dim:]).astype(BF16)
+        both = (dot(path[:, :dim].astype(BF16), state) + path[:, dim:]).astype(BF16)
         later = flags_ref[0] == 1
-        keep_ref[head] = jnp.where(later, both[:, dim:], both[:, :dim])
-        send_ref[head] = jnp.where(later, both[:, :dim], both[:, dim:])
+        keep_ref[head] = jnp.where(later, both[dim:], both[:dim])
+        send_ref[head] = jnp.where(later, both[:dim], both[dim:])
 
 
 def finish_kernel(place, flags_ref, keep_ref, came_ref, both_ref, gain_ref, out_ref):
@@ -395,8 +415,8 @@
         state = keep_ref[head % count]
         if count < heads:
             state = jnp.where(flags_ref[0] == head // count, state, came_ref[head % count])
-        reach = both_ref[place, head, :, dim:].astype(BF16)
-        rows = both_ref[place, head, :, :dim] + dot(reach, state, NT)
+        reach = both_ref[place, head, :, :dim].astype(BF16)
+        rows = both_ref[place, head, :, dim:] + dot(reach, state)
         scale = lax.rsqrt(jnp.mean(rows * rows, 1, keepdims=True) + 1e-5)
         out_ref[:, span] = (rows * scale * gain_ref[:, span]).astype(BF16)
 
@@ -406,18 +426,12 @@
     out_ref[...] = dot(normed_ref[...], w_ref[...]).astype(BF16)
 
 
-def half_kernel(flags_ref, w_ref, part_ref):
-    rows = part_ref.shape[0]
-    part_ref[...] = w_ref[pl.ds(pl.multiple_of(flags_ref[0] * rows, rows), rows)]
-
-
-def output_kernel(flags_ref, theirs_ref, part_ref, rest_ref, mine_ref, out_ref):
-    rows = part_ref.shape[0]
-    later = flags_ref[0] == 1
-    low, high = theirs_ref[:, :rows], theirs_ref[:, rows:]
-    total = dot(jnp.where(later, high, low), part_ref[...])
-    total = total + dot(jnp.where(later, low, high), rest_ref[...])
-    theirs = total.astype(BF16).astype(F32)
+def hold_kernel(w_ref, held_ref):
+    held_ref[...] = w_ref[...]
+
+
+def output_kernel(theirs_ref, w_ref, mine_ref, out_ref):
+    theirs = dot(theirs_ref[...], w_ref[...]).astype(BF16).astype(F32)
     out_ref[...] = (mine_ref[...].astype(F32) + theirs).astype(BF16)
 
 
@@ -475,7 +489,7 @@
         swapped = jnp.zeros((), jnp.int32)
 
     gain = norm_gain.reshape(1, columns)
-    pair_shape = (heads, 2 * dim, dim)
+    pair_shape = (heads, dim, 2 * dim)
     kept = heads // 2 if heads % 2 == 0 else heads
     kept_shape = (kept,) + pair_shape[1:]
     levels = shards.bit_length() - 1
@@ -496,7 +510,7 @@
             (kept_shape, BF16),
             (kept_shape, BF16),
             ((heads, rows), F32),
-            ((heads, rows, 6 * dim), BF16),
+            ((heads, 2 * rows + 2 * dim, 2 * dim), BF16),
             ((heads, HALO, 2 * dim), F32),
         ],
         [late] + weights + [head, tail, halo, behind, pair0],
@@ -504,6 +518,9 @@
         scratch=[pltpu.VMEM((3, rows + 3 * HALO, columns), F32)],
         grant=24,
     )
+    if groups == 2:
+        w_sent, keep = together(w_out, keep)
+        w_other = shift(w_sent, "head", swap)
     own = keep
     for level in range(levels):
         partner = [(i, i ^ (1 << level)) for i in range(shards)]
@@ -518,20 +535,13 @@
                 scalars=[flags],
             )[0]
             came, path, both = together(came, path, both)
-            if groups == 2:
-                part = call(
-                    half_kernel,
-                    [((w_out.shape[0] // 2, width), BF16)],
-                    [w_out],
-                    scalars=[bits[0]],
-                )[0]
         elif level > 1:
             came, path = together(came, path)
         if level == levels - 1:
             break
         send = call(
             join_kernel,
-            [((kept, dim if level == levels - 2 else 2 * dim, dim), BF16)],
+            [((kept, dim, dim if level == levels - 2 else 2 * dim), BF16)],
             [own, came],
             scalars=[bits[level]],
         )[0]
@@ -545,9 +555,6 @@
             path = call(
                 path_kernel, [((kept, 2 * dim, 2 * dim), F32)], [path, came], scalars=[bits[level]]
             )[0]
-            if level == 1 and groups == 2:
-                part, path = together(part, path)
-                part = shift(part, "head", swap)
         own = send
     keep, send = call(
         enter_kernel,
@@ -571,14 +578,10 @@
             scalars=[bits[0]],
             scratch=[pltpu.VMEM((rows, columns), BF16)],
         )[0]
-        part, gone = together(part, gone)
-        rest = shift(part, "seq", [(i, i ^ 1) for i in range(shards)])
-        return call(
-            output_kernel,
-            [((rows, width), BF16)],
-            [theirs, part, rest, mine],
-            scalars=[bits[0]],
-        )[0]
+        w_other, gone = together(w_other, gone)
+        whole = call(hold_kernel, [(w_out.shape, BF16)], [w_other])[0]
+        theirs, whole = together(theirs, whole)
+        return call(output_kernel, [((rows, width), BF16)], [theirs, whole, mine])[0]
     normed = call(
         functools.partial(finish_kernel, 0),
         [((rows, columns), BF16)],

time: 63.3 us -> 59.2 us (0.935)
  local copies, waits for them, and re-layouts: 8.71 us -> 5.95 us
  waiting for transfers between devices: 13.1 us -> 12.1 us
    unnamed x42 -> x26, local copies, waits for them, and re-layouts: 8.71 us -> 5.95 us
    ppermute x11 -> x10, waiting for transfers between devices: 13.1 us -> 12.1 us  [shift(): return lax.ppermute(block, axes, pairs)]
    ppermute x11 -> x10, starting transfers between devices: 19.4 us -> 18.9 us  [shift(): return lax.ppermute(block, axes, pairs)]
  transfers between devices with their start and end apart: 11 -> 10, of which waited for: 7 -> 7; matrix products, arithmetic and copies ran while one was open for 0% -> 0% of each run, Pallas kernels for 17% -> 23%
where the time goes in v3:
time: 59.2 us; the launch traced here: 58.7 us
  Pallas kernels  21.5 us (36%)
  starting transfers between devices  18.9 us (32%)
  waiting for transfers between devices  12.1 us (20%)
  local copies, waits for them, and re-layouts  5.95 us (10%)
    pallas_call x15, Pallas kernels, call(): pl.pallas_call(kernel, out_shape=[jax.ShapeDtypeStruct(shape, dtype) for...  21.5 us
    ppermute x10, starting transfers between devices, shift(): return lax.ppermute(block, axes, pairs)  18.9 us
    ppermute x10, waiting for transfers between devices, shift(): return lax.ppermute(block, axes, pairs)  12.1 us
    unnamed x26, local copies, waits for them, and re-layouts  5.95 us
  transfers between devices with their start and end apart: 10, of which 7 were waited for; matrix products, arithmetic and copies ran while one was open for 0% of the time, Pallas kernels for 23%

profile of v3, /device:TPU:0, one launch (start us, length us, event | category | flops | bytes accessed | tf_op | source)
XLA Modules:
  0.0 58.7 jit_solution(17355946769858082552)
XLA Ops:
  0.0 3.0 %collective-permute-start = (bf16[256,1024]{1,0:T(8,128)(2,1)}, bf16[256,1024]{1,0:T(8,128)(2,1)}, u32[]{:S(2)}, u32[]{:S(2)}) collective-permute-start(bf16[256,1024]{1,0:T(8,128)(2,1)} %x_ref.3), channel_id=1, source_target_pairs={{0,1},{1,0},{2,3},{3,2},{4,5},{5,4},{6,7},{7,6},{8,9},{9,8},{10,11... | collective-permute-start | bytes 1572872 | tf_op jit(solution)/shard_map/ppermute | solution.py:457
  3.0 1.1 %copy-done.7 = bf16[256,1024]{1,0:T(8,128)(2,1)S(1)} copy-done((bf16[256,1024]{1,0:T(8,128)(2,1)S(1)}, bf16[256,1024]{1,0:T(8,128)(2,1)}, u32[]{:S(2)}) %copy-start.7) | copy-done | bytes 524312
  4.1 2.2 %collective-permute-start.1 = (bf16[16,1024]{1,0:T(8,128)(2,1)S(1)}, bf16[16,1024]{1,0:T(8,128)(2,1)S(1)}, u32[]{:S(2)}, u32[]{:S(2)}) collective-permute-start(bf16[16,1024]{1,0:T(8,128)(2,1)S(1)} %get-tuple-element.38.tail_ref), channel_id=1, source_target_pairs={{0,1},{1,2},{2,3},{3,4},{4,5},{5,6},{6,7},{7,8},{8,9},{9,10},{10,1... | collective-permute-start | bytes 98312 | tf_op jit(solution)/shard_map/ppermute | solution.py:457
  6.3 1.5 %collective-permute-start.2 = (bf16[16,1024]{1,0:T(8,128)(2,1)S(1)}, bf16[16,1024]{1,0:T(8,128)(2,1)S(1)}, u32[]{:S(2)}, u32[]{:S(2)}) collective-permute-start(bf16[16,1024]{1,0:T(8,128)(2,1)S(1)} %get-tuple-element.38.tail_ref), channel_id=1, source_target_pairs={{0,2},{2,4},{4,6},{6,8},{8,10},{10,12},{12,14},{14,16},{16,18},{18... | collective-permute-start | bytes 98312 | tf_op jit(solution)/shard_map/ppermute | solution.py:457
  7.8 0.1 pad_add_fusion.1.flags_ref
  7.9 0.0 copy-done
  7.9 0.0 copy-done.1
  7.9 0.0 copy-done.2
  7.9 0.0 copy-done.9
  7.9 0.0 copy-done.10
  7.9 0.0 copy-done.12
  7.9 0.0 copy-start.8
  7.9 1.0 %copy-done.8 = bf16[256,1024]{1,0:T(8,128)(2,1)S(1)} copy-done((bf16[256,1024]{1,0:T(8,128)(2,1)S(1)}, bf16[256,1024]{1,0:T(8,128)(2,1)}, u32[]{:S(2)}) %copy-start.8) | copy-done | bytes 524312
  8.9 6.0 %shard_map.92 = (f32[4,128,256]{2,1,0:T(8,128)S(1)}, f32[4,256,256]{2,1,0:T(8,128)S(1)}) custom-call(f32[4]{0:T(128)S(1)} %copy-done.12, bf16[256,1024]{1,0:T(8,128)(2,1)S(1)} %copy-done.8, bf16[1024,512]{1,0:T(8,128)(2,1)S(1)} %copy-done, bf16[1024,512]{1,0:T(8,128)(2,1)S(1)} %copy-done.1, bf16[1024,512]{1,0:T(8,128)(2,1)S(1)} %copy-done.2, ...), custom_call_target="tpu_custom_call" | custom-call | flops 10000000 | bytes 100000 | tf_op jit(solution)/shard_map/pallas_call | solution.py:441
  15.0 0.2 collective-permute-done.1.halo_ref
  15.1 0.0 collective-permute-done.2.behind_ref
  15.1 0.1 collective-permute-done.x_ref
  15.3 6.8 %shard_map.93 = (bf16[2,128,256]{2,1,0:T(8,128)(2,1)S(1)}, bf16[2,128,256]{2,1,0:T(8,128)(2,1)S(1)}, f32[4,256]{1,0:T(4,128)S(1)}, bf16[4,768,256]{2,1,0:T(8,128)(2,1)S(1)}, f32[4,16,256]{2,1,0:T(8,128)S(1)}) custom-call(s32[2]{0:T(128)S(1)} %pad_add_fusion.1.flags_ref, f32[4]{0:T(128)S(1)} %copy-done.12, bf16[256,1024]{1,0:T(8,128)(2,1)} %collective-permute-done.x_ref, ...), custom_call_target="tpu_custom_call" | custom-call | flops 10000000 | bytes 100000 | tf_op jit(solution)/shard_map/pallas_call | solution.py:441
  22.1 1.2 %copy-done.3 = bf16[4,768,256]{2,1,0:T(8,128)(2,1)} copy-done((bf16[4,768,256]{2,1,0:T(8,128)(2,1)}, bf16[4,768,256]{2,1,0:T(8,128)(2,1)S(1)}, u32[]{:S(2)}) %copy-start.3) | copy-done | bytes 1572888
  23.3 3.4 %collective-permute-start.9 = (bf16[512,1024]{1,0:T(8,128)(2,1)}, bf16[512,1024]{1,0:T(8,128)(2,1)}, u32[]{:S(2)}, u32[]{:S(2)}) collective-permute-start(bf16[512,1024]{1,0:T(8,128)(2,1)} %w_ref.1), channel_id=1, source_target_pairs={{0,1},{1,0},{2,3},{3,2},{4,5},{5,4},{6,7},{7,6},{8,9},{9,8},{10,11... | collective-permute-start | bytes 3145736 | tf_op jit(solution)/shard_map/ppermute | solution.py:457
  26.7 0.0 collective-permute-start.3
  26.7 1.3 %collective-permute-done.3.other_ref = bf16[2,128,256]{2,1,0:T(8,128)(2,1)S(1)} collective-permute-done((bf16[2,128,256]{2,1,0:T(8,128)(2,1)S(1)}, bf16[2,128,256]{2,1,0:T(8,128)(2,1)S(1)}, u32[]{:S(2)}, u32[]{:S(2)}) %collective-permute-start.3) | collective-permute-done | bytes 131104 | tf_op jit(solution)/shard_map/ppermute | solution.py:457
  28.1 0.2 shard_map.94.own_ref
  28.2 1.6 %collective-permute-start.4 = (bf16[2,128,256]{2,1,0:T(8,128)(2,1)S(1)}, bf16[2,128,256]{2,1,0:T(8,128)(2,1)S(1)}, u32[]{:S(2)}, u32[]{:S(2)}) collective-permute-start(bf16[2,128,256]{2,1,0:T(8,128)(2,1)S(1)} %shard_map.94.own_ref), channel_id=1, source_target_pairs={{0,4},{2,6},{4,0},{6,2},{8,12},{10,14},{12,8},{14,10},{16,20},{18,... | collective-permute-start | bytes 393224 | tf_op jit(solution)/shard_map/ppermute | solution.py:457
  29.9 1.4 %copy-done.4 = bf16[4,768,256]{2,1,0:T(8,128)(2,1)S(1)} copy-done((bf16[4,768,256]{2,1,0:T(8,128)(2,1)S(1)}, bf16[4,768,256]{2,1,0:T(8,128)(2,1)}, u32[]{:S(2)}) %copy-start.4) | copy-done | bytes 1572888
  31.3 1.2 %copy-done.6 = f32[4,256,256]{2,1,0:T(8,128)S(1)} copy-done((f32[4,256,256]{2,1,0:T(8,128)S(1)}, f32[4,256,256]{2,1,0:T(8,128)}, u32[]{:S(2)}) %copy-start.6) | copy-done | bytes 1048600
  32.5 1.9 %shard_map.96.both_ref = f32[2,4,256,256]{3,2,1,0:T(8,128)S(1)} custom-call(s32[2]{0:T(128)S(1)} %pad_add_fusion.1.flags_ref, f32[4,256]{1,0:T(4,128)S(1)} %get-tuple-element.46.norm_ref, bf16[4,768,256]{2,1,0:T(8,128)(2,1)S(1)} %copy-done.4, f32[4,16,256]{2,1,0:T(8,128)S(1)} %get-tuple-element.48.mini_ref, f32[4,256,256]{2,1,0:T(8,128)S(1)} %copy-done.6), custom_call_target="tpu_custom_call" | custom-call | flops 10000000 | bytes 100000 | tf_op jit(solution)/shard_map/pallas_call | solution.py:441
  34.5 0.0 copy-start.11
  34.5 0.0 collective-permute-done.4.other_ref.came_ref
  34.5 0.2 shard_map.97.own_ref
  34.7 1.6 %collective-permute-start.5 = (bf16[2,128,256]{2,1,0:T(8,128)(2,1)S(1)}, bf16[2,128,256]{2,1,0:T(8,128)(2,1)S(1)}, u32[]{:S(2)}, u32[]{:S(2)}) collective-permute-start(bf16[2,128,256]{2,1,0:T(8,128)(2,1)S(1)} %shard_map.97.own_ref), channel_id=1, source_target_pairs={{0,8},{2,10},{4,12},{6,14},{8,0},{10,2},{12,4},{14,6},{16,24},{18,... | collective-permute-start | bytes 393224 | tf_op jit(solution)/shard_map/ppermute | solution.py:457
  36.4 0.3 shard_map.98.path_ref
  36.6 3.4 %collective-permute-done.5.other_ref.came_ref = bf16[2,128,256]{2,1,0:T(8,128)(2,1)S(1)} collective-permute-done((bf16[2,128,256]{2,1,0:T(8,128)(2,1)S(1)}, bf16[2,128,256]{2,1,0:T(8,128)(2,1)S(1)}, u32[]{:S(2)}, u32[]{:S(2)}) %collective-permute-start.5) | collective-permute-done | bytes 131104 | tf_op jit(solution)/shard_map/ppermute | solution.py:457
  40.0 0.2 shard_map.99
  40.2 4.5 %collective-permute-start.6 = (bf16[2,128,128]{2,1,0:T(8,128)(2,1)S(1)}, bf16[2,128,128]{2,1,0:T(8,128)(2,1)S(1)}, u32[]{:S(2)}, u32[]{:S(2)}) collective-permute-start(bf16[2,128,128]{2,1,0:T(8,128)(2,1)S(1)} %shard_map.99), channel_id=1, source_target_pairs={{0,16},{2,18},{4,20},{6,22},{8,24},{10,26},{12,28},{14,30},{1,17},... | collective-permute-start | bytes 196616 | tf_op jit(solution)/shard_map/ppermute | solution.py:457
  44.7 0.1 pad_add_fusion.flags_ref
  44.8 0.3 shard_map.100.path_ref
  45.1 1.5 %collective-permute-done.6.state_ref = bf16[2,128,128]{2,1,0:T(8,128)(2,1)S(1)} collective-permute-done((bf16[2,128,128]{2,1,0:T(8,128)(2,1)S(1)}, bf16[2,128,128]{2,1,0:T(8,128)(2,1)S(1)}, u32[]{:S(2)}, u32[]{:S(2)}) %collective-permute-start.6) | collective-permute-done | bytes 65568 | tf_op jit(solution)/shard_map/ppermute | solution.py:457
  46.6 0.7 %shard_map.101 = (bf16[2,128,128]{2,1,0:T(8,128)(2,1)S(1)}, bf16[2,128,128]{2,1,0:T(8,128)(2,1)S(1)}) custom-call(s32[2]{0:T(128)S(1)} %pad_add_fusion.flags_ref, bf16[2,128,128]{2,1,0:T(8,128)(2,1)S(1)} %collective-permute-done.6.state_ref, f32[2,256,256]{2,1,0:T(8,128)S(1)} %shard_map.100.path_ref), custom_call_target="tpu_custom_call" | custom-call | flops 10000000 | bytes 100000 | tf_op jit(solution)/shard_map/pallas_call | solution.py:441
  47.3 0.1 collective-permute-start.7
  47.4 1.2 %collective-permute-done.7.came_ref = bf16[2,128,128]{2,1,0:T(8,128)(2,1)S(1)} collective-permute-done((bf16[2,128,128]{2,1,0:T(8,128)(2,1)S(1)}, bf16[2,128,128]{2,1,0:T(8,128)(2,1)S(1)}, u32[]{:S(2)}, u32[]{:S(2)}) %collective-permute-start.7) | collective-permute-done | bytes 65568 | tf_op jit(solution)/shard_map/ppermute | solution.py:457
  48.7 0.4 shard_map.102
  49.1 1.0 %collective-permute-start.8 = (bf16[256,512]{1,0:T(8,128)(2,1)S(1)}, bf16[256,512]{1,0:T(8,128)(2,1)S(1)}, u32[]{:S(2)}, u32[]{:S(2)}) collective-permute-start(bf16[256,512]{1,0:T(8,128)(2,1)S(1)} %shard_map.102), channel_id=1, source_target_pairs={{0,1},{1,0},{2,3},{3,2},{4,5},{5,4},{6,7},{7,6},{8,9},{9,8},{10,11... | collective-permute-start | bytes 786440 | tf_op jit(solution)/shard_map/ppermute | solution.py:457
  50.0 1.9 %shard_map.104.mine_ref = bf16[256,1024]{1,0:T(8,128)(2,1)S(1)} custom-call(s32[1]{0:T(128)} %bitcast.flags_ref, bf16[2,128,128]{2,1,0:T(8,128)(2,1)S(1)} %get-tuple-element.62.keep_ref, bf16[2,128,128]{2,1,0:T(8,128)(2,1)S(1)} %collective-permute-done.7.came_ref, f32[2,4,256,256]{3,2,1,0:T(8,128)S(1)} %shard_map.96.both_ref, f32[1,512]{1,0:T(1,128)S(1)} %bitcast.10, ...), custom_call_target="tpu_custom_call" | custom-call | flops 10000000 | bytes 100000 | tf_op jit(solution)/shard_map/pallas_call | solution.py:441
  51.9 0.0 collective-permute-done.9.w_ref
  51.9 1.3 %shard_map.103.w_ref = bf16[512,1024]{1,0:T(8,128)(2,1)S(1)} custom-call(bf16[512,1024]{1,0:T(8,128)(2,1)} %collective-permute-done.9.w_ref), custom_call_target="tpu_custom_call" | custom-call | flops 10000000 | bytes 100000 | tf_op jit(solution)/shard_map/pallas_call | solution.py:441
  53.2 4.2 %collective-permute-done.8.theirs_ref = bf16[256,512]{1,0:T(8,128)(2,1)S(1)} collective-permute-done((bf16[256,512]{1,0:T(8,128)(2,1)S(1)}, bf16[256,512]{1,0:T(8,128)(2,1)S(1)}, u32[]{:S(2)}, u32[]{:S(2)}) %collective-permute-start.8) | collective-permute-done | bytes 262176 | tf_op jit(solution)/shard_map/ppermute | solution.py:457
  57.5 1.2 %shard_map.105 = bf16[256,1024]{1,0:T(8,128)(2,1)} custom-call(bf16[256,512]{1,0:T(8,128)(2,1)S(1)} %collective-permute-done.8.theirs_ref, bf16[512,1024]{1,0:T(8,128)(2,1)S(1)} %shard_map.103.w_ref, bf16[256,1024]{1,0:T(8,128)(2,1)S(1)} %shard_map.104.mine_ref), custom_call_target="tpu_custom_call" | custom-call | flops 10000000 | bytes 100000 | tf_op jit(solution)/shard_map/pallas_call | solution.py:441
  (15 shorter events, 0.1 us)
Async XLA Ops:
  0.0 7.9 %copy-start = (bf16[1024,512]{1,0:T(8,128)(2,1)S(1)}, bf16[1024,512]{1,0:T(8,128)(2,1)}, u32[]{:S(2)}) copy-start(bf16[1024,512]{1,0:T(8,128)(2,1)} %wq_ref.3) | copy-start | bytes 3145732
  0.0 7.9 %copy-start.1 = (bf16[1024,512]{1,0:T(8,128)(2,1)S(1)}, bf16[1024,512]{1,0:T(8,128)(2,1)}, u32[]{:S(2)}) copy-start(bf16[1024,512]{1,0:T(8,128)(2,1)} %wk_ref.3) | copy-start | bytes 3145732
  0.0 7.9 %copy-start.2 = (bf16[1024,512]{1,0:T(8,128)(2,1)S(1)}, bf16[1024,512]{1,0:T(8,128)(2,1)}, u32[]{:S(2)}) copy-start(bf16[1024,512]{1,0:T(8,128)(2,1)} %wv_ref.3) | copy-start | bytes 3145732
  0.0 15.3 %collective-permute-start = (bf16[256,1024]{1,0:T(8,128)(2,1)}, bf16[256,1024]{1,0:T(8,128)(2,1)}, u32[]{:S(2)}, u32[]{:S(2)}) collective-permute-start(bf16[256,1024]{1,0:T(8,128)(2,1)} %x_ref.3), channel_id=1, source_target_pairs={{0,1},{1,0},{2,3},{3,2},{4,5},{5,4},{6,7},{7,6},{8,9},{9,8},{10,11... | collective-permute-start | bytes 1572872 | tf_op jit(solution)/shard_map/ppermute | solution.py:457
  3.0 1.1 %copy-start.7 = (bf16[256,1024]{1,0:T(8,128)(2,1)S(1)}, bf16[256,1024]{1,0:T(8,128)(2,1)}, u32[]{:S(2)}) copy-start(bf16[256,1024]{1,0:T(8,128)(2,1)} %x_ref.3) | copy-start | bytes 1572868
  4.1 3.8 %copy-start.9 = (f32[3,4,512]{2,1,0:T(4,128)S(1)}, f32[3,4,512]{2,1,0:T(4,128)}, u32[]{:S(2)}) copy-start(f32[3,4,512]{2,1,0:T(4,128)} %conv_ref.3) | copy-start | bytes 73732
  4.1 3.8 %copy-start.10 = (bf16[1024,4]{0,1:T(4,128)(2,1)S(1)}, bf16[1024,4]{0,1:T(4,128)(2,1)}, u32[]{:S(2)}) copy-start(bf16[1024,4]{0,1:T(4,128)(2,1)} %param.13) | copy-start | bytes 24580
  4.1 3.8 %copy-start.12 = (f32[4]{0:T(128)S(1)}, f32[4]{0:T(128)}, u32[]{:S(2)}) copy-start(f32[4]{0:T(128)} %bias_ref.3) | copy-start | bytes 52
  4.1 11.0 %collective-permute-start.1 = (bf16[16,1024]{1,0:T(8,128)(2,1)S(1)}, bf16[16,1024]{1,0:T(8,128)(2,1)S(1)}, u32[]{:S(2)}, u32[]{:S(2)}) collective-permute-start(bf16[16,1024]{1,0:T(8,128)(2,1)S(1)} %get-tuple-element.38.tail_ref), channel_id=1, source_target_pairs={{0,1},{1,2},{2,3},{3,4},{4,5},{5,6},{6,7},{7,8},{8,9},{9,10},{10,1... | collective-permute-start | bytes 98312 | tf_op jit(solution)/shard_map/ppermute | solution.py:457
  6.3 8.8 %collective-permute-start.2 = (bf16[16,1024]{1,0:T(8,128)(2,1)S(1)}, bf16[16,1024]{1,0:T(8,128)(2,1)S(1)}, u32[]{:S(2)}, u32[]{:S(2)}) collective-permute-start(bf16[16,1024]{1,0:T(8,128)(2,1)S(1)} %get-tuple-element.38.tail_ref), channel_id=1, source_target_pairs={{0,2},{2,4},{4,6},{6,8},{8,10},{10,12},{12,14},{14,16},{16,18},{18... | collective-permute-start | bytes 98312 | tf_op jit(solution)/shard_map/ppermute | solution.py:457
  7.9 1.0 %copy-start.8 = (bf16[256,1024]{1,0:T(8,128)(2,1)S(1)}, bf16[256,1024]{1,0:T(8,128)(2,1)}, u32[]{:S(2)}) copy-start(bf16[256,1024]{1,0:T(8,128)(2,1)} %x_ref.3) | copy-start | bytes 1572868
  15.0 7.2 %copy-start.5 = (f32[4,256,256]{2,1,0:T(8,128)}, f32[4,256,256]{2,1,0:T(8,128)S(1)}, u32[]{:S(2)}) copy-start(f32[4,256,256]{2,1,0:T(8,128)S(1)} %get-tuple-element.49.early_ref) | copy-start | bytes 3145732
  22.1 1.2 %copy-start.3 = (bf16[4,768,256]{2,1,0:T(8,128)(2,1)}, bf16[4,768,256]{2,1,0:T(8,128)(2,1)S(1)}, u32[]{:S(2)}) copy-start(bf16[4,768,256]{2,1,0:T(8,128)(2,1)S(1)} %get-tuple-element.47.held_ref) | copy-start | bytes 4718596
  23.3 28.6 %collective-permute-start.9 = (bf16[512,1024]{1,0:T(8,128)(2,1)}, bf16[512,1024]{1,0:T(8,128)(2,1)}, u32[]{:S(2)}, u32[]{:S(2)}) collective-permute-start(bf16[512,1024]{1,0:T(8,128)(2,1)} %w_ref.1), channel_id=1, source_target_pairs={{0,1},{1,0},{2,3},{3,2},{4,5},{5,4},{6,7},{7,6},{8,9},{9,8},{10,11... | collective-permute-start | bytes 3145736 | tf_op jit(solution)/shard_map/ppermute | solution.py:457
  26.7 1.3 %collective-permute-start.3 = (bf16[2,128,256]{2,1,0:T(8,128)(2,1)S(1)}, bf16[2,128,256]{2,1,0:T(8,128)(2,1)S(1)}, u32[]{:S(2)}, u32[]{:S(2)}) collective-permute-start(bf16[2,128,256]{2,1,0:T(8,128)(2,1)S(1)} %get-tuple-element.42), channel_id=1, source_target_pairs={{0,2},{2,0},{4,6},{6,4},{8,10},{10,8},{12,14},{14,12},{16,18},{18,... | collective-permute-start | bytes 393224 | tf_op jit(solution)/shard_map/ppermute | solution.py:457
  28.2 6.3 %collective-permute-start.4 = (bf16[2,128,256]{2,1,0:T(8,128)(2,1)S(1)}, bf16[2,128,256]{2,1,0:T(8,128)(2,1)S(1)}, u32[]{:S(2)}, u32[]{:S(2)}) collective-permute-start(bf16[2,128,256]{2,1,0:T(8,128)(2,1)S(1)} %shard_map.94.own_ref), channel_id=1, source_target_pairs={{0,4},{2,6},{4,0},{6,2},{8,12},{10,14},{12,8},{14,10},{16,20},{18,... | collective-permute-start | bytes 393224 | tf_op jit(solution)/shard_map/ppermute | solution.py:457
  29.9 1.4 %copy-start.4 = (bf16[4,768,256]{2,1,0:T(8,128)(2,1)S(1)}, bf16[4,768,256]{2,1,0:T(8,128)(2,1)}, u32[]{:S(2)}) copy-start(bf16[4,768,256]{2,1,0:T(8,128)(2,1)} %copy-done.3) | copy-start | bytes 4718596
  31.3 1.2 %copy-start.6 = (f32[4,256,256]{2,1,0:T(8,128)S(1)}, f32[4,256,256]{2,1,0:T(8,128)}, u32[]{:S(2)}) copy-start(f32[4,256,256]{2,1,0:T(8,128)} %copy-done.5) | copy-start | bytes 3145732
  34.5 14.2 %copy-start.11 = (f32[512]{0:T(512)S(1)}, f32[512]{0:T(512)}, u32[]{:S(2)}) copy-start(f32[512]{0:T(512)} %param.16) | copy-start | bytes 6148
  34.7 5.3 %collective-permute-start.5 = (bf16[2,128,256]{2,1,0:T(8,128)(2,1)S(1)}, bf16[2,128,256]{2,1,0:T(8,128)(2,1)S(1)}, u32[]{:S(2)}, u32[]{:S(2)}) collective-permute-start(bf16[2,128,256]{2,1,0:T(8,128)(2,1)S(1)} %shard_map.97.own_ref), channel_id=1, source_target_pairs={{0,8},{2,10},{4,12},{6,14},{8,0},{10,2},{12,4},{14,6},{16,24},{18,... | collective-permute-start | bytes 393224 | tf_op jit(solution)/shard_map/ppermute | solution.py:457
  40.2 6.4 %collective-permute-start.6 = (bf16[2,128,128]{2,1,0:T(8,128)(2,1)S(1)}, bf16[2,128,128]{2,1,0:T(8,128)(2,1)S(1)}, u32[]{:S(2)}, u32[]{:S(2)}) collective-permute-start(bf16[2,128,128]{2,1,0:T(8,128)(2,1)S(1)} %shard_map.99), channel_id=1, source_target_pairs={{0,16},{2,18},{4,20},{6,22},{8,24},{10,26},{12,28},{14,30},{1,17},... | collective-permute-start | bytes 196616 | tf_op jit(solution)/shard_map/ppermute | solution.py:457
  47.3 1.3 %collective-permute-start.7 = (bf16[2,128,128]{2,1,0:T(8,128)(2,1)S(1)}, bf16[2,128,128]{2,1,0:T(8,128)(2,1)S(1)}, u32[]{:S(2)}, u32[]{:S(2)}) collective-permute-start(bf16[2,128,128]{2,1,0:T(8,128)(2,1)S(1)} %get-tuple-element.63), channel_id=1, source_target_pairs={{0,2},{2,0},{4,6},{6,4},{8,10},{10,8},{12,14},{14,12},{16,18},{18,... | collective-permute-start | bytes 196616 | tf_op jit(solution)/shard_map/ppermute | solution.py:457
  49.1 8.4 %collective-permute-start.8 = (bf16[256,512]{1,0:T(8,128)(2,1)S(1)}, bf16[256,512]{1,0:T(8,128)(2,1)S(1)}, u32[]{:S(2)}, u32[]{:S(2)}) collective-permute-start(bf16[256,512]{1,0:T(8,128)(2,1)S(1)} %shard_map.102), channel_id=1, source_target_pairs={{0,1},{1,0},{2,3},{3,2},{4,5},{5,4},{6,7},{7,6},{8,9},{9,8},{10,11... | collective-permute-start | bytes 786440 | tf_op jit(solution)/shard_map/ppermute | solution.py:457

commit v4 on v3

--- a/solution.py
+++ b/solution.py
@@ -174,11 +174,18 @@
     return inverses
 
 
-def transitions(keys, values, rates, invert=invert):
+def within(shape, group):
+    row = lax.broadcasted_iota(jnp.int32, shape, 0)
+    lane = lax.broadcasted_iota(jnp.int32, shape, 1)
+    if group is None or group >= shape[0]:
+        return row, lane, True
+    return row, lane, row // group == lane // group
+
+
+def solve(keys, values, rates, invert=invert, group=None):
     rows, dim = keys[0].shape
-    row = lax.broadcasted_iota(jnp.int32, (rows, rows), 0)
-    lane = lax.broadcasted_iota(jnp.int32, (rows, rows), 1)
-    norms, norm_rows, rate_rows, lowers = [], [], [], []
+    row, lane, same = within((rows, rows), group)
+    norms, norm_rows, lowers = [], [], []
     for key, rate_row in zip(keys, rates):
         rate = jnp.sum(jnp.where(row == lane, rate_row, 0.0), 1, keepdims=True)
         wide_key = key.astype(F32)
@@ -186,29 +193,34 @@
         norm_row = jnp.sum(jnp.where(row == lane, norm, 0.0), 0, keepdims=True)
         norms.append(norm)
         norm_rows.append(norm_row)
-        rate_rows.append(rate_row)
         gram = dot(key, key, NT)
-        lowers.append(jnp.where(row > lane, gram * (rate * norm) * norm_row, 0.0))
-    inverses = [each * rate for each, rate in zip(invert(lowers), rate_rows)]
-    eye = jnp.eye(dim, dtype=F32)
+        lowers.append(jnp.where((row > lane) & same, gram * (rate * norm) * norm_row, 0.0))
     solved = []
-    for key, value, inverse, norm_row in zip(keys, values, inverses, norm_rows):
-        fresh = dot_half(inverse, value)
-        weight = dot_half(inverse * norm_row, key)
-        solved.append(jnp.concatenate([weight, fresh], 1))
-    pairs = []
-    for key, each, norm in zip(keys, solved, norms):
-        top, rest = split(each * norm)
-        moved = dot(key, top, TN) + dot(key, rest, TN)
-        pairs.append(jnp.concatenate([eye - moved[:, :dim], moved[:, dim:]], 1))
-    return pairs, solved, norm_rows
-
-
-def look(query, key, norm_row, solved):
+    for key, value, inverse, rate_row, norm in zip(keys, values, invert(lowers), rates, norms):
+        top, rest = split(inverse * rate_row)
+        unit, unit_rest = split(key.astype(F32) * norm)
+        both = jnp.concatenate([unit, value], 1)
+        each = dot(top, both) + dot(rest, both)
+        solved.append(jnp.concatenate([each[:, :dim] + dot(top, unit_rest), each[:, dim:]], 1))
+    return solved, norms, norm_rows
+
+
+def pair_of(key, solved, norm):
+    dim = key.shape[1]
+    top, rest = split(solved * norm)
+    moved = dot(key, top, TN) + dot(key, rest, TN)
+    return jnp.concatenate([jnp.eye(dim, dtype=F32) - moved[:, :dim], moved[:, dim:]], 1)
+
+
+def transitions(keys, values, rates):
+    solved, norms, norm_rows = solve(keys, values, rates)
+    return [pair_of(*each) for each in zip(keys, solved, norms)], solved, norm_rows
+
+
+def look(query, key, norm_row, solved, group=None):
     rows, dim = query.shape
-    row = lax.broadcasted_iota(jnp.int32, (rows, rows), 0)
-    lane = lax.broadcasted_iota(jnp.int32, (rows, rows), 1)
-    attend = jnp.where(row >= lane, dot(query, key, NT) * norm_row, 0.0)
+    row, lane, same = within((rows, rows), group)
+    attend = jnp.where((row >= lane) & same, dot(query, key, NT) * norm_row, 0.0)
     seen = dot_half(attend, solved)
     return jnp.concatenate([query.astype(F32) - seen[:, :dim], seen[:, dim:]], 1)
 
@@ -249,11 +261,12 @@
         pair_ref[head] = pairs[head]
         look_ref[head] = look(
             queries[head], keys[head], norm_rows[head], solved[head].astype(BF16)
-        )
+        ).astype(BF16)
 
 
 def late_kernel(
-    flags_ref,
+    swapped_ref,
+    bit_ref,
     bias_ref,
     x_ref,
     wq_ref,
@@ -270,13 +283,12 @@
     send_ref,
     norm_ref,
     held_ref,
-    mini_ref,
     proj_ref,
 ):
     heads = early_ref.shape[0]
     kept = keep_ref.shape[0]
     rows = x_ref.shape[0]
-    swapped = flags_ref[0] == 1
+    swapped = swapped_ref[0] == 1
     halo = jnp.where(swapped, behind_ref[...], tail_ref[...])
     x = jnp.concatenate([halo, x_ref[...], halo_ref[...], head_ref[...]], 0)
     active, few = activate(
@@ -290,22 +302,31 @@
     queries, keys, values = ([each[:, span] for span in spans] for each in active)
     rates = write_rates(x_ref[...], wb_ref[...], bias_ref)
     lane = lax.broadcasted_iota(jnp.int32, (1, HALO), 1)
-    few_rates = [
-        jnp.where(lane < conv_ref.shape[1] - 1, each, 0.0)
-        for each in write_rates(head_ref[...], wb_ref[...], bias_ref)
-    ]
-    few_queries, few_keys, few_values = ([each[:, span] for span in spans] for each in few)
-    few_pairs, few_solved, few_norm_rows = transitions(
-        few_keys, few_values, few_rates, functools.partial(invert_few, conv_ref.shape[1] - 1)
-    )
-    early = []
+    few_rates = jnp.concatenate(
+        [
+            jnp.where(lane < conv_ref.shape[1] - 1, each, 0.0)
+            for each in write_rates(head_ref[...], wb_ref[...], bias_ref)
+        ],
+        1,
+    )
+    stacked = [jnp.concatenate([each[:, span] for span in spans], 0) for each in few]
+    few_solved, few_norms, few_norm_row = solve(
+        stacked[1:2],
+        stacked[2:],
+        [few_rates],
+        functools.partial(invert_few, conv_ref.shape[1] - 1),
+        HALO,
+    )
+    few_solved, few_norms = few_solved[0], few_norms[0]
+    mini = look(stacked[0], stacked[1], few_norm_row[0], few_solved.astype(BF16), HALO)
+    few_pairs, early = [], []
     for head in range(heads):
-        mini_ref[head] = look(
-            few_queries[head], few_keys[head], few_norm_rows[head], few_solved[head].astype(BF16)
-        )
-        early.append(compose(few_pairs[head], early_ref[head]))
+        at = slice(head * HALO, (head + 1) * HALO)
+        few_pair = pair_of(stacked[1][at], few_solved[at], few_norms[at])
+        few_pairs.append(few_pair.astype(BF16))
+        early.append(compose(few_pair, early_ref[head]))
     pairs, solved, norm_rows = transitions(keys, values, rates)
-    bit = flags_ref[1]
+    bit = bit_ref[0]
     wholes = []
     for head, late in enumerate(pairs):
         norm_ref[head : head + 1] = norm_rows[head]
@@ -315,7 +336,8 @@
                 solved[head].astype(BF16),
                 jnp.concatenate([queries[head], keys[head]], 1),
                 low.astype(BF16),
-                few_pairs[head].astype(BF16),
+                few_pairs[head],
+                mini[head * HALO : (head + 1) * HALO].astype(BF16),
             ],
             0,
         )
@@ -336,12 +358,10 @@
     return jnp.concatenate([through[:, :dim], through[:, dim:] + reads[:, dim:]], 1)
 
 
-def look_kernel(taps, flags_ref, norm_ref, held_ref, mini_ref, early_ref, both_ref):
-    swapped = flags_ref[0] == 1
+def look_late_kernel(swapped_ref, norm_ref, held_ref, late_ref):
     heads = held_ref.shape[0]
+    rows = norm_ref.shape[1]
     dim = held_ref.shape[2] // 2
-    rows = (held_ref.shape[1] - 2 * dim) // 2
-    row = lax.broadcasted_iota(jnp.int32, (HALO, 2 * dim), 0)
     for head in range(heads):
         late = look(
             held_ref[head, rows : 2 * rows, :dim],
@@ -349,13 +369,22 @@
             norm_ref[head : head + 1],
             held_ref[head, :rows],
         )
-        first = held_ref[head, 2 * rows : 2 * rows + dim]
-        early = after(early_ref[head], held_ref[head, 2 * rows + dim :])
-        top = jnp.where(row < taps - 1, mini_ref[head], early[:HALO])
+        later = after(late, held_ref[head, 2 * rows : 2 * rows + dim])
+        late_ref[head] = jnp.where(swapped_ref[0] == 1, late, later).astype(BF16)
+
+
+def look_early_kernel(taps, swapped_ref, held_ref, early_ref, out_ref):
+    heads, rows, wide = early_ref.shape
+    dim = wide // 2
+    row = lax.broadcasted_iota(jnp.int32, (HALO, wide), 0)
+    start = 2 * rows
+    for head in range(heads):
+        early = after(early_ref[head].astype(F32), held_ref[head, start + dim : start + 2 * dim])
+        few = held_ref[head, start + 2 * dim :].astype(F32)
+        top = jnp.where(row < taps - 1, few, early[:HALO])
         early = jnp.concatenate([top, early[HALO:]], 0)
-        later = after(jnp.where(swapped, early, late), first)
-        both_ref[0, head] = jnp.where(swapped, later, early)
-        both_ref[1, head] = jnp.where(swapped, late, later)
+        later = after(early, held_ref[head, start : start + dim])
+        out_ref[head] = jnp.where(swapped_ref[0] == 1, later, early).astype(BF16)
 
 
 def compose(low, high):
@@ -383,46 +412,46 @@
     row = lax.broadcasted_iota(jnp.int32, (dim, 2 * dim), 0)
     lane = lax.broadcasted_iota(jnp.int32, (dim, 2 * dim), 1)
     for head in range(own_ref.shape[0]):
-        path_ref[head, :dim] = (row == lane).astype(F32)
+        path_ref[head, :dim] = (row == lane).astype(BF16)
         low = jnp.where(flags_ref[0] == 1, other_ref[head], own_ref[head])
-        path_ref[head, dim:] = low.astype(F32)
+        path_ref[head, dim:] = low
 
 
 def path_kernel(flags_ref, path_ref, came_ref, out_ref):
     dim = came_ref.shape[1]
     for head in range(came_ref.shape[0]):
         path = path_ref[head]
-        through = dot_half(path[:, :dim], came_ref[head])
-        longer = jnp.concatenate([through[:, :dim], through[:, dim:] + path[:, dim:]], 1)
-        out_ref[head] = jnp.where(flags_ref[0] == 1, longer, path)
-
-
-def enter_kernel(flags_ref, state_ref, path_ref, keep_ref, send_ref):
+        through = dot(path[:, :dim], came_ref[head])
+        longer = jnp.concatenate([through[:, :dim], through[:, dim:] + path[:, dim:].astype(F32)], 1)
+        out_ref[head] = jnp.where(flags_ref[0] == 1, longer.astype(BF16), path)
+
+
+def enter_kernel(bit_ref, reached_ref, state_ref, path_ref, keep_ref, send_ref):
     dim = state_ref.shape[1]
     for head in range(keep_ref.shape[0]):
-        state = jnp.where(flags_ref[1] == 1, state_ref[head], jnp.zeros_like(state_ref[head]))
+        state = jnp.where(reached_ref[0] == 1, state_ref[head], jnp.zeros_like(state_ref[head]))
         path = path_ref[head]
-        both = (dot(path[:, :dim].astype(BF16), state) + path[:, dim:]).astype(BF16)
-        later = flags_ref[0] == 1
+        both = (dot(path[:, :dim], state) + path[:, dim:].astype(F32)).astype(BF16)
+        later = bit_ref[0] == 1
         keep_ref[head] = jnp.where(later, both[dim:], both[:dim])
         send_ref[head] = jnp.where(later, both[:dim], both[dim:])
 
 
-def finish_kernel(place, flags_ref, keep_ref, came_ref, both_ref, gain_ref, out_ref):
+def finish_kernel(flags_ref, keep_ref, came_ref, reads_ref, gain_ref, out_ref):
     count, dim = keep_ref.shape[:2]
-    heads = both_ref.shape[1]
+    heads = reads_ref.shape[0]
     for head, span in enumerate(spans_of(heads, heads * dim)):
         state = keep_ref[head % count]
         if count < heads:
             state = jnp.where(flags_ref[0] == head // count, state, came_ref[head % count])
-        reach = both_ref[place, head, :, :dim].astype(BF16)
-        rows = both_ref[place, head, :, dim:] + dot(reach, state)
+        reach = reads_ref[head, :, :dim]
+        rows = reads_ref[head, :, dim:].astype(F32) + dot(reach, state)
         scale = lax.rsqrt(jnp.mean(rows * rows, 1, keepdims=True) + 1e-5)
         out_ref[:, span] = (rows * scale * gain_ref[:, span]).astype(BF16)
 
 
-def finish_mine_kernel(flags_ref, keep_ref, came_ref, both_ref, gain_ref, w_ref, out_ref, normed_ref):
-    finish_kernel(0, flags_ref, keep_ref, came_ref, both_ref, gain_ref, normed_ref)
+def finish_mine_kernel(flags_ref, keep_ref, came_ref, reads_ref, gain_ref, w_ref, out_ref, normed_ref):
+    finish_kernel(flags_ref, keep_ref, came_ref, reads_ref, gain_ref, normed_ref)
     out_ref[...] = dot(normed_ref[...], w_ref[...]).astype(BF16)
 
 
@@ -494,27 +523,26 @@
     kept_shape = (kept,) + pair_shape[1:]
     levels = shards.bit_length() - 1
     bits = [((me_seq >> level) & 1).astype(jnp.int32).reshape(1) for level in range(levels)]
-    flags = jnp.concatenate([swapped.astype(jnp.int32).reshape(1), bits[0]])
+    swapped = swapped.astype(jnp.int32).reshape(1)
     weights = [w_query, w_key, w_value, w_beta.T, conv_weight]
     pair0, look0 = call(
         early_kernel,
-        [(pair_shape, F32), ((heads, rows, 2 * dim), F32)],
+        [(pair_shape, F32), ((heads, rows, 2 * dim), BF16)],
         [early] + weights,
         scalars=[beta_bias],
         scratch=[pltpu.VMEM((3, rows + HALO, columns), F32)],
         grant=24,
     )
-    keep, send, *held = call(
+    keep, send, norm, held = call(
         late_kernel,
         [
             (kept_shape, BF16),
             (kept_shape, BF16),
             ((heads, rows), F32),
-            ((heads, 2 * rows + 2 * dim, 2 * dim), BF16),
-            ((heads, HALO, 2 * dim), F32),
+            ((heads, 2 * rows + 2 * dim + HALO, 2 * dim), BF16),
         ],
         [late] + weights + [head, tail, halo, behind, pair0],
-        scalars=[flags, beta_bias],
+        scalars=[swapped, bits[0], beta_bias],
         scratch=[pltpu.VMEM((3, rows + 3 * HALO, columns), F32)],
         grant=24,
     )
@@ -528,14 +556,22 @@
             partner = [(i, j) for i, j in partner if j > i]
         came = shift(send, "seq", partner)
         if level == 1:
-            both = call(
-                functools.partial(look_kernel, conv_weight.shape[1]),
-                [((2, heads, rows, 2 * dim), F32)],
-                held + [look0],
-                scalars=[flags],
+            late = call(
+                look_late_kernel,
+                [((heads, rows, 2 * dim), BF16)],
+                [norm, held],
+                scalars=[swapped],
             )[0]
-            came, path, both = together(came, path, both)
-        elif level > 1:
+            came, path, late = together(came, path, late)
+        elif level == 2:
+            early = call(
+                functools.partial(look_early_kernel, conv_weight.shape[1]),
+                [((heads, rows, 2 * dim), BF16)],
+                [held, look0],
+                scalars=[swapped],
+            )[0]
+            came, path, early = together(came, path, early)
+        elif level > 2:
             came, path = together(came, path)
         if level == levels - 1:
             break
@@ -548,25 +584,25 @@
         if level == 0:
             own, came, send = together(own, came, send)
             path = call(
-                open_kernel, [((kept, 2 * dim, 2 * dim), F32)], [own, came], scalars=[bits[0]]
+                open_kernel, [((kept, 2 * dim, 2 * dim), BF16)], [own, came], scalars=[bits[0]]
             )[0]
         else:
             path, came, send = together(path, came, send)
             path = call(
-                path_kernel, [((kept, 2 * dim, 2 * dim), F32)], [path, came], scalars=[bits[level]]
+                path_kernel, [((kept, 2 * dim, 2 * dim), BF16)], [path, came], scalars=[bits[level]]
             )[0]
         own = send
     keep, send = call(
         enter_kernel,
         [((kept, dim, dim), BF16)] * 2,
         [came, path],
-        scalars=[jnp.concatenate([bits[0], bits[levels - 1]])],
+        scalars=[bits[0], bits[levels - 1]],
     )
     came = shift(send, "seq", [(i, i ^ 1) for i in range(shards)]) if kept < heads else send
     gone = call(
-        functools.partial(finish_kernel, 1),
+        finish_kernel,
         [((rows, columns), BF16)],
-        [keep, came, both, gain],
+        [keep, came, late, gain],
         scalars=[bits[0]],
     )[0]
     if groups == 2:
@@ -574,7 +610,7 @@
         mine = call(
             finish_mine_kernel,
             [((rows, width), BF16)],
-            [keep, came, both, gain, w_out],
+            [keep, came, early, gain, w_out],
             scalars=[bits[0]],
             scratch=[pltpu.VMEM((rows, columns), BF16)],
         )[0]
@@ -583,9 +619,9 @@
         theirs, whole = together(theirs, whole)
         return call(output_kernel, [((rows, width), BF16)], [theirs, whole, mine])[0]
     normed = call(
-        functools.partial(finish_kernel, 0),
+        finish_kernel,
         [((rows, columns), BF16)],
-        [keep, came, both, gain],
+        [keep, came, early, gain],
         scalars=[bits[0]],
     )[0]
     product = jnp.dot(

time: 59.2 us -> 56.6 us (0.956)
  local copies, waits for them, and re-layouts: 5.95 us -> 4.16 us
  Pallas kernels: 21.5 us -> 20.2 us
  waiting for transfers between devices: 12.1 us -> 13.2 us
    unnamed x26 -> x24, local copies, waits for them, and re-layouts: 5.95 us -> 4.16 us
    pallas_call x15 -> x16, Pallas kernels: 21.5 us -> 20.2 us  [call(): pl.pallas_call(kernel, out_shape=[jax.ShapeDtypeStruct(shape, dtype) for...]
    ppermute x10, waiting for transfers between devices: 12.1 us -> 13.2 us  [shift(): return lax.ppermute(block, axes, pairs)]
where the time goes in v4:
time: 56.6 us; the launch traced here: 56.3 us
  Pallas kernels  20.2 us (36%)
  starting transfers between devices  18.5 us (33%)
  waiting for transfers between devices  13.2 us (23%)
  local copies, waits for them, and re-layouts  4.16 us (7%)
    pallas_call x16, Pallas kernels, call(): pl.pallas_call(kernel, out_shape=[jax.ShapeDtypeStruct(shape, dtype) for...  20.2 us
    ppermute x10, starting transfers between devices, shift(): return lax.ppermute(block, axes, pairs)  18.5 us
    ppermute x10, waiting for transfers between devices, shift(): return lax.ppermute(block, axes, pairs)  13.2 us
    unnamed x24, local copies, waits for them, and re-layouts  4.16 us
  transfers between devices with their start and end apart: 10, of which 7 were waited for; matrix products, arithmetic and copies ran while one was open for 0% of the time, Pallas kernels for 23%

profile of v4, /device:TPU:0, one launch (start us, length us, event | category | flops | bytes accessed | tf_op | source)
XLA Modules:
  0.0 56.3 jit_solution(12100615815590781470)
XLA Ops:
  0.0 3.0 %collective-permute-start = (bf16[256,1024]{1,0:T(8,128)(2,1)}, bf16[256,1024]{1,0:T(8,128)(2,1)S(1)}, u32[]{:S(2)}, u32[]{:S(2)}) collective-permute-start(bf16[256,1024]{1,0:T(8,128)(2,1)} %x_ref.3), channel_id=1, source_target_pairs={{0,1},{1,0},{2,3},{3,2},{4,5},{5,4},{6,7},{7,6},{8,9},{9,8},{10,11... | collective-permute-start | bytes 1572872 | tf_op jit(solution)/shard_map/ppermute | solution.py:486
  3.0 1.1 %copy-done.4 = bf16[256,1024]{1,0:T(8,128)(2,1)S(1)} copy-done((bf16[256,1024]{1,0:T(8,128)(2,1)S(1)}, bf16[256,1024]{1,0:T(8,128)(2,1)}, u32[]{:S(2)}) %copy-start.4) | copy-done | bytes 524312
  4.1 1.6 %collective-permute-start.2 = (bf16[16,1024]{1,0:T(8,128)(2,1)S(1)}, bf16[16,1024]{1,0:T(8,128)(2,1)S(1)}, u32[]{:S(2)}, u32[]{:S(2)}) collective-permute-start(bf16[16,1024]{1,0:T(8,128)(2,1)S(1)} %get-tuple-element.38.tail_ref), channel_id=1, source_target_pairs={{0,2},{2,4},{4,6},{6,8},{8,10},{10,12},{12,14},{14,16},{16,18},{18... | collective-permute-start | bytes 98312 | tf_op jit(solution)/shard_map/ppermute | solution.py:486
  5.7 2.3 %collective-permute-start.1 = (bf16[16,1024]{1,0:T(8,128)(2,1)S(1)}, bf16[16,1024]{1,0:T(8,128)(2,1)S(1)}, u32[]{:S(2)}, u32[]{:S(2)}) collective-permute-start(bf16[16,1024]{1,0:T(8,128)(2,1)S(1)} %get-tuple-element.38.tail_ref), channel_id=1, source_target_pairs={{0,1},{1,2},{2,3},{3,4},{4,5},{5,6},{6,7},{7,8},{8,9},{9,10},{10,1... | collective-permute-start | bytes 98312 | tf_op jit(solution)/shard_map/ppermute | solution.py:486
  8.0 0.0 copy-done.1
  8.0 0.0 copy-done
  8.0 0.0 copy-done.5
  8.0 0.0 copy-done.8
  8.0 0.0 copy-done.9
  8.0 0.0 copy-done.11
  8.1 0.0 copy-start.3
  8.1 1.2 %copy-done.3 = bf16[1024,512]{1,0:T(8,128)(2,1)S(1)} copy-done((bf16[1024,512]{1,0:T(8,128)(2,1)S(1)}, bf16[1024,512]{1,0:T(8,128)(2,1)}, u32[]{:S(2)}) %copy-start.3) | copy-done | bytes 1048600
  9.3 5.9 %shard_map.92 = (f32[4,128,256]{2,1,0:T(8,128)S(1)}, bf16[4,256,256]{2,1,0:T(8,128)(2,1)S(1)}) custom-call(f32[4]{0:T(128)S(1)} %copy-done.11, bf16[256,1024]{1,0:T(8,128)(2,1)S(1)} %copy-done.5, bf16[1024,512]{1,0:T(8,128)(2,1)S(1)} %copy-done, bf16[1024,512]{1,0:T(8,128)(2,1)S(1)} %copy-done.1, bf16[1024,512]{1,0:T(8,128)(2,1)S(1)} %copy-done.3, ...), custom_call_target="tpu_custom_call" | custom-call | flops 10000000 | bytes 100000 | tf_op jit(solution)/shard_map/pallas_call | solution.py:470
  15.2 0.0 copy-start.6
  15.2 0.8 %copy-done.6 = bf16[4,256,256]{2,1,0:T(8,128)(2,1)} copy-done((bf16[4,256,256]{2,1,0:T(8,128)(2,1)}, bf16[4,256,256]{2,1,0:T(8,128)(2,1)S(1)}, u32[]{:S(2)}) %copy-start.6) | copy-done | bytes 524312
  16.0 0.0 collective-permute-done.2.behind_ref
  16.0 0.0 collective-permute-done.1.halo_ref
  16.0 0.0 collective-permute-done.x_ref
  16.0 6.1 %shard_map.93 = (bf16[2,128,256]{2,1,0:T(8,128)(2,1)S(1)}, bf16[2,128,256]{2,1,0:T(8,128)(2,1)S(1)}, f32[4,256]{1,0:T(4,128)S(1)}, bf16[4,784,256]{2,1,0:T(8,128)(2,1)S(1)}) custom-call(s32[1]{0:T(128)} %bitcast.2.swapped_ref, s32[1]{0:T(128)} %bitcast.bit_ref.flags_ref, f32[4]{0:T(128)S(1)} %copy-done.11, bf16[256,1024]{1,0:T(8,128)(2,1)S(1)} %collective-permute-done.x_ref, ...), custom_call_target="tpu_custom_call" | custom-call | flops 10000000 | bytes 100000 | tf_op jit(solution)/shard_map/pallas_call | solution.py:470
  22.1 3.4 %collective-permute-start.9 = (bf16[512,1024]{1,0:T(8,128)(2,1)}, bf16[512,1024]{1,0:T(8,128)(2,1)}, u32[]{:S(2)}, u32[]{:S(2)}) collective-permute-start(bf16[512,1024]{1,0:T(8,128)(2,1)} %w_ref.1), channel_id=1, source_target_pairs={{0,1},{1,0},{2,3},{3,2},{4,5},{5,4},{6,7},{7,6},{8,9},{9,8},{10,11... | collective-permute-start | bytes 3145736 | tf_op jit(solution)/shard_map/ppermute | solution.py:486
  25.5 0.0 collective-permute-start.3
  25.5 1.3 %collective-permute-done.3.other_ref = bf16[2,128,256]{2,1,0:T(8,128)(2,1)S(1)} collective-permute-done((bf16[2,128,256]{2,1,0:T(8,128)(2,1)S(1)}, bf16[2,128,256]{2,1,0:T(8,128)(2,1)S(1)}, u32[]{:S(2)}, u32[]{:S(2)}) %collective-permute-start.3) | collective-permute-done | bytes 131104 | tf_op jit(solution)/shard_map/ppermute | solution.py:486
  26.8 0.2 shard_map.94.own_ref
  27.0 1.6 %collective-permute-start.4 = (bf16[2,128,256]{2,1,0:T(8,128)(2,1)S(1)}, bf16[2,128,256]{2,1,0:T(8,128)(2,1)S(1)}, u32[]{:S(2)}, u32[]{:S(2)}) collective-permute-start(bf16[2,128,256]{2,1,0:T(8,128)(2,1)S(1)} %shard_map.94.own_ref), channel_id=1, source_target_pairs={{0,4},{2,6},{4,0},{6,2},{8,12},{10,14},{12,8},{14,10},{16,20},{18,... | collective-permute-start | bytes 393224 | tf_op jit(solution)/shard_map/ppermute | solution.py:486
  28.6 1.7 %shard_map.96.reads_ref = bf16[4,256,256]{2,1,0:T(8,128)(2,1)S(1)} custom-call(s32[1]{0:T(128)} %bitcast.2.swapped_ref, f32[4,256]{1,0:T(4,128)S(1)} %get-tuple-element.46.norm_ref, bf16[4,784,256]{2,1,0:T(8,128)(2,1)S(1)} %get-tuple-element.47.held_ref), custom_call_target="tpu_custom_call" | custom-call | flops 10000000 | bytes 100000 | tf_op jit(solution)/shard_map/pallas_call | solution.py:470
  30.3 2.3 %collective-permute-done.4.other_ref.came_ref = bf16[2,128,256]{2,1,0:T(8,128)(2,1)S(1)} collective-permute-done((bf16[2,128,256]{2,1,0:T(8,128)(2,1)S(1)}, bf16[2,128,256]{2,1,0:T(8,128)(2,1)S(1)}, u32[]{:S(2)}, u32[]{:S(2)}) %collective-permute-start.4) | collective-permute-done | bytes 131104 | tf_op jit(solution)/shard_map/ppermute | solution.py:486
  32.6 0.2 shard_map.97.own_ref
  32.8 1.6 %collective-permute-start.5 = (bf16[2,128,256]{2,1,0:T(8,128)(2,1)S(1)}, bf16[2,128,256]{2,1,0:T(8,128)(2,1)S(1)}, u32[]{:S(2)}, u32[]{:S(2)}) collective-permute-start(bf16[2,128,256]{2,1,0:T(8,128)(2,1)S(1)} %shard_map.97.own_ref), channel_id=1, source_target_pairs={{0,8},{2,10},{4,12},{6,14},{8,0},{10,2},{12,4},{14,6},{16,24},{18,... | collective-permute-start | bytes 393224 | tf_op jit(solution)/shard_map/ppermute | solution.py:486
  34.4 1.0 %copy-done.7 = bf16[4,256,256]{2,1,0:T(8,128)(2,1)S(1)} copy-done((bf16[4,256,256]{2,1,0:T(8,128)(2,1)S(1)}, bf16[4,256,256]{2,1,0:T(8,128)(2,1)}, u32[]{:S(2)}) %copy-start.7) | copy-done | bytes 524312
  35.5 0.5 shard_map.99.reads_ref
  36.0 0.0 copy-start.10
  36.0 0.2 shard_map.98.path_ref
  36.2 1.6 %collective-permute-done.5.other_ref.came_ref = bf16[2,128,256]{2,1,0:T(8,128)(2,1)S(1)} collective-permute-done((bf16[2,128,256]{2,1,0:T(8,128)(2,1)S(1)}, bf16[2,128,256]{2,1,0:T(8,128)(2,1)S(1)}, u32[]{:S(2)}, u32[]{:S(2)}) %collective-permute-start.5) | collective-permute-done | bytes 131104 | tf_op jit(solution)/shard_map/ppermute | solution.py:486
  37.8 0.2 shard_map.100
  38.0 4.5 %collective-permute-start.6 = (bf16[2,128,128]{2,1,0:T(8,128)(2,1)S(1)}, bf16[2,128,128]{2,1,0:T(8,128)(2,1)S(1)}, u32[]{:S(2)}, u32[]{:S(2)}) collective-permute-start(bf16[2,128,128]{2,1,0:T(8,128)(2,1)S(1)} %shard_map.100), channel_id=1, source_target_pairs={{0,16},{2,18},{4,20},{6,22},{8,24},{10,26},{12,28},{14,30},{1,17},... | collective-permute-start | bytes 196616 | tf_op jit(solution)/shard_map/ppermute | solution.py:486
  42.5 0.2 shard_map.101.path_ref
  42.7 1.7 %collective-permute-done.6.state_ref = bf16[2,128,128]{2,1,0:T(8,128)(2,1)S(1)} collective-permute-done((bf16[2,128,128]{2,1,0:T(8,128)(2,1)S(1)}, bf16[2,128,128]{2,1,0:T(8,128)(2,1)S(1)}, u32[]{:S(2)}, u32[]{:S(2)}) %collective-permute-start.6) | collective-permute-done | bytes 65568 | tf_op jit(solution)/shard_map/ppermute | solution.py:486
  44.4 0.2 shard_map.102
  44.6 0.1 collective-permute-start.7
  44.7 1.2 %collective-permute-done.7.came_ref = bf16[2,128,128]{2,1,0:T(8,128)(2,1)S(1)} collective-permute-done((bf16[2,128,128]{2,1,0:T(8,128)(2,1)S(1)}, bf16[2,128,128]{2,1,0:T(8,128)(2,1)S(1)}, u32[]{:S(2)}, u32[]{:S(2)}) %collective-permute-start.7) | collective-permute-done | bytes 65568 | tf_op jit(solution)/shard_map/ppermute | solution.py:486
  45.9 0.0 copy-done.10
  45.9 0.4 shard_map.103
  46.3 0.4 collective-permute-start.8
  46.7 1.9 %shard_map.105.mine_ref = bf16[256,1024]{1,0:T(8,128)(2,1)S(1)} custom-call(s32[1]{0:T(128)} %bitcast.bit_ref.flags_ref, bf16[2,128,128]{2,1,0:T(8,128)(2,1)S(1)} %get-tuple-element.61.keep_ref, bf16[2,128,128]{2,1,0:T(8,128)(2,1)S(1)} %collective-permute-done.7.came_ref, bf16[4,256,256]{2,1,0:T(8,128)(2,1)S(1)} %shard_map.99.reads_ref, ...), custom_call_target="tpu_custom_call" | custom-call | flops 10000000 | bytes 100000 | tf_op jit(solution)/shard_map/pallas_call | solution.py:470
  48.6 1.1 %collective-permute-done.9.w_ref = bf16[512,1024]{1,0:T(8,128)(2,1)} collective-permute-done((bf16[512,1024]{1,0:T(8,128)(2,1)}, bf16[512,1024]{1,0:T(8,128)(2,1)}, u32[]{:S(2)}, u32[]{:S(2)}) %collective-permute-start.9) | collective-permute-done | bytes 1048608 | tf_op jit(solution)/shard_map/ppermute | solution.py:486
  49.8 1.3 %shard_map.104.w_ref = bf16[512,1024]{1,0:T(8,128)(2,1)S(1)} custom-call(bf16[512,1024]{1,0:T(8,128)(2,1)} %collective-permute-done.9.w_ref), custom_call_target="tpu_custom_call" | custom-call | flops 10000000 | bytes 100000 | tf_op jit(solution)/shard_map/pallas_call | solution.py:470
  51.1 3.9 %collective-permute-done.8.theirs_ref = bf16[256,512]{1,0:T(8,128)(2,1)S(1)} collective-permute-done((bf16[256,512]{1,0:T(8,128)(2,1)S(1)}, bf16[256,512]{1,0:T(8,128)(2,1)S(1)}, u32[]{:S(2)}, u32[]{:S(2)}) %collective-permute-start.8) | collective-permute-done | bytes 262176 | tf_op jit(solution)/shard_map/ppermute | solution.py:486
  55.0 1.2 %shard_map.106 = bf16[256,1024]{1,0:T(8,128)(2,1)} custom-call(bf16[256,512]{1,0:T(8,128)(2,1)S(1)} %collective-permute-done.8.theirs_ref, bf16[512,1024]{1,0:T(8,128)(2,1)S(1)} %shard_map.104.w_ref, bf16[256,1024]{1,0:T(8,128)(2,1)S(1)} %shard_map.105.mine_ref), custom_call_target="tpu_custom_call" | custom-call | flops 10000000 | bytes 100000 | tf_op jit(solution)/shard_map/pallas_call | solution.py:470
  (12 shorter events, 0.1 us)
Async XLA Ops:
  0.0 8.0 %copy-start.1 = (bf16[1024,512]{1,0:T(8,128)(2,1)S(1)}, bf16[1024,512]{1,0:T(8,128)(2,1)}, u32[]{:S(2)}) copy-start(bf16[1024,512]{1,0:T(8,128)(2,1)} %wk_ref.3) | copy-start | bytes 3145732
  0.0 8.0 %copy-start = (bf16[1024,512]{1,0:T(8,128)(2,1)S(1)}, bf16[1024,512]{1,0:T(8,128)(2,1)}, u32[]{:S(2)}) copy-start(bf16[1024,512]{1,0:T(8,128)(2,1)} %wq_ref.3) | copy-start | bytes 3145732
  0.0 16.0 %collective-permute-start = (bf16[256,1024]{1,0:T(8,128)(2,1)}, bf16[256,1024]{1,0:T(8,128)(2,1)S(1)}, u32[]{:S(2)}, u32[]{:S(2)}) collective-permute-start(bf16[256,1024]{1,0:T(8,128)(2,1)} %x_ref.3), channel_id=1, source_target_pairs={{0,1},{1,0},{2,3},{3,2},{4,5},{5,4},{6,7},{7,6},{8,9},{9,8},{10,11... | collective-permute-start | bytes 1572872 | tf_op jit(solution)/shard_map/ppermute | solution.py:486
  3.0 1.1 %copy-start.4 = (bf16[256,1024]{1,0:T(8,128)(2,1)S(1)}, bf16[256,1024]{1,0:T(8,128)(2,1)}, u32[]{:S(2)}) copy-start(bf16[256,1024]{1,0:T(8,128)(2,1)} %x_ref.3) | copy-start | bytes 1572868
  4.0 4.0 %copy-start.5 = (bf16[256,1024]{1,0:T(8,128)(2,1)S(1)}, bf16[256,1024]{1,0:T(8,128)(2,1)}, u32[]{:S(2)}) copy-start(bf16[256,1024]{1,0:T(8,128)(2,1)} %x_ref.3) | copy-start | bytes 1572868
  4.0 4.0 %copy-start.8 = (f32[3,4,512]{2,1,0:T(4,128)S(1)}, f32[3,4,512]{2,1,0:T(4,128)}, u32[]{:S(2)}) copy-start(f32[3,4,512]{2,1,0:T(4,128)} %conv_ref.3) | copy-start | bytes 73732
  4.1 4.0 %copy-start.9 = (bf16[1024,4]{0,1:T(4,128)(2,1)S(1)}, bf16[1024,4]{0,1:T(4,128)(2,1)}, u32[]{:S(2)}) copy-start(bf16[1024,4]{0,1:T(4,128)(2,1)} %param.13) | copy-start | bytes 24580
  4.1 4.0 %copy-start.11 = (f32[4]{0:T(128)S(1)}, f32[4]{0:T(128)}, u32[]{:S(2)}) copy-start(f32[4]{0:T(128)} %bias_ref.3) | copy-start | bytes 52
  4.1 11.9 %collective-permute-start.2 = (bf16[16,1024]{1,0:T(8,128)(2,1)S(1)}, bf16[16,1024]{1,0:T(8,128)(2,1)S(1)}, u32[]{:S(2)}, u32[]{:S(2)}) collective-permute-start(bf16[16,1024]{1,0:T(8,128)(2,1)S(1)} %get-tuple-element.38.tail_ref), channel_id=1, source_target_pairs={{0,2},{2,4},{4,6},{6,8},{8,10},{10,12},{12,14},{14,16},{16,18},{18... | collective-permute-start | bytes 98312 | tf_op jit(solution)/shard_map/ppermute | solution.py:486
  5.7 10.3 %collective-permute-start.1 = (bf16[16,1024]{1,0:T(8,128)(2,1)S(1)}, bf16[16,1024]{1,0:T(8,128)(2,1)S(1)}, u32[]{:S(2)}, u32[]{:S(2)}) collective-permute-start(bf16[16,1024]{1,0:T(8,128)(2,1)S(1)} %get-tuple-element.38.tail_ref), channel_id=1, source_target_pairs={{0,1},{1,2},{2,3},{3,4},{4,5},{5,6},{6,7},{7,8},{8,9},{9,10},{10,1... | collective-permute-start | bytes 98312 | tf_op jit(solution)/shard_map/ppermute | solution.py:486
  8.1 1.2 %copy-start.3 = (bf16[1024,512]{1,0:T(8,128)(2,1)S(1)}, bf16[1024,512]{1,0:T(8,128)(2,1)}, u32[]{:S(2)}) copy-start(bf16[1024,512]{1,0:T(8,128)(2,1)} %wv_ref.3) | copy-start | bytes 3145732
  9.3 6.7 %copy-start.2 = (bf16[1024,512]{1,0:T(8,128)(2,1)S(1)}, bf16[1024,512]{1,0:T(8,128)(2,1)}, u32[]{:S(2)}) copy-start(bf16[1024,512]{1,0:T(8,128)(2,1)} %wk_ref.3) | copy-start | bytes 3145732
  15.2 0.8 %copy-start.6 = (bf16[4,256,256]{2,1,0:T(8,128)(2,1)}, bf16[4,256,256]{2,1,0:T(8,128)(2,1)S(1)}, u32[]{:S(2)}) copy-start(bf16[4,256,256]{2,1,0:T(8,128)(2,1)S(1)} %get-tuple-element.53.early_ref) | copy-start | bytes 1572868
  22.1 27.7 %collective-permute-start.9 = (bf16[512,1024]{1,0:T(8,128)(2,1)}, bf16[512,1024]{1,0:T(8,128)(2,1)}, u32[]{:S(2)}, u32[]{:S(2)}) collective-permute-start(bf16[512,1024]{1,0:T(8,128)(2,1)} %w_ref.1), channel_id=1, source_target_pairs={{0,1},{1,0},{2,3},{3,2},{4,5},{5,4},{6,7},{7,6},{8,9},{9,8},{10,11... | collective-permute-start | bytes 3145736 | tf_op jit(solution)/shard_map/ppermute | solution.py:486
  25.5 1.3 %collective-permute-start.3 = (bf16[2,128,256]{2,1,0:T(8,128)(2,1)S(1)}, bf16[2,128,256]{2,1,0:T(8,128)(2,1)S(1)}, u32[]{:S(2)}, u32[]{:S(2)}) collective-permute-start(bf16[2,128,256]{2,1,0:T(8,128)(2,1)S(1)} %get-tuple-element.42), channel_id=1, source_target_pairs={{0,2},{2,0},{4,6},{6,4},{8,10},{10,8},{12,14},{14,12},{16,18},{18,... | collective-permute-start | bytes 393224 | tf_op jit(solution)/shard_map/ppermute | solution.py:486
  27.0 5.6 %collective-permute-start.4 = (bf16[2,128,256]{2,1,0:T(8,128)(2,1)S(1)}, bf16[2,128,256]{2,1,0:T(8,128)(2,1)S(1)}, u32[]{:S(2)}, u32[]{:S(2)}) collective-permute-start(bf16[2,128,256]{2,1,0:T(8,128)(2,1)S(1)} %shard_map.94.own_ref), channel_id=1, source_target_pairs={{0,4},{2,6},{4,0},{6,2},{8,12},{10,14},{12,8},{14,10},{16,20},{18,... | collective-permute-start | bytes 393224 | tf_op jit(solution)/shard_map/ppermute | solution.py:486
  32.8 5.0 %collective-permute-start.5 = (bf16[2,128,256]{2,1,0:T(8,128)(2,1)S(1)}, bf16[2,128,256]{2,1,0:T(8,128)(2,1)S(1)}, u32[]{:S(2)}, u32[]{:S(2)}) collective-permute-start(bf16[2,128,256]{2,1,0:T(8,128)(2,1)S(1)} %shard_map.97.own_ref), channel_id=1, source_target_pairs={{0,8},{2,10},{4,12},{6,14},{8,0},{10,2},{12,4},{14,6},{16,24},{18,... | collective-permute-start | bytes 393224 | tf_op jit(solution)/shard_map/ppermute | solution.py:486
  34.4 1.0 %copy-start.7 = (bf16[4,256,256]{2,1,0:T(8,128)(2,1)S(1)}, bf16[4,256,256]{2,1,0:T(8,128)(2,1)}, u32[]{:S(2)}) copy-start(bf16[4,256,256]{2,1,0:T(8,128)(2,1)} %copy-done.6) | copy-start | bytes 1572868
  36.0 9.9 %copy-start.10 = (f32[512]{0:T(512)S(1)}, f32[512]{0:T(512)}, u32[]{:S(2)}) copy-start(f32[512]{0:T(512)} %param.16) | copy-start | bytes 6148
  38.0 6.4 %collective-permute-start.6 = (bf16[2,128,128]{2,1,0:T(8,128)(2,1)S(1)}, bf16[2,128,128]{2,1,0:T(8,128)(2,1)S(1)}, u32[]{:S(2)}, u32[]{:S(2)}) collective-permute-start(bf16[2,128,128]{2,1,0:T(8,128)(2,1)S(1)} %shard_map.100), channel_id=1, source_target_pairs={{0,16},{2,18},{4,20},{6,22},{8,24},{10,26},{12,28},{14,30},{1,17},... | collective-permute-start | bytes 196616 | tf_op jit(solution)/shard_map/ppermute | solution.py:486
  44.6 1.3 %collective-permute-start.7 = (bf16[2,128,128]{2,1,0:T(8,128)(2,1)S(1)}, bf16[2,128,128]{2,1,0:T(8,128)(2,1)S(1)}, u32[]{:S(2)}, u32[]{:S(2)}) collective-permute-start(bf16[2,128,128]{2,1,0:T(8,128)(2,1)S(1)} %get-tuple-element.62), channel_id=1, source_target_pairs={{0,2},{2,0},{4,6},{6,4},{8,10},{10,8},{12,14},{14,12},{16,18},{18,... | collective-permute-start | bytes 196616 | tf_op jit(solution)/shard_map/ppermute | solution.py:486
  46.3 8.8 %collective-permute-start.8 = (bf16[256,512]{1,0:T(8,128)(2,1)S(1)}, bf16[256,512]{1,0:T(8,128)(2,1)S(1)}, u32[]{:S(2)}, u32[]{:S(2)}) collective-permute-start(bf16[256,512]{1,0:T(8,128)(2,1)S(1)} %shard_map.103), channel_id=1, source_target_pairs={{0,1},{1,0},{2,3},{3,2},{4,5},{5,4},{6,7},{7,6},{8,9},{9,8},{10,11... | collective-permute-start | bytes 786440 | tf_op jit(solution)/shard_map/ppermute | solution.py:486

commit v5 on v4

--- a/solution.py
+++ b/solution.py
@@ -243,6 +243,25 @@
     tail_ref[...] = x_ref[x_ref.shape[0] - tail_ref.shape[0] :]
 
 
+def half_kernel(bit_ref, w_ref, part_ref):
+    part_ref[...] = w_ref[...]
+
+
+def half_rows(w_out, bit):
+    half = (w_out.shape[0] // 2, w_out.shape[1])
+    return pl.pallas_call(
+        half_kernel,
+        grid_spec=pltpu.PrefetchScalarGridSpec(
+            num_scalar_prefetch=1,
+            grid=(1,),
+            in_specs=[pl.BlockSpec(half, lambda at, bit: (bit[0], 0))],
+            out_specs=pl.BlockSpec(half, lambda at, bit: (0, 0)),
+        ),
+        out_shape=jax.ShapeDtypeStruct(half, w_out.dtype),
+        cost_estimate=pl.CostEstimate(flops=10**7, bytes_accessed=10**5, transcendentals=0),
+    )(bit, w_out)
+
+
 def early_kernel(
     bias_ref, x_ref, wq_ref, wk_ref, wv_ref, wb_ref, conv_ref, pair_ref, look_ref, proj_ref
 ):
@@ -455,8 +474,11 @@
     out_ref[...] = dot(normed_ref[...], w_ref[...]).astype(BF16)
 
 
-def hold_kernel(w_ref, held_ref):
-    held_ref[...] = w_ref[...]
+def hold_kernel(bit_ref, part_ref, rest_ref, whole_ref):
+    rows = part_ref.shape[0]
+    later = bit_ref[0] == 1
+    whole_ref[:rows] = jnp.where(later, rest_ref[...], part_ref[...])
+    whole_ref[rows:] = jnp.where(later, part_ref[...], rest_ref[...])
 
 
 def output_kernel(theirs_ref, w_ref, mine_ref, out_ref):
@@ -546,14 +568,9 @@
         scratch=[pltpu.VMEM((3, rows + 3 * HALO, columns), F32)],
         grant=24,
     )
-    if groups == 2:
-        w_sent, keep = together(w_out, keep)
-        w_other = shift(w_sent, "head", swap)
     own = keep
     for level in range(levels):
         partner = [(i, i ^ (1 << level)) for i in range(shards)]
-        if level == levels - 1:
-            partner = [(i, j) for i, j in partner if j > i]
         came = shift(send, "seq", partner)
         if level == 1:
             late = call(
@@ -563,6 +580,9 @@
                 scalars=[swapped],
             )[0]
             came, path, late = together(came, path, late)
+            if groups == 2:
+                came, part = together(came, part)
+                part = shift(part, "head", swap)
         elif level == 2:
             early = call(
                 functools.partial(look_early_kernel, conv_weight.shape[1]),
@@ -583,6 +603,9 @@
         )[0]
         if level == 0:
             own, came, send = together(own, came, send)
+            if groups == 2:
+                w_sent, send = together(w_out, send)
+                part = half_rows(w_sent, bits[0])
             path = call(
                 open_kernel, [((kept, 2 * dim, 2 * dim), BF16)], [own, came], scalars=[bits[0]]
             )[0]
@@ -613,9 +636,12 @@
             [keep, came, early, gain, w_out],
             scalars=[bits[0]],
             scratch=[pltpu.VMEM((rows, columns), BF16)],
+            grant=62,
+            flops=6 * 10**9,
         )[0]
-        w_other, gone = together(w_other, gone)
-        whole = call(hold_kernel, [(w_out.shape, BF16)], [w_other])[0]
+        part, gone = together(part, gone)
+        rest = shift(part, "seq", [(i, i ^ 1) for i in range(shards)])
+        whole = call(hold_kernel, [(w_out.shape, BF16)], [part, rest], scalars=[bits[0]])[0]
         theirs, whole = together(theirs, whole)
         return call(output_kernel, [((rows, width), BF16)], [theirs, whole, mine])[0]
     normed = call(

time: 56.6 us -> 55.2 us (0.975)
  Pallas kernels: 20.2 us -> 22.1 us
  waiting for transfers between devices: 13.2 us -> 11.3 us
  starting transfers between devices: 18.5 us -> 17 us
    ppermute x10 -> x11, waiting for transfers between devices: 13.2 us -> 11.3 us  [shift(): return lax.ppermute(block, axes, pairs)]
    pallas_call x0 -> x1, Pallas kernels: none -> 1.87 us  [half_rows(): pl.pallas_call(half_kernel, grid_spec=pltpu.PrefetchScalarGridSpec(num_sc...]
    ppermute x10 -> x11, starting transfers between devices: 18.5 us -> 17 us  [shift(): return lax.ppermute(block, axes, pairs)]
    unnamed x24 -> x32, local copies, waits for them, and re-layouts: 4.16 us -> 4.2 us
  transfers between devices with their start and end apart: 10 -> 11, of which waited for: 7 -> 6; matrix products, arithmetic and copies ran while one was open for 0% -> 0% of each run, Pallas kernels for 23% -> 27%
where the time goes in v5:
time: 55.2 us; the launch traced here: 54.9 us
  Pallas kernels  22.1 us (40%)
  starting transfers between devices  17 us (31%)
  waiting for transfers between devices  11.3 us (20%)
  local copies, waits for them, and re-layouts  4.2 us (8%)
    pallas_call x16, Pallas kernels, call(): pl.pallas_call(kernel, out_shape=[jax.ShapeDtypeStruct(shape, dtype) for...  20.2 us
    ppermute x11, starting transfers between devices, shift(): return lax.ppermute(block, axes, pairs)  17 us
    ppermute x11, waiting for transfers between devices, shift(): return lax.ppermute(block, axes, pairs)  11.3 us
    unnamed x32, local copies, waits for them, and re-layouts  4.2 us
    pallas_call x1, Pallas kernels, half_rows(): pl.pallas_call(half_kernel, grid_spec=pltpu.PrefetchScalarGridSpec(num_sc...  1.87 us
  transfers between devices with their start and end apart: 11, of which 6 were waited for; matrix products, arithmetic and copies ran while one was open for 0% of the time, Pallas kernels for 27%

profile of v5, /device:TPU:0, one launch (start us, length us, event | category | flops | bytes accessed | tf_op | source)
XLA Modules:
  0.0 54.9 jit_solution(2071912097902959177)
XLA Ops:
  0.0 3.0 %collective-permute-start = (bf16[256,1024]{1,0:T(8,128)(2,1)}, bf16[256,1024]{1,0:T(8,128)(2,1)S(1)}, u32[]{:S(2)}, u32[]{:S(2)}) collective-permute-start(bf16[256,1024]{1,0:T(8,128)(2,1)} %x_ref.3), channel_id=1, source_target_pairs={{0,1},{1,0},{2,3},{3,2},{4,5},{5,4},{6,7},{7,6},{8,9},{9,8},{10,11... | collective-permute-start | bytes 1572872 | tf_op jit(solution)/shard_map/ppermute | solution.py:508
  3.0 1.1 %copy-done.4 = bf16[256,1024]{1,0:T(8,128)(2,1)S(1)} copy-done((bf16[256,1024]{1,0:T(8,128)(2,1)S(1)}, bf16[256,1024]{1,0:T(8,128)(2,1)}, u32[]{:S(2)}) %copy-start.4) | copy-done | bytes 524312
  4.1 1.6 %collective-permute-start.2 = (bf16[16,1024]{1,0:T(8,128)(2,1)S(1)}, bf16[16,1024]{1,0:T(8,128)(2,1)S(1)}, u32[]{:S(2)}, u32[]{:S(2)}) collective-permute-start(bf16[16,1024]{1,0:T(8,128)(2,1)S(1)} %get-tuple-element.40.tail_ref), channel_id=1, source_target_pairs={{0,2},{2,4},{4,6},{6,8},{8,10},{10,12},{12,14},{14,16},{16,18},{18... | collective-permute-start | bytes 98312 | tf_op jit(solution)/shard_map/ppermute | solution.py:508
  5.7 2.3 %collective-permute-start.1 = (bf16[16,1024]{1,0:T(8,128)(2,1)S(1)}, bf16[16,1024]{1,0:T(8,128)(2,1)S(1)}, u32[]{:S(2)}, u32[]{:S(2)}) collective-permute-start(bf16[16,1024]{1,0:T(8,128)(2,1)S(1)} %get-tuple-element.40.tail_ref), channel_id=1, source_target_pairs={{0,1},{1,2},{2,3},{3,4},{4,5},{5,6},{6,7},{7,8},{8,9},{9,10},{10,1... | collective-permute-start | bytes 98312 | tf_op jit(solution)/shard_map/ppermute | solution.py:508
  8.0 0.0 copy-done.1
  8.0 0.0 copy-done
  8.0 0.0 copy-done.5
  8.1 0.0 copy-start.3
  8.1 1.2 %copy-done.3 = bf16[1024,512]{1,0:T(8,128)(2,1)S(1)} copy-done((bf16[1024,512]{1,0:T(8,128)(2,1)S(1)}, bf16[1024,512]{1,0:T(8,128)(2,1)}, u32[]{:S(2)}) %copy-start.3) | copy-done | bytes 1048600
  9.3 5.9 %shard_map.92 = (f32[4,128,256]{2,1,0:T(8,128)S(1)}, bf16[4,256,256]{2,1,0:T(8,128)(2,1)S(1)}) custom-call(f32[4]{0:T(128)S(1)} %copy-done.15, bf16[256,1024]{1,0:T(8,128)(2,1)S(1)} %copy-done.5, bf16[1024,512]{1,0:T(8,128)(2,1)S(1)} %copy-done, bf16[1024,512]{1,0:T(8,128)(2,1)S(1)} %copy-done.1, bf16[1024,512]{1,0:T(8,128)(2,1)S(1)} %copy-done.3, ...), custom_call_target="tpu_custom_call" | custom-call | flops 10000000 | bytes 100000 | tf_op jit(solution)/shard_map/pallas_call | solution.py:492
  15.2 0.8 %copy-done.6 = bf16[4,256,256]{2,1,0:T(8,128)(2,1)} copy-done((bf16[4,256,256]{2,1,0:T(8,128)(2,1)}, bf16[4,256,256]{2,1,0:T(8,128)(2,1)S(1)}, u32[]{:S(2)}) %copy-start.6) | copy-done | bytes 524312
  16.0 0.0 collective-permute-done.2.behind_ref
  16.0 0.0 collective-permute-done.1.halo_ref
  16.0 0.0 collective-permute-done.x_ref
  16.0 0.0 copy-done.2
  16.0 6.1 %shard_map.93 = (bf16[2,128,256]{2,1,0:T(8,128)(2,1)S(1)}, bf16[2,128,256]{2,1,0:T(8,128)(2,1)S(1)}, f32[4,256]{1,0:T(4,128)S(1)}, bf16[4,784,256]{2,1,0:T(8,128)(2,1)S(1)}) custom-call(s32[1]{0:T(128)} %bitcast.2.swapped_ref, s32[1]{0:T(128)} %bitcast.bit_ref.flags_ref, f32[4]{0:T(128)S(1)} %copy-done.15, bf16[256,1024]{1,0:T(8,128)(2,1)S(1)} %collective-permute-done.x_ref, ...), custom_call_target="tpu_custom_call" | custom-call | flops 10000000 | bytes 100000 | tf_op jit(solution)/shard_map/pallas_call | solution.py:492
  22.1 2.0 %collective-permute-start.3 = (bf16[2,128,256]{2,1,0:T(8,128)(2,1)S(1)}, bf16[2,128,256]{2,1,0:T(8,128)(2,1)S(1)}, u32[]{:S(2)}, u32[]{:S(2)}) collective-permute-start(bf16[2,128,256]{2,1,0:T(8,128)(2,1)S(1)} %get-tuple-element.43), channel_id=1, source_target_pairs={{0,2},{2,0},{4,6},{6,4},{8,10},{10,8},{12,14},{14,12},{16,18},{18,... | collective-permute-start | bytes 393224 | tf_op jit(solution)/shard_map/ppermute | solution.py:508
  24.2 1.0 %collective-permute-done.3.other_ref = bf16[2,128,256]{2,1,0:T(8,128)(2,1)S(1)} collective-permute-done((bf16[2,128,256]{2,1,0:T(8,128)(2,1)S(1)}, bf16[2,128,256]{2,1,0:T(8,128)(2,1)S(1)}, u32[]{:S(2)}, u32[]{:S(2)}) %collective-permute-start.3) | collective-permute-done | bytes 131104 | tf_op jit(solution)/shard_map/ppermute | solution.py:508
  25.2 0.2 shard_map.94.own_ref
  25.3 1.6 %collective-permute-start.4 = (bf16[2,128,256]{2,1,0:T(8,128)(2,1)S(1)}, bf16[2,128,256]{2,1,0:T(8,128)(2,1)S(1)}, u32[]{:S(2)}, u32[]{:S(2)}) collective-permute-start(bf16[2,128,256]{2,1,0:T(8,128)(2,1)S(1)} %shard_map.94.own_ref), channel_id=1, source_target_pairs={{0,4},{2,6},{4,0},{6,2},{8,12},{10,14},{12,8},{14,10},{16,20},{18,... | collective-permute-start | bytes 393224 | tf_op jit(solution)/shard_map/ppermute | solution.py:508
  27.0 1.7 %shard_map.96.reads_ref = bf16[4,256,256]{2,1,0:T(8,128)(2,1)S(1)} custom-call(s32[1]{0:T(128)} %bitcast.2.swapped_ref, f32[4,256]{1,0:T(4,128)S(1)} %get-tuple-element.48.norm_ref, bf16[4,784,256]{2,1,0:T(8,128)(2,1)S(1)} %get-tuple-element.49.held_ref), custom_call_target="tpu_custom_call" | custom-call | flops 10000000 | bytes 100000 | tf_op jit(solution)/shard_map/pallas_call | solution.py:492
  28.6 1.9 %shard_map.97 = bf16[256,1024]{1,0:T(8,128)(2,1)} custom-call(s32[1]{0:T(128)} %bitcast.bit_ref.flags_ref, bf16[512,1024]{1,0:T(8,128)(2,1)} %w_ref.2), custom_call_target="tpu_custom_call" | custom-call | flops 10000000 | bytes 100000 | tf_op jit(solution)/shard_map/pallas_call | solution.py:252
  30.5 0.6 %collective-permute-done.4.other_ref.came_ref = bf16[2,128,256]{2,1,0:T(8,128)(2,1)S(1)} collective-permute-done((bf16[2,128,256]{2,1,0:T(8,128)(2,1)S(1)}, bf16[2,128,256]{2,1,0:T(8,128)(2,1)S(1)}, u32[]{:S(2)}, u32[]{:S(2)}) %collective-permute-start.4) | collective-permute-done | bytes 131104 | tf_op jit(solution)/shard_map/ppermute | solution.py:508
  31.2 1.5 %collective-permute-start.9 = (bf16[256,1024]{1,0:T(8,128)(2,1)}, bf16[256,1024]{1,0:T(8,128)(2,1)S(1)}, u32[]{:S(2)}, u32[]{:S(2)}) collective-permute-start(bf16[256,1024]{1,0:T(8,128)(2,1)} %shard_map.97), channel_id=1, source_target_pairs={{0,1},{1,0},{2,3},{3,2},{4,5},{5,4},{6,7},{7,6},{8,9},{9,8},{10,11... | collective-permute-start | bytes 1572872 | tf_op jit(solution)/shard_map/ppermute | solution.py:508
  32.6 0.2 shard_map.98.own_ref
  32.8 1.6 %collective-permute-start.5 = (bf16[2,128,256]{2,1,0:T(8,128)(2,1)S(1)}, bf16[2,128,256]{2,1,0:T(8,128)(2,1)S(1)}, u32[]{:S(2)}, u32[]{:S(2)}) collective-permute-start(bf16[2,128,256]{2,1,0:T(8,128)(2,1)S(1)} %shard_map.98.own_ref), channel_id=1, source_target_pairs={{0,8},{2,10},{4,12},{6,14},{8,0},{10,2},{12,4},{14,6},{16,24},{18,... | collective-permute-start | bytes 393224 | tf_op jit(solution)/shard_map/ppermute | solution.py:508
  34.5 1.0 %copy-done.7 = bf16[4,256,256]{2,1,0:T(8,128)(2,1)S(1)} copy-done((bf16[4,256,256]{2,1,0:T(8,128)(2,1)S(1)}, bf16[4,256,256]{2,1,0:T(8,128)(2,1)}, u32[]{:S(2)}) %copy-start.7) | copy-done | bytes 524312
  35.5 0.7 %shard_map.100.reads_ref = bf16[4,256,256]{2,1,0:T(8,128)(2,1)S(1)} custom-call(s32[1]{0:T(128)} %bitcast.2.swapped_ref, bf16[4,784,256]{2,1,0:T(8,128)(2,1)S(1)} %get-tuple-element.49.held_ref, bf16[4,256,256]{2,1,0:T(8,128)(2,1)S(1)} %copy-done.7), custom_call_target="tpu_custom_call" | custom-call | flops 10000000 | bytes 100000 | tf_op jit(solution)/shard_map/pallas_call | solution.py:492
  36.2 0.0 copy-start.14
  36.2 0.2 shard_map.99.path_ref
  36.4 1.4 %collective-permute-done.5.other_ref.came_ref = bf16[2,128,256]{2,1,0:T(8,128)(2,1)S(1)} collective-permute-done((bf16[2,128,256]{2,1,0:T(8,128)(2,1)S(1)}, bf16[2,128,256]{2,1,0:T(8,128)(2,1)S(1)}, u32[]{:S(2)}, u32[]{:S(2)}) %collective-permute-start.5) | collective-permute-done | bytes 131104 | tf_op jit(solution)/shard_map/ppermute | solution.py:508
  37.8 0.2 shard_map.101
  38.0 2.7 %collective-permute-start.6 = (bf16[2,128,128]{2,1,0:T(8,128)(2,1)S(1)}, bf16[2,128,128]{2,1,0:T(8,128)(2,1)S(1)}, u32[]{:S(2)}, u32[]{:S(2)}) collective-permute-start(bf16[2,128,128]{2,1,0:T(8,128)(2,1)S(1)} %shard_map.101), channel_id=1, source_target_pairs={{0,16},{2,18},{4,20},{6,22},{8,24},{10,26},{12,28},{14,30},{16,0},... | collective-permute-start | bytes 196616 | tf_op jit(solution)/shard_map/ppermute | solution.py:508
  40.7 0.2 shard_map.102.path_ref
  40.9 2.4 %collective-permute-done.6.state_ref = bf16[2,128,128]{2,1,0:T(8,128)(2,1)S(1)} collective-permute-done((bf16[2,128,128]{2,1,0:T(8,128)(2,1)S(1)}, bf16[2,128,128]{2,1,0:T(8,128)(2,1)S(1)}, u32[]{:S(2)}, u32[]{:S(2)}) %collective-permute-start.6) | collective-permute-done | bytes 65568 | tf_op jit(solution)/shard_map/ppermute | solution.py:508
  43.3 0.2 shard_map.103
  43.5 0.1 collective-permute-start.7
  43.5 1.2 %collective-permute-done.7.came_ref = bf16[2,128,128]{2,1,0:T(8,128)(2,1)S(1)} collective-permute-done((bf16[2,128,128]{2,1,0:T(8,128)(2,1)S(1)}, bf16[2,128,128]{2,1,0:T(8,128)(2,1)S(1)}, u32[]{:S(2)}, u32[]{:S(2)}) %collective-permute-start.7) | collective-permute-done | bytes 65568 | tf_op jit(solution)/shard_map/ppermute | solution.py:508
  44.8 0.4 shard_map.104
  45.2 0.6 %collective-permute-start.8 = (bf16[256,512]{1,0:T(8,128)(2,1)S(1)}, bf16[256,512]{1,0:T(8,128)(2,1)S(1)}, u32[]{:S(2)}, u32[]{:S(2)}) collective-permute-start(bf16[256,512]{1,0:T(8,128)(2,1)S(1)} %shard_map.104), channel_id=1, source_target_pairs={{0,1},{1,0},{2,3},{3,2},{4,5},{5,4},{6,7},{7,6},{8,9},{9,8},{10,11... | collective-permute-start | bytes 786440 | tf_op jit(solution)/shard_map/ppermute | solution.py:508
  45.8 0.0 collective-permute-done.9.part_ref
  45.8 0.0 collective-permute-start.10
  45.8 0.0 copy-done.12
  45.8 3.0 %shard_map.106.mine_ref = bf16[256,1024]{1,0:T(8,128)(2,1)} custom-call(s32[1]{0:T(128)} %bitcast.bit_ref.flags_ref, bf16[2,128,128]{2,1,0:T(8,128)(2,1)} %copy-done.11, bf16[2,128,128]{2,1,0:T(8,128)(2,1)} %copy-done.12, bf16[4,256,256]{2,1,0:T(8,128)(2,1)} %copy-done.8, f32[1,512]{1,0:T(1,128)} %bitcast.9, bf16[512,1024]{1,0:T(8,128)(2,1)} %w_ref.2), custom_call_target="tpu_custom_call" | custom-call | flops 6000000000 | bytes 100000 | tf_op jit(solution)/shard_map/pallas_call | solution.py:492
  48.8 0.0 collective-permute-done.10.rest_ref
  48.8 0.1 shard_map.105.w_ref
  48.9 4.7 %collective-permute-done.8.theirs_ref = bf16[256,512]{1,0:T(8,128)(2,1)S(1)} collective-permute-done((bf16[256,512]{1,0:T(8,128)(2,1)S(1)}, bf16[256,512]{1,0:T(8,128)(2,1)S(1)}, u32[]{:S(2)}, u32[]{:S(2)}) %collective-permute-start.8) | collective-permute-done | bytes 262176 | tf_op jit(solution)/shard_map/ppermute | solution.py:508
  53.6 1.2 %shard_map.107 = bf16[256,1024]{1,0:T(8,128)(2,1)} custom-call(bf16[256,512]{1,0:T(8,128)(2,1)S(1)} %collective-permute-done.8.theirs_ref, bf16[512,1024]{1,0:T(8,128)(2,1)S(1)} %shard_map.105.w_ref, bf16[256,1024]{1,0:T(8,128)(2,1)S(1)} %copy-done.9), custom_call_target="tpu_custom_call" | custom-call | flops 10000000 | bytes 100000 | tf_op jit(solution)/shard_map/pallas_call | solution.py:492
  (23 shorter events, 0.1 us)
Async XLA Ops:
  0.0 8.0 %copy-start.1 = (bf16[1024,512]{1,0:T(8,128)(2,1)S(1)}, bf16[1024,512]{1,0:T(8,128)(2,1)}, u32[]{:S(2)}) copy-start(bf16[1024,512]{1,0:T(8,128)(2,1)} %wk_ref.3) | copy-start | bytes 3145732
  0.0 8.0 %copy-start = (bf16[1024,512]{1,0:T(8,128)(2,1)S(1)}, bf16[1024,512]{1,0:T(8,128)(2,1)}, u32[]{:S(2)}) copy-start(bf16[1024,512]{1,0:T(8,128)(2,1)} %wq_ref.3) | copy-start | bytes 3145732
  0.0 16.0 %collective-permute-start = (bf16[256,1024]{1,0:T(8,128)(2,1)}, bf16[256,1024]{1,0:T(8,128)(2,1)S(1)}, u32[]{:S(2)}, u32[]{:S(2)}) collective-permute-start(bf16[256,1024]{1,0:T(8,128)(2,1)} %x_ref.3), channel_id=1, source_target_pairs={{0,1},{1,0},{2,3},{3,2},{4,5},{5,4},{6,7},{7,6},{8,9},{9,8},{10,11... | collective-permute-start | bytes 1572872 | tf_op jit(solution)/shard_map/ppermute | solution.py:508
  3.0 1.1 %copy-start.4 = (bf16[256,1024]{1,0:T(8,128)(2,1)S(1)}, bf16[256,1024]{1,0:T(8,128)(2,1)}, u32[]{:S(2)}) copy-start(bf16[256,1024]{1,0:T(8,128)(2,1)} %x_ref.3) | copy-start | bytes 1572868
  4.0 4.0 %copy-start.5 = (bf16[256,1024]{1,0:T(8,128)(2,1)S(1)}, bf16[256,1024]{1,0:T(8,128)(2,1)}, u32[]{:S(2)}) copy-start(bf16[256,1024]{1,0:T(8,128)(2,1)} %x_ref.3) | copy-start | bytes 1572868
  4.0 4.0 %copy-start.10 = (f32[3,4,512]{2,1,0:T(4,128)S(1)}, f32[3,4,512]{2,1,0:T(4,128)}, u32[]{:S(2)}) copy-start(f32[3,4,512]{2,1,0:T(4,128)} %conv_ref.3) | copy-start | bytes 73732
  4.1 4.0 %copy-start.13 = (bf16[1024,4]{0,1:T(4,128)(2,1)S(1)}, bf16[1024,4]{0,1:T(4,128)(2,1)}, u32[]{:S(2)}) copy-start(bf16[1024,4]{0,1:T(4,128)(2,1)} %param.13) | copy-start | bytes 24580
  4.1 4.0 %copy-start.15 = (f32[4]{0:T(128)S(1)}, f32[4]{0:T(128)}, u32[]{:S(2)}) copy-start(f32[4]{0:T(128)} %bias_ref.3) | copy-start | bytes 52
  4.1 12.0 %collective-permute-start.2 = (bf16[16,1024]{1,0:T(8,128)(2,1)S(1)}, bf16[16,1024]{1,0:T(8,128)(2,1)S(1)}, u32[]{:S(2)}, u32[]{:S(2)}) collective-permute-start(bf16[16,1024]{1,0:T(8,128)(2,1)S(1)} %get-tuple-element.40.tail_ref), channel_id=1, source_target_pairs={{0,2},{2,4},{4,6},{6,8},{8,10},{10,12},{12,14},{14,16},{16,18},{18... | collective-permute-start | bytes 98312 | tf_op jit(solution)/shard_map/ppermute | solution.py:508
  5.7 10.4 %collective-permute-start.1 = (bf16[16,1024]{1,0:T(8,128)(2,1)S(1)}, bf16[16,1024]{1,0:T(8,128)(2,1)S(1)}, u32[]{:S(2)}, u32[]{:S(2)}) collective-permute-start(bf16[16,1024]{1,0:T(8,128)(2,1)S(1)} %get-tuple-element.40.tail_ref), channel_id=1, source_target_pairs={{0,1},{1,2},{2,3},{3,4},{4,5},{5,6},{6,7},{7,8},{8,9},{9,10},{10,1... | collective-permute-start | bytes 98312 | tf_op jit(solution)/shard_map/ppermute | solution.py:508
  8.1 1.2 %copy-start.3 = (bf16[1024,512]{1,0:T(8,128)(2,1)S(1)}, bf16[1024,512]{1,0:T(8,128)(2,1)}, u32[]{:S(2)}) copy-start(bf16[1024,512]{1,0:T(8,128)(2,1)} %wv_ref.3) | copy-start | bytes 3145732
  9.3 6.8 %copy-start.2 = (bf16[1024,512]{1,0:T(8,128)(2,1)S(1)}, bf16[1024,512]{1,0:T(8,128)(2,1)}, u32[]{:S(2)}) copy-start(bf16[1024,512]{1,0:T(8,128)(2,1)} %wk_ref.3) | copy-start | bytes 3145732
  15.2 0.8 %copy-start.6 = (bf16[4,256,256]{2,1,0:T(8,128)(2,1)}, bf16[4,256,256]{2,1,0:T(8,128)(2,1)S(1)}, u32[]{:S(2)}) copy-start(bf16[4,256,256]{2,1,0:T(8,128)(2,1)S(1)} %get-tuple-element.57.early_ref) | copy-start | bytes 1572868
  22.1 3.0 %collective-permute-start.3 = (bf16[2,128,256]{2,1,0:T(8,128)(2,1)S(1)}, bf16[2,128,256]{2,1,0:T(8,128)(2,1)S(1)}, u32[]{:S(2)}, u32[]{:S(2)}) collective-permute-start(bf16[2,128,256]{2,1,0:T(8,128)(2,1)S(1)} %get-tuple-element.43), channel_id=1, source_target_pairs={{0,2},{2,0},{4,6},{6,4},{8,10},{10,8},{12,14},{14,12},{16,18},{18,... | collective-permute-start | bytes 393224 | tf_op jit(solution)/shard_map/ppermute | solution.py:508
  25.3 5.8 %collective-permute-start.4 = (bf16[2,128,256]{2,1,0:T(8,128)(2,1)S(1)}, bf16[2,128,256]{2,1,0:T(8,128)(2,1)S(1)}, u32[]{:S(2)}, u32[]{:S(2)}) collective-permute-start(bf16[2,128,256]{2,1,0:T(8,128)(2,1)S(1)} %shard_map.94.own_ref), channel_id=1, source_target_pairs={{0,4},{2,6},{4,0},{6,2},{8,12},{10,14},{12,8},{14,10},{16,20},{18,... | collective-permute-start | bytes 393224 | tf_op jit(solution)/shard_map/ppermute | solution.py:508
  31.2 14.6 %collective-permute-start.9 = (bf16[256,1024]{1,0:T(8,128)(2,1)}, bf16[256,1024]{1,0:T(8,128)(2,1)S(1)}, u32[]{:S(2)}, u32[]{:S(2)}) collective-permute-start(bf16[256,1024]{1,0:T(8,128)(2,1)} %shard_map.97), channel_id=1, source_target_pairs={{0,1},{1,0},{2,3},{3,2},{4,5},{5,4},{6,7},{7,6},{8,9},{9,8},{10,11... | collective-permute-start | bytes 1572872 | tf_op jit(solution)/shard_map/ppermute | solution.py:508
  32.8 5.0 %collective-permute-start.5 = (bf16[2,128,256]{2,1,0:T(8,128)(2,1)S(1)}, bf16[2,128,256]{2,1,0:T(8,128)(2,1)S(1)}, u32[]{:S(2)}, u32[]{:S(2)}) collective-permute-start(bf16[2,128,256]{2,1,0:T(8,128)(2,1)S(1)} %shard_map.98.own_ref), channel_id=1, source_target_pairs={{0,8},{2,10},{4,12},{6,14},{8,0},{10,2},{12,4},{14,6},{16,24},{18,... | collective-permute-start | bytes 393224 | tf_op jit(solution)/shard_map/ppermute | solution.py:508
  34.5 1.0 %copy-start.7 = (bf16[4,256,256]{2,1,0:T(8,128)(2,1)S(1)}, bf16[4,256,256]{2,1,0:T(8,128)(2,1)}, u32[]{:S(2)}) copy-start(bf16[4,256,256]{2,1,0:T(8,128)(2,1)} %copy-done.6) | copy-start | bytes 1572868
  36.2 1.8 %copy-start.8 = (bf16[4,256,256]{2,1,0:T(8,128)(2,1)}, bf16[4,256,256]{2,1,0:T(8,128)(2,1)S(1)}, u32[]{:S(2)}) copy-start(bf16[4,256,256]{2,1,0:T(8,128)(2,1)S(1)} %shard_map.100.reads_ref) | copy-start | bytes 1572868
  36.2 8.6 %copy-start.14 = (f32[512]{0:T(512)S(1)}, f32[512]{0:T(512)}, u32[]{:S(2)}) copy-start(f32[512]{0:T(512)} %param.16) | copy-start | bytes 6148
  38.0 5.2 %collective-permute-start.6 = (bf16[2,128,128]{2,1,0:T(8,128)(2,1)S(1)}, bf16[2,128,128]{2,1,0:T(8,128)(2,1)S(1)}, u32[]{:S(2)}, u32[]{:S(2)}) collective-permute-start(bf16[2,128,128]{2,1,0:T(8,128)(2,1)S(1)} %shard_map.101), channel_id=1, source_target_pairs={{0,16},{2,18},{4,20},{6,22},{8,24},{10,26},{12,28},{14,30},{16,0},... | collective-permute-start | bytes 196616 | tf_op jit(solution)/shard_map/ppermute | solution.py:508
  43.5 2.4 %copy-start.11 = (bf16[2,128,128]{2,1,0:T(8,128)(2,1)}, bf16[2,128,128]{2,1,0:T(8,128)(2,1)S(1)}, u32[]{:S(2)}) copy-start(bf16[2,128,128]{2,1,0:T(8,128)(2,1)S(1)} %get-tuple-element.65.keep_ref) | copy-start | bytes 196612
  43.5 1.3 %collective-permute-start.7 = (bf16[2,128,128]{2,1,0:T(8,128)(2,1)S(1)}, bf16[2,128,128]{2,1,0:T(8,128)(2,1)S(1)}, u32[]{:S(2)}, u32[]{:S(2)}) collective-permute-start(bf16[2,128,128]{2,1,0:T(8,128)(2,1)S(1)} %get-tuple-element.66), channel_id=1, source_target_pairs={{0,2},{2,0},{4,6},{6,4},{8,10},{10,8},{12,14},{14,12},{16,18},{18,... | collective-permute-start | bytes 196616 | tf_op jit(solution)/shard_map/ppermute | solution.py:508
  44.8 1.0 %copy-start.12 = (bf16[2,128,128]{2,1,0:T(8,128)(2,1)}, bf16[2,128,128]{2,1,0:T(8,128)(2,1)S(1)}, u32[]{:S(2)}) copy-start(bf16[2,128,128]{2,1,0:T(8,128)(2,1)S(1)} %collective-permute-done.7.came_ref) | copy-start | bytes 196612
  45.2 8.4 %collective-permute-start.8 = (bf16[256,512]{1,0:T(8,128)(2,1)S(1)}, bf16[256,512]{1,0:T(8,128)(2,1)S(1)}, u32[]{:S(2)}, u32[]{:S(2)}) collective-permute-start(bf16[256,512]{1,0:T(8,128)(2,1)S(1)} %shard_map.104), channel_id=1, source_target_pairs={{0,1},{1,0},{2,3},{3,2},{4,5},{5,4},{6,7},{7,6},{8,9},{9,8},{10,11... | collective-permute-start | bytes 786440 | tf_op jit(solution)/shard_map/ppermute | solution.py:508
  45.8 3.0 %collective-permute-start.10 = (bf16[256,1024]{1,0:T(8,128)(2,1)S(1)}, bf16[256,1024]{1,0:T(8,128)(2,1)S(1)}, u32[]{:S(2)}, u32[]{:S(2)}) collective-permute-start(bf16[256,1024]{1,0:T(8,128)(2,1)S(1)} %collective-permute-done.9.part_ref), channel_id=1, source_target_pairs={{0,2},{2,0},{4,6},{6,4},{8,10},{10,8},{12,14},{14,12},{16,18},{18,... | collective-permute-start | bytes 1572872 | tf_op jit(solution)/shard_map/ppermute | solution.py:508
  48.8 4.8 %copy-start.9 = (bf16[256,1024]{1,0:T(8,128)(2,1)S(1)}, bf16[256,1024]{1,0:T(8,128)(2,1)}, u32[]{:S(2)}) copy-start(bf16[256,1024]{1,0:T(8,128)(2,1)} %shard_map.106.mine_ref) | copy-start | bytes 1572868

commit v6 on v5

--- a/solution.py
+++ b/solution.py
@@ -456,33 +456,40 @@
         send_ref[head] = jnp.where(later, both[:dim], both[dim:])
 
 
-def finish_kernel(flags_ref, keep_ref, came_ref, reads_ref, gain_ref, out_ref):
-    count, dim = keep_ref.shape[:2]
-    heads = reads_ref.shape[0]
-    for head, span in enumerate(spans_of(heads, heads * dim)):
-        state = keep_ref[head % count]
-        if count < heads:
-            state = jnp.where(flags_ref[0] == head // count, state, came_ref[head % count])
-        reach = reads_ref[head, :, :dim]
-        rows = reads_ref[head, :, dim:].astype(F32) + dot(reach, state)
-        scale = lax.rsqrt(jnp.mean(rows * rows, 1, keepdims=True) + 1e-5)
-        out_ref[:, span] = (rows * scale * gain_ref[:, span]).astype(BF16)
-
-
-def finish_mine_kernel(flags_ref, keep_ref, came_ref, reads_ref, gain_ref, w_ref, out_ref, normed_ref):
-    finish_kernel(flags_ref, keep_ref, came_ref, reads_ref, gain_ref, normed_ref)
-    out_ref[...] = dot(normed_ref[...], w_ref[...]).astype(BF16)
-
-
-def hold_kernel(bit_ref, part_ref, rest_ref, whole_ref):
-    rows = part_ref.shape[0]
-    later = bit_ref[0] == 1
-    whole_ref[:rows] = jnp.where(later, rest_ref[...], part_ref[...])
-    whole_ref[rows:] = jnp.where(later, part_ref[...], rest_ref[...])
-
-
-def output_kernel(theirs_ref, w_ref, mine_ref, out_ref):
-    theirs = dot(theirs_ref[...], w_ref[...]).astype(BF16).astype(F32)
+def normed_rows(state, reads, gain):
+    dim = state.shape[0]
+    rows = reads[:, dim:].astype(F32) + dot(reads[:, :dim], state)
+    scale = lax.rsqrt(jnp.mean(rows * rows, 1, keepdims=True) + 1e-5)
+    return (rows * scale * gain).astype(BF16)
+
+
+def finish_kernel(side, bit_ref, state_ref, reads_ref, gain_ref, out_ref):
+    count = state_ref.shape[0]
+    own = bit_ref[0] if side == 0 else 1 - bit_ref[0]
+    first = own * count if count < reads_ref.shape[0] else 0
+    for head, span in enumerate(spans_of(count, out_ref.shape[1])):
+        out_ref[:, span] = normed_rows(
+            state_ref[head], reads_ref[first + head], gain_ref[first + head]
+        )
+
+
+def finish_mine_kernel(
+    bit_ref, keep_ref, came_ref, reads_ref, gain_ref, w_ref, out_ref, normed_ref
+):
+    size = normed_ref.shape[2]
+    total = None
+    for side, state_ref in enumerate((keep_ref, came_ref)):
+        finish_kernel(side, bit_ref, state_ref, reads_ref, gain_ref, normed_ref.at[side])
+        own = bit_ref[0] if side == 0 else 1 - bit_ref[0]
+        rows = w_ref[pl.ds(pl.multiple_of(own * size, size), size)]
+        each = dot(normed_ref[side], rows)
+        total = each if total is None else total + each
+    out_ref[...] = total.astype(BF16)
+
+
+def output_kernel(own_ref, other_ref, w_own_ref, w_other_ref, mine_ref, out_ref):
+    total = dot(own_ref[...], w_own_ref[...]) + dot(other_ref[...], w_other_ref[...])
+    theirs = total.astype(BF16).astype(F32)
     out_ref[...] = (mine_ref[...].astype(F32) + theirs).astype(BF16)
 
 
@@ -519,7 +526,9 @@
     me_seq = lax.axis_index("seq")
     ahead = [(i, i + 1) for i in range(shards - 1)]
 
-    if groups == 2:
+    kept = heads // 2 if heads % 2 == 0 else heads
+    lean = groups == 2 and kept < heads
+    if lean:
         rows = tokens.shape[0]
         swap = [(0, 1), (1, 0)]
         early = tokens
@@ -539,9 +548,8 @@
         head, tail = early[:HALO], early[rows - HALO :]
         swapped = jnp.zeros((), jnp.int32)
 
-    gain = norm_gain.reshape(1, columns)
+    gain = norm_gain.reshape(heads, 1, dim)
     pair_shape = (heads, dim, 2 * dim)
-    kept = heads // 2 if heads % 2 == 0 else heads
     kept_shape = (kept,) + pair_shape[1:]
     levels = shards.bit_length() - 1
     bits = [((me_seq >> level) & 1).astype(jnp.int32).reshape(1) for level in range(levels)]
@@ -580,7 +588,7 @@
                 scalars=[swapped],
             )[0]
             came, path, late = together(came, path, late)
-            if groups == 2:
+            if lean:
                 came, part = together(came, part)
                 part = shift(part, "head", swap)
         elif level == 2:
@@ -603,7 +611,7 @@
         )[0]
         if level == 0:
             own, came, send = together(own, came, send)
-            if groups == 2:
+            if lean:
                 w_sent, send = together(w_out, send)
                 part = half_rows(w_sent, bits[0])
             path = call(
@@ -621,37 +629,40 @@
         [came, path],
         scalars=[bits[0], bits[levels - 1]],
     )
-    came = shift(send, "seq", [(i, i ^ 1) for i in range(shards)]) if kept < heads else send
-    gone = call(
-        finish_kernel,
-        [((rows, columns), BF16)],
-        [keep, came, late, gain],
-        scalars=[bits[0]],
-    )[0]
-    if groups == 2:
-        theirs = shift(gone, "head", swap)
+    states = [keep]
+    if kept < heads:
+        states.append(shift(send, "seq", [(i, i ^ 1) for i in range(shards)]))
+
+    def finish(side, reads):
+        return call(
+            functools.partial(finish_kernel, side),
+            [((rows, kept * dim), BF16)],
+            [states[side], reads, gain],
+            scalars=[bits[0]],
+        )[0]
+
+    gone = [finish(side, late) for side in range(len(states))]
+    if lean:
+        theirs = [shift(each, "head", swap) for each in gone]
+        early, theirs[0] = together(early, theirs[0])
         mine = call(
             finish_mine_kernel,
             [((rows, width), BF16)],
-            [keep, came, early, gain, w_out],
+            states + [early, gain, w_out],
             scalars=[bits[0]],
-            scratch=[pltpu.VMEM((rows, columns), BF16)],
+            scratch=[pltpu.VMEM((2, rows, kept * dim), BF16)],
             grant=62,
             flops=6 * 10**9,
         )[0]
-        part, gone = together(part, gone)
+        part, *_ = together(part, *gone)
         rest = shift(part, "seq", [(i, i ^ 1) for i in range(shards)])
-        whole = call(hold_kernel, [(w_out.shape, BF16)], [part, rest], scalars=[bits[0]])[0]
-        theirs, whole = together(theirs, whole)
-        return call(output_kernel, [((rows, width), BF16)], [theirs, whole, mine])[0]
-    normed = call(
-        finish_kernel,
-        [((rows, columns), BF16)],
-        [keep, came, early, gain],
-        scalars=[bits[0]],
-    )[0]
+        return call(output_kernel, [((rows, width), BF16)], theirs + [part, rest, mine])[0]
+    here = [finish(side, early) for side in range(len(states))]
+    normed = [jnp.concatenate(each, 0) for each in zip(here, gone)]
+    if len(normed) > 1:
+        normed = [jnp.where(bits[0] == side, normed[0], normed[1]) for side in range(2)]
     product = jnp.dot(
-        jnp.concatenate([normed, gone], 0), w_out, preferred_element_type=F32
+        jnp.concatenate(normed, 1), w_out, preferred_element_type=F32
     ).astype(BF16)
     return lax.psum_scatter(product, "head", scatter_dimension=0, tiled=True)
 

time: 55.2 us -> 54.5 us (0.987)
  waiting for transfers between devices: 11.3 us -> 7.96 us
  starting transfers between devices: 17 us -> 18.4 us
  local copies, waits for them, and re-layouts: 4.2 us -> 5.22 us
    ppermute x11 -> x12, waiting for transfers between devices: 11.3 us -> 7.96 us  [shift(): return lax.ppermute(block, axes, pairs)]
    ppermute x11 -> x12, starting transfers between devices: 17 us -> 18.4 us  [shift(): return lax.ppermute(block, axes, pairs)]
    unnamed x32, local copies, waits for them, and re-layouts: 4.2 us -> 5.22 us
  transfers between devices with their start and end apart: 11 -> 12, of which waited for: 6 -> 6; matrix products, arithmetic and copies ran while one was open for 0% -> 0% of each run, Pallas kernels for 27% -> 27%
where the time goes in v6:
time: 54.5 us; the launch traced here: 54.1 us
  Pallas kernels  22.2 us (41%)
  starting transfers between devices  18.4 us (34%)
  waiting for transfers between devices  7.96 us (15%)
  local copies, waits for them, and re-layouts  5.22 us (10%)
    pallas_call x16, Pallas kernels, call(): pl.pallas_call(kernel, out_shape=[jax.ShapeDtypeStruct(shape, dtype) for...  20.3 us
    ppermute x12, starting transfers between devices, shift(): return lax.ppermute(block, axes, pairs)  18.4 us
    ppermute x12, waiting for transfers between devices, shift(): return lax.ppermute(block, axes, pairs)  7.96 us
    unnamed x32, local copies, waits for them, and re-layouts  5.22 us
    pallas_call x1, Pallas kernels, half_rows(): pl.pallas_call(half_kernel, grid_spec=pltpu.PrefetchScalarGridSpec(num_sc...  1.87 us
  transfers between devices with their start and end apart: 12, of which 6 were waited for; matrix products, arithmetic and copies ran while one was open for 0% of the time, Pallas kernels for 27%

profile of v6, /device:TPU:0, one launch (start us, length us, event | category | flops | bytes accessed | tf_op | source)
XLA Modules:
  0.0 54.1 jit_solution(8485667360252887246)
XLA Ops:
  0.0 3.0 %collective-permute-start = (bf16[256,1024]{1,0:T(8,128)(2,1)}, bf16[256,1024]{1,0:T(8,128)(2,1)S(1)}, u32[]{:S(2)}, u32[]{:S(2)}) collective-permute-start(bf16[256,1024]{1,0:T(8,128)(2,1)} %x_ref.3), channel_id=1, source_target_pairs={{0,1},{1,0},{2,3},{3,2},{4,5},{5,4},{6,7},{7,6},{8,9},{9,8},{10,11... | collective-permute-start | bytes 1572872 | tf_op jit(solution)/shard_map/ppermute | solution.py:515
  3.0 1.1 %copy-done.4 = bf16[256,1024]{1,0:T(8,128)(2,1)S(1)} copy-done((bf16[256,1024]{1,0:T(8,128)(2,1)S(1)}, bf16[256,1024]{1,0:T(8,128)(2,1)}, u32[]{:S(2)}) %copy-start.4) | copy-done | bytes 524312
  4.1 1.6 %collective-permute-start.2 = (bf16[16,1024]{1,0:T(8,128)(2,1)S(1)}, bf16[16,1024]{1,0:T(8,128)(2,1)S(1)}, u32[]{:S(2)}, u32[]{:S(2)}) collective-permute-start(bf16[16,1024]{1,0:T(8,128)(2,1)S(1)} %get-tuple-element.40.tail_ref), channel_id=1, source_target_pairs={{0,2},{2,4},{4,6},{6,8},{8,10},{10,12},{12,14},{14,16},{16,18},{18... | collective-permute-start | bytes 98312 | tf_op jit(solution)/shard_map/ppermute | solution.py:515
  5.7 2.3 %collective-permute-start.1 = (bf16[16,1024]{1,0:T(8,128)(2,1)S(1)}, bf16[16,1024]{1,0:T(8,128)(2,1)S(1)}, u32[]{:S(2)}, u32[]{:S(2)}) collective-permute-start(bf16[16,1024]{1,0:T(8,128)(2,1)S(1)} %get-tuple-element.40.tail_ref), channel_id=1, source_target_pairs={{0,1},{1,2},{2,3},{3,4},{4,5},{5,6},{6,7},{7,8},{8,9},{9,10},{10,1... | collective-permute-start | bytes 98312 | tf_op jit(solution)/shard_map/ppermute | solution.py:515
  8.0 0.0 copy-done.1
  8.1 0.0 copy-start.3
  8.1 1.2 %copy-done.3 = bf16[1024,512]{1,0:T(8,128)(2,1)S(1)} copy-done((bf16[1024,512]{1,0:T(8,128)(2,1)S(1)}, bf16[1024,512]{1,0:T(8,128)(2,1)}, u32[]{:S(2)}) %copy-start.3) | copy-done | bytes 1048600
  9.3 5.9 %shard_map.92 = (f32[4,128,256]{2,1,0:T(8,128)S(1)}, bf16[4,256,256]{2,1,0:T(8,128)(2,1)S(1)}) custom-call(f32[4]{0:T(128)S(1)} %copy-done.15, bf16[256,1024]{1,0:T(8,128)(2,1)S(1)} %copy-done.5, bf16[1024,512]{1,0:T(8,128)(2,1)S(1)} %copy-done, bf16[1024,512]{1,0:T(8,128)(2,1)S(1)} %copy-done.1, bf16[1024,512]{1,0:T(8,128)(2,1)S(1)} %copy-done.3, ...), custom_call_target="tpu_custom_call" | custom-call | flops 10000000 | bytes 100000 | tf_op jit(solution)/shard_map/pallas_call | solution.py:499
  15.2 0.8 %copy-done.7 = bf16[4,256,256]{2,1,0:T(8,128)(2,1)} copy-done((bf16[4,256,256]{2,1,0:T(8,128)(2,1)}, bf16[4,256,256]{2,1,0:T(8,128)(2,1)S(1)}, u32[]{:S(2)}) %copy-start.7) | copy-done | bytes 524312
  16.0 0.0 collective-permute-done.2.behind_ref
  16.0 0.0 collective-permute-done.1.halo_ref
  16.0 0.0 collective-permute-done.x_ref
  16.0 0.0 copy-done.2
  16.0 6.1 %shard_map.93 = (bf16[2,128,256]{2,1,0:T(8,128)(2,1)S(1)}, bf16[2,128,256]{2,1,0:T(8,128)(2,1)S(1)}, f32[4,256]{1,0:T(4,128)S(1)}, bf16[4,784,256]{2,1,0:T(8,128)(2,1)S(1)}) custom-call(s32[1]{0:T(128)} %bitcast.swapped_ref, s32[1]{0:T(128)} %bitcast.1.bit_ref.flags_ref, f32[4]{0:T(128)S(1)} %copy-done.15, bf16[256,1024]{1,0:T(8,128)(2,1)S(1)} %collective-permute-done.x_ref, ...), custom_call_target="tpu_custom_call" | custom-call | flops 10000000 | bytes 100000 | tf_op jit(solution)/shard_map/pallas_call | solution.py:499
  22.1 2.0 %collective-permute-start.3 = (bf16[2,128,256]{2,1,0:T(8,128)(2,1)S(1)}, bf16[2,128,256]{2,1,0:T(8,128)(2,1)S(1)}, u32[]{:S(2)}, u32[]{:S(2)}) collective-permute-start(bf16[2,128,256]{2,1,0:T(8,128)(2,1)S(1)} %get-tuple-element.43), channel_id=1, source_target_pairs={{0,2},{2,0},{4,6},{6,4},{8,10},{10,8},{12,14},{14,12},{16,18},{18,... | collective-permute-start | bytes 393224 | tf_op jit(solution)/shard_map/ppermute | solution.py:515
  24.2 1.0 %collective-permute-done.3.other_ref = bf16[2,128,256]{2,1,0:T(8,128)(2,1)S(1)} collective-permute-done((bf16[2,128,256]{2,1,0:T(8,128)(2,1)S(1)}, bf16[2,128,256]{2,1,0:T(8,128)(2,1)S(1)}, u32[]{:S(2)}, u32[]{:S(2)}) %collective-permute-start.3) | collective-permute-done | bytes 131104 | tf_op jit(solution)/shard_map/ppermute | solution.py:515
  25.1 0.2 shard_map.94.own_ref
  25.3 1.6 %collective-permute-start.4 = (bf16[2,128,256]{2,1,0:T(8,128)(2,1)S(1)}, bf16[2,128,256]{2,1,0:T(8,128)(2,1)S(1)}, u32[]{:S(2)}, u32[]{:S(2)}) collective-permute-start(bf16[2,128,256]{2,1,0:T(8,128)(2,1)S(1)} %shard_map.94.own_ref), channel_id=1, source_target_pairs={{0,4},{2,6},{4,0},{6,2},{8,12},{10,14},{12,8},{14,10},{16,20},{18,... | collective-permute-start | bytes 393224 | tf_op jit(solution)/shard_map/ppermute | solution.py:515
  27.0 1.7 %shard_map.96.reads_ref = bf16[4,256,256]{2,1,0:T(8,128)(2,1)S(1)} custom-call(s32[1]{0:T(128)} %bitcast.swapped_ref, f32[4,256]{1,0:T(4,128)S(1)} %get-tuple-element.48.norm_ref, bf16[4,784,256]{2,1,0:T(8,128)(2,1)S(1)} %get-tuple-element.49.held_ref), custom_call_target="tpu_custom_call" | custom-call | flops 10000000 | bytes 100000 | tf_op jit(solution)/shard_map/pallas_call | solution.py:499
  28.6 1.9 %shard_map.97 = bf16[256,1024]{1,0:T(8,128)(2,1)} custom-call(s32[1]{0:T(128)} %bitcast.1.bit_ref.flags_ref, bf16[512,1024]{1,0:T(8,128)(2,1)} %w_ref.2), custom_call_target="tpu_custom_call" | custom-call | flops 10000000 | bytes 100000 | tf_op jit(solution)/shard_map/pallas_call | solution.py:252
  30.5 0.6 %collective-permute-done.4.other_ref.came_ref = bf16[2,128,256]{2,1,0:T(8,128)(2,1)S(1)} collective-permute-done((bf16[2,128,256]{2,1,0:T(8,128)(2,1)S(1)}, bf16[2,128,256]{2,1,0:T(8,128)(2,1)S(1)}, u32[]{:S(2)}, u32[]{:S(2)}) %collective-permute-start.4) | collective-permute-done | bytes 131104 | tf_op jit(solution)/shard_map/ppermute | solution.py:515
  31.1 1.5 %collective-permute-start.10 = (bf16[256,1024]{1,0:T(8,128)(2,1)}, bf16[256,1024]{1,0:T(8,128)(2,1)S(1)}, u32[]{:S(2)}, u32[]{:S(2)}) collective-permute-start(bf16[256,1024]{1,0:T(8,128)(2,1)} %shard_map.97), channel_id=1, source_target_pairs={{0,1},{1,0},{2,3},{3,2},{4,5},{5,4},{6,7},{7,6},{8,9},{9,8},{10,11... | collective-permute-start | bytes 1572872 | tf_op jit(solution)/shard_map/ppermute | solution.py:515
  32.6 0.2 shard_map.98.own_ref
  32.8 1.6 %collective-permute-start.5 = (bf16[2,128,256]{2,1,0:T(8,128)(2,1)S(1)}, bf16[2,128,256]{2,1,0:T(8,128)(2,1)S(1)}, u32[]{:S(2)}, u32[]{:S(2)}) collective-permute-start(bf16[2,128,256]{2,1,0:T(8,128)(2,1)S(1)} %shard_map.98.own_ref), channel_id=1, source_target_pairs={{0,8},{2,10},{4,12},{6,14},{8,0},{10,2},{12,4},{14,6},{16,24},{18,... | collective-permute-start | bytes 393224 | tf_op jit(solution)/shard_map/ppermute | solution.py:515
  34.4 1.0 %copy-done.8 = bf16[4,256,256]{2,1,0:T(8,128)(2,1)S(1)} copy-done((bf16[4,256,256]{2,1,0:T(8,128)(2,1)S(1)}, bf16[4,256,256]{2,1,0:T(8,128)(2,1)}, u32[]{:S(2)}) %copy-start.8) | copy-done | bytes 524312
  35.5 0.7 %shard_map.100.reads_ref = bf16[4,256,256]{2,1,0:T(8,128)(2,1)S(1)} custom-call(s32[1]{0:T(128)} %bitcast.swapped_ref, bf16[4,784,256]{2,1,0:T(8,128)(2,1)S(1)} %get-tuple-element.49.held_ref, bf16[4,256,256]{2,1,0:T(8,128)(2,1)S(1)} %copy-done.8), custom_call_target="tpu_custom_call" | custom-call | flops 10000000 | bytes 100000 | tf_op jit(solution)/shard_map/pallas_call | solution.py:499
  36.2 0.0 copy-start.14
  36.2 0.2 shard_map.99.path_ref
  36.4 1.4 %collective-permute-done.5.other_ref.came_ref = bf16[2,128,256]{2,1,0:T(8,128)(2,1)S(1)} collective-permute-done((bf16[2,128,256]{2,1,0:T(8,128)(2,1)S(1)}, bf16[2,128,256]{2,1,0:T(8,128)(2,1)S(1)}, u32[]{:S(2)}, u32[]{:S(2)}) %collective-permute-start.5) | collective-permute-done | bytes 131104 | tf_op jit(solution)/shard_map/ppermute | solution.py:515
  37.8 0.2 shard_map.101
  38.0 2.7 %collective-permute-start.6 = (bf16[2,128,128]{2,1,0:T(8,128)(2,1)S(1)}, bf16[2,128,128]{2,1,0:T(8,128)(2,1)S(1)}, u32[]{:S(2)}, u32[]{:S(2)}) collective-permute-start(bf16[2,128,128]{2,1,0:T(8,128)(2,1)S(1)} %shard_map.101), channel_id=1, source_target_pairs={{0,16},{2,18},{4,20},{6,22},{8,24},{10,26},{12,28},{14,30},{16,0},... | collective-permute-start | bytes 196616 | tf_op jit(solution)/shard_map/ppermute | solution.py:515
  40.7 0.2 shard_map.102.path_ref
  40.9 2.4 %collective-permute-done.6.state_ref = bf16[2,128,128]{2,1,0:T(8,128)(2,1)S(1)} collective-permute-done((bf16[2,128,128]{2,1,0:T(8,128)(2,1)S(1)}, bf16[2,128,128]{2,1,0:T(8,128)(2,1)S(1)}, u32[]{:S(2)}, u32[]{:S(2)}) %collective-permute-start.6) | collective-permute-done | bytes 65568 | tf_op jit(solution)/shard_map/ppermute | solution.py:515
  43.2 0.2 shard_map.103
  43.5 0.3 shard_map.104
  43.8 0.6 %collective-permute-start.7 = (bf16[256,256]{1,0:T(8,128)(2,1)S(1)}, bf16[256,256]{1,0:T(8,128)(2,1)S(1)}, u32[]{:S(2)}, u32[]{:S(2)}) collective-permute-start(bf16[256,256]{1,0:T(8,128)(2,1)S(1)} %shard_map.104), channel_id=1, source_target_pairs={{0,1},{1,0},{2,3},{3,2},{4,5},{5,4},{6,7},{7,6},{8,9},{9,8},{10,11... | collective-permute-start | bytes 393224 | tf_op jit(solution)/shard_map/ppermute | solution.py:515
  44.4 0.0 collective-permute-start.8
  44.4 1.3 %collective-permute-done.8.state_ref.came_ref = bf16[2,128,128]{2,1,0:T(8,128)(2,1)S(1)} collective-permute-done((bf16[2,128,128]{2,1,0:T(8,128)(2,1)S(1)}, bf16[2,128,128]{2,1,0:T(8,128)(2,1)S(1)}, u32[]{:S(2)}, u32[]{:S(2)}) %collective-permute-start.8) | collective-permute-done | bytes 65568 | tf_op jit(solution)/shard_map/ppermute | solution.py:515
  45.7 0.3 shard_map.105
  46.0 1.5 %collective-permute-start.9 = (bf16[256,256]{1,0:T(8,128)(2,1)S(1)}, bf16[256,256]{1,0:T(8,128)(2,1)S(1)}, u32[]{:S(2)}, u32[]{:S(2)}) collective-permute-start(bf16[256,256]{1,0:T(8,128)(2,1)S(1)} %shard_map.105), channel_id=1, source_target_pairs={{0,1},{1,0},{2,3},{3,2},{4,5},{5,4},{6,7},{7,6},{8,9},{9,8},{10,11... | collective-permute-start | bytes 393224 | tf_op jit(solution)/shard_map/ppermute | solution.py:515
  47.5 1.3 %collective-permute-done.7.own_ref = bf16[256,256]{1,0:T(8,128)(2,1)S(1)} collective-permute-done((bf16[256,256]{1,0:T(8,128)(2,1)S(1)}, bf16[256,256]{1,0:T(8,128)(2,1)S(1)}, u32[]{:S(2)}, u32[]{:S(2)}) %collective-permute-start.7) | collective-permute-done | bytes 131104 | tf_op jit(solution)/shard_map/ppermute | solution.py:515
  48.8 0.0 collective-permute-done.10.w_own_ref
  48.8 0.0 collective-permute-start.11
  48.8 3.0 %shard_map.106.mine_ref = bf16[256,1024]{1,0:T(8,128)(2,1)} custom-call(s32[1]{0:T(128)} %bitcast.1.bit_ref.flags_ref, bf16[2,128,128]{2,1,0:T(8,128)(2,1)} %copy-done.11, bf16[2,128,128]{2,1,0:T(8,128)(2,1)} %copy-done.12, bf16[4,256,256]{2,1,0:T(8,128)(2,1)} %copy-done.6, f32[4,1,128]{2,1,0:T(1,128)} %bitcast.9, bf16[512,1024]{1,0:T(8,128)(2,1)} %w_ref.2), custom_call_target="tpu_custom_call" | custom-call | flops 6000000000 | bytes 100000 | tf_op jit(solution)/shard_map/pallas_call | solution.py:499
  51.8 0.0 collective-permute-done.9.other_ref
  51.8 0.0 collective-permute-done.11.w_other_ref
  51.8 1.0 %copy-done.9 = bf16[256,1024]{1,0:T(8,128)(2,1)S(1)} copy-done((bf16[256,1024]{1,0:T(8,128)(2,1)S(1)}, bf16[256,1024]{1,0:T(8,128)(2,1)}, u32[]{:S(2)}) %copy-start.9) | copy-done | bytes 524312
  52.9 1.2 %shard_map.107 = bf16[256,1024]{1,0:T(8,128)(2,1)} custom-call(bf16[256,256]{1,0:T(8,128)(2,1)S(1)} %collective-permute-done.7.own_ref, bf16[256,256]{1,0:T(8,128)(2,1)S(1)} %collective-permute-done.9.other_ref, bf16[256,1024]{1,0:T(8,128)(2,1)S(1)} %collective-permute-done.10.w_own_ref, bf16[256,1024]{1,0:T(8,128)(2,1)S(1)} %collective-permute-done.11.w_other_ref, ...), custom_call_target="tpu_custom_call" | custom-call | flops 10000000 | bytes 100000 | tf_op jit(solution)/shard_map/pallas_call | solution.py:499
  (25 shorter events, 0.1 us)
Async XLA Ops:
  0.0 8.0 %copy-start.1 = (bf16[1024,512]{1,0:T(8,128)(2,1)S(1)}, bf16[1024,512]{1,0:T(8,128)(2,1)}, u32[]{:S(2)}) copy-start(bf16[1024,512]{1,0:T(8,128)(2,1)} %wk_ref.3) | copy-start | bytes 3145732
  0.0 8.0 %copy-start = (bf16[1024,512]{1,0:T(8,128)(2,1)S(1)}, bf16[1024,512]{1,0:T(8,128)(2,1)}, u32[]{:S(2)}) copy-start(bf16[1024,512]{1,0:T(8,128)(2,1)} %wq_ref.3) | copy-start | bytes 3145732
  0.0 16.0 %collective-permute-start = (bf16[256,1024]{1,0:T(8,128)(2,1)}, bf16[256,1024]{1,0:T(8,128)(2,1)S(1)}, u32[]{:S(2)}, u32[]{:S(2)}) collective-permute-start(bf16[256,1024]{1,0:T(8,128)(2,1)} %x_ref.3), channel_id=1, source_target_pairs={{0,1},{1,0},{2,3},{3,2},{4,5},{5,4},{6,7},{7,6},{8,9},{9,8},{10,11... | collective-permute-start | bytes 1572872 | tf_op jit(solution)/shard_map/ppermute | solution.py:515
  3.0 1.1 %copy-start.4 = (bf16[256,1024]{1,0:T(8,128)(2,1)S(1)}, bf16[256,1024]{1,0:T(8,128)(2,1)}, u32[]{:S(2)}) copy-start(bf16[256,1024]{1,0:T(8,128)(2,1)} %x_ref.3) | copy-start | bytes 1572868
  4.0 4.0 %copy-start.5 = (bf16[256,1024]{1,0:T(8,128)(2,1)S(1)}, bf16[256,1024]{1,0:T(8,128)(2,1)}, u32[]{:S(2)}) copy-start(bf16[256,1024]{1,0:T(8,128)(2,1)} %x_ref.3) | copy-start | bytes 1572868
  4.0 4.0 %copy-start.10 = (f32[3,4,512]{2,1,0:T(4,128)S(1)}, f32[3,4,512]{2,1,0:T(4,128)}, u32[]{:S(2)}) copy-start(f32[3,4,512]{2,1,0:T(4,128)} %conv_ref.3) | copy-start | bytes 73732
  4.1 4.0 %copy-start.13 = (bf16[1024,4]{0,1:T(4,128)(2,1)S(1)}, bf16[1024,4]{0,1:T(4,128)(2,1)}, u32[]{:S(2)}) copy-start(bf16[1024,4]{0,1:T(4,128)(2,1)} %param.13) | copy-start | bytes 24580
  4.1 4.0 %copy-start.15 = (f32[4]{0:T(128)S(1)}, f32[4]{0:T(128)}, u32[]{:S(2)}) copy-start(f32[4]{0:T(128)} %bias_ref.3) | copy-start | bytes 52
  4.1 11.9 %collective-permute-start.2 = (bf16[16,1024]{1,0:T(8,128)(2,1)S(1)}, bf16[16,1024]{1,0:T(8,128)(2,1)S(1)}, u32[]{:S(2)}, u32[]{:S(2)}) collective-permute-start(bf16[16,1024]{1,0:T(8,128)(2,1)S(1)} %get-tuple-element.40.tail_ref), channel_id=1, source_target_pairs={{0,2},{2,4},{4,6},{6,8},{8,10},{10,12},{12,14},{14,16},{16,18},{18... | collective-permute-start | bytes 98312 | tf_op jit(solution)/shard_map/ppermute | solution.py:515
  5.7 10.3 %collective-permute-start.1 = (bf16[16,1024]{1,0:T(8,128)(2,1)S(1)}, bf16[16,1024]{1,0:T(8,128)(2,1)S(1)}, u32[]{:S(2)}, u32[]{:S(2)}) collective-permute-start(bf16[16,1024]{1,0:T(8,128)(2,1)S(1)} %get-tuple-element.40.tail_ref), channel_id=1, source_target_pairs={{0,1},{1,2},{2,3},{3,4},{4,5},{5,6},{6,7},{7,8},{8,9},{9,10},{10,1... | collective-permute-start | bytes 98312 | tf_op jit(solution)/shard_map/ppermute | solution.py:515
  8.1 1.2 %copy-start.3 = (bf16[1024,512]{1,0:T(8,128)(2,1)S(1)}, bf16[1024,512]{1,0:T(8,128)(2,1)}, u32[]{:S(2)}) copy-start(bf16[1024,512]{1,0:T(8,128)(2,1)} %wv_ref.3) | copy-start | bytes 3145732
  9.3 6.7 %copy-start.2 = (bf16[1024,512]{1,0:T(8,128)(2,1)S(1)}, bf16[1024,512]{1,0:T(8,128)(2,1)}, u32[]{:S(2)}) copy-start(bf16[1024,512]{1,0:T(8,128)(2,1)} %wk_ref.3) | copy-start | bytes 3145732
  15.2 0.8 %copy-start.7 = (bf16[4,256,256]{2,1,0:T(8,128)(2,1)}, bf16[4,256,256]{2,1,0:T(8,128)(2,1)S(1)}, u32[]{:S(2)}) copy-start(bf16[4,256,256]{2,1,0:T(8,128)(2,1)S(1)} %get-tuple-element.57.early_ref) | copy-start | bytes 1572868
  22.1 3.0 %collective-permute-start.3 = (bf16[2,128,256]{2,1,0:T(8,128)(2,1)S(1)}, bf16[2,128,256]{2,1,0:T(8,128)(2,1)S(1)}, u32[]{:S(2)}, u32[]{:S(2)}) collective-permute-start(bf16[2,128,256]{2,1,0:T(8,128)(2,1)S(1)} %get-tuple-element.43), channel_id=1, source_target_pairs={{0,2},{2,0},{4,6},{6,4},{8,10},{10,8},{12,14},{14,12},{16,18},{18,... | collective-permute-start | bytes 393224 | tf_op jit(solution)/shard_map/ppermute | solution.py:515
  25.3 5.8 %collective-permute-start.4 = (bf16[2,128,256]{2,1,0:T(8,128)(2,1)S(1)}, bf16[2,128,256]{2,1,0:T(8,128)(2,1)S(1)}, u32[]{:S(2)}, u32[]{:S(2)}) collective-permute-start(bf16[2,128,256]{2,1,0:T(8,128)(2,1)S(1)} %shard_map.94.own_ref), channel_id=1, source_target_pairs={{0,4},{2,6},{4,0},{6,2},{8,12},{10,14},{12,8},{14,10},{16,20},{18,... | collective-permute-start | bytes 393224 | tf_op jit(solution)/shard_map/ppermute | solution.py:515
  31.1 17.7 %collective-permute-start.10 = (bf16[256,1024]{1,0:T(8,128)(2,1)}, bf16[256,1024]{1,0:T(8,128)(2,1)S(1)}, u32[]{:S(2)}, u32[]{:S(2)}) collective-permute-start(bf16[256,1024]{1,0:T(8,128)(2,1)} %shard_map.97), channel_id=1, source_target_pairs={{0,1},{1,0},{2,3},{3,2},{4,5},{5,4},{6,7},{7,6},{8,9},{9,8},{10,11... | collective-permute-start | bytes 1572872 | tf_op jit(solution)/shard_map/ppermute | solution.py:515
  32.8 5.0 %collective-permute-start.5 = (bf16[2,128,256]{2,1,0:T(8,128)(2,1)S(1)}, bf16[2,128,256]{2,1,0:T(8,128)(2,1)S(1)}, u32[]{:S(2)}, u32[]{:S(2)}) collective-permute-start(bf16[2,128,256]{2,1,0:T(8,128)(2,1)S(1)} %shard_map.98.own_ref), channel_id=1, source_target_pairs={{0,8},{2,10},{4,12},{6,14},{8,0},{10,2},{12,4},{14,6},{16,24},{18,... | collective-permute-start | bytes 393224 | tf_op jit(solution)/shard_map/ppermute | solution.py:515
  34.4 1.0 %copy-start.8 = (bf16[4,256,256]{2,1,0:T(8,128)(2,1)S(1)}, bf16[4,256,256]{2,1,0:T(8,128)(2,1)}, u32[]{:S(2)}) copy-start(bf16[4,256,256]{2,1,0:T(8,128)(2,1)} %copy-done.7) | copy-start | bytes 1572868
  36.2 1.8 %copy-start.6 = (bf16[4,256,256]{2,1,0:T(8,128)(2,1)}, bf16[4,256,256]{2,1,0:T(8,128)(2,1)S(1)}, u32[]{:S(2)}) copy-start(bf16[4,256,256]{2,1,0:T(8,128)(2,1)S(1)} %shard_map.100.reads_ref) | copy-start | bytes 1572868
  36.2 7.3 %copy-start.14 = (f32[512]{0:T(512)S(1)}, f32[512]{0:T(512)}, u32[]{:S(2)}) copy-start(f32[512]{0:T(512)} %param.16) | copy-start | bytes 6148
  38.0 5.2 %collective-permute-start.6 = (bf16[2,128,128]{2,1,0:T(8,128)(2,1)S(1)}, bf16[2,128,128]{2,1,0:T(8,128)(2,1)S(1)}, u32[]{:S(2)}, u32[]{:S(2)}) collective-permute-start(bf16[2,128,128]{2,1,0:T(8,128)(2,1)S(1)} %shard_map.101), channel_id=1, source_target_pairs={{0,16},{2,18},{4,20},{6,22},{8,24},{10,26},{12,28},{14,30},{16,0},... | collective-permute-start | bytes 196616 | tf_op jit(solution)/shard_map/ppermute | solution.py:515
  43.4 5.4 %copy-start.11 = (bf16[2,128,128]{2,1,0:T(8,128)(2,1)}, bf16[2,128,128]{2,1,0:T(8,128)(2,1)S(1)}, u32[]{:S(2)}) copy-start(bf16[2,128,128]{2,1,0:T(8,128)(2,1)S(1)} %get-tuple-element.66.state_ref.keep_ref) | copy-start | bytes 196612
  43.8 5.0 %collective-permute-start.7 = (bf16[256,256]{1,0:T(8,128)(2,1)S(1)}, bf16[256,256]{1,0:T(8,128)(2,1)S(1)}, u32[]{:S(2)}, u32[]{:S(2)}) collective-permute-start(bf16[256,256]{1,0:T(8,128)(2,1)S(1)} %shard_map.104), channel_id=1, source_target_pairs={{0,1},{1,0},{2,3},{3,2},{4,5},{5,4},{6,7},{7,6},{8,9},{9,8},{10,11... | collective-permute-start | bytes 393224 | tf_op jit(solution)/shard_map/ppermute | solution.py:515
  44.4 1.3 %collective-permute-start.8 = (bf16[2,128,128]{2,1,0:T(8,128)(2,1)S(1)}, bf16[2,128,128]{2,1,0:T(8,128)(2,1)S(1)}, u32[]{:S(2)}, u32[]{:S(2)}) collective-permute-start(bf16[2,128,128]{2,1,0:T(8,128)(2,1)S(1)} %get-tuple-element.69), channel_id=1, source_target_pairs={{0,2},{2,0},{4,6},{6,4},{8,10},{10,8},{12,14},{14,12},{16,18},{18,... | collective-permute-start | bytes 196616 | tf_op jit(solution)/shard_map/ppermute | solution.py:515
  45.7 3.2 %copy-start.12 = (bf16[2,128,128]{2,1,0:T(8,128)(2,1)}, bf16[2,128,128]{2,1,0:T(8,128)(2,1)S(1)}, u32[]{:S(2)}) copy-start(bf16[2,128,128]{2,1,0:T(8,128)(2,1)S(1)} %collective-permute-done.8.state_ref.came_ref) | copy-start | bytes 196612
  46.0 5.9 %collective-permute-start.9 = (bf16[256,256]{1,0:T(8,128)(2,1)S(1)}, bf16[256,256]{1,0:T(8,128)(2,1)S(1)}, u32[]{:S(2)}, u32[]{:S(2)}) collective-permute-start(bf16[256,256]{1,0:T(8,128)(2,1)S(1)} %shard_map.105), channel_id=1, source_target_pairs={{0,1},{1,0},{2,3},{3,2},{4,5},{5,4},{6,7},{7,6},{8,9},{9,8},{10,11... | collective-permute-start | bytes 393224 | tf_op jit(solution)/shard_map/ppermute | solution.py:515
  48.8 3.0 %collective-permute-start.11 = (bf16[256,1024]{1,0:T(8,128)(2,1)S(1)}, bf16[256,1024]{1,0:T(8,128)(2,1)S(1)}, u32[]{:S(2)}, u32[]{:S(2)}) collective-permute-start(bf16[256,1024]{1,0:T(8,128)(2,1)S(1)} %collective-permute-done.10.w_own_ref), channel_id=1, source_target_pairs={{0,2},{2,0},{4,6},{6,4},{8,10},{10,8},{12,14},{14,12},{16,18},{18,... | collective-permute-start | bytes 1572872 | tf_op jit(solution)/shard_map/ppermute | solution.py:515
  51.8 1.0 %copy-start.9 = (bf16[256,1024]{1,0:T(8,128)(2,1)S(1)}, bf16[256,1024]{1,0:T(8,128)(2,1)}, u32[]{:S(2)}) copy-start(bf16[256,1024]{1,0:T(8,128)(2,1)} %shard_map.106.mine_ref) | copy-start | bytes 1572868

commit v7 on v6

--- a/solution.py
+++ b/solution.py
@@ -485,6 +485,10 @@
         each = dot(normed_ref[side], rows)
         total = each if total is None else total + each
     out_ref[...] = total.astype(BF16)
+
+
+def hold_kernel(w_ref, held_ref):
+    held_ref[...] = w_ref[...]
 
 
 def output_kernel(own_ref, other_ref, w_own_ref, w_other_ref, mine_ref, out_ref):
@@ -644,14 +648,15 @@
     gone = [finish(side, late) for side in range(len(states))]
     if lean:
         theirs = [shift(each, "head", swap) for each in gone]
-        early, theirs[0] = together(early, theirs[0])
+        w_mine, *_ = together(w_out, *gone)
+        w_mine = call(hold_kernel, [(w_out.shape, BF16)], [w_mine], grant=62)[0]
+        early, theirs[0], w_mine = together(early, theirs[0], w_mine)
         mine = call(
             finish_mine_kernel,
             [((rows, width), BF16)],
-            states + [early, gain, w_out],
+            states + [early, gain, w_mine],
             scalars=[bits[0]],
             scratch=[pltpu.VMEM((2, rows, kept * dim), BF16)],
-            grant=62,
             flops=6 * 10**9,
         )[0]
         part, *_ = together(part, *gone)

time: 54.5 us -> 54.3 us (level)
  waiting for transfers between devices: 7.96 us -> 6.64 us
  Pallas kernels: 22.2 us -> 22.9 us
    ppermute x12, waiting for transfers between devices: 7.96 us -> 6.64 us  [shift(): return lax.ppermute(block, axes, pairs)]
    pallas_call x16 -> x17, Pallas kernels: 20.3 us -> 21 us  [call(): pl.pallas_call(kernel, out_shape=[jax.ShapeDtypeStruct(shape, dtype) for...]
    unnamed x32 -> x34, local copies, waits for them, and re-layouts: 5.22 us -> 5.72 us
  transfers between devices with their start and end apart: 12 -> 12, of which waited for: 6 -> 5; matrix products, arithmetic and copies ran while one was open for 0% -> 0% of each run, Pallas kernels for 27% -> 29%
where the time goes in v7:
time: 54.3 us; the launch traced here: 53.9 us
  Pallas kernels  22.9 us (42%)
  starting transfers between devices  18.3 us (34%)
  waiting for transfers between devices  6.64 us (12%)
  local copies, waits for them, and re-layouts  5.72 us (11%)
    pallas_call x17, Pallas kernels, call(): pl.pallas_call(kernel, out_shape=[jax.ShapeDtypeStruct(shape, dtype) for...  21 us
    ppermute x12, starting transfers between devices, shift(): return lax.ppermute(block, axes, pairs)  18.3 us
    ppermute x12, waiting for transfers between devices, shift(): return lax.ppermute(block, axes, pairs)  6.64 us
    unnamed x34, local copies, waits for them, and re-layouts  5.72 us
    pallas_call x1, Pallas kernels, half_rows(): pl.pallas_call(half_kernel, grid_spec=pltpu.PrefetchScalarGridSpec(num_sc...  1.87 us
  transfers between devices with their start and end apart: 12, of which 5 were waited for; matrix products, arithmetic and copies ran while one was open for 0% of the time, Pallas kernels for 29%

profile of v7, /device:TPU:0, one launch (start us, length us, event | category | flops | bytes accessed | tf_op | source)
XLA Modules:
  0.0 53.9 jit_solution(8883843464242880046)
XLA Ops:
  0.0 3.0 %collective-permute-start = (bf16[256,1024]{1,0:T(8,128)(2,1)}, bf16[256,1024]{1,0:T(8,128)(2,1)S(1)}, u32[]{:S(2)}, u32[]{:S(2)}) collective-permute-start(bf16[256,1024]{1,0:T(8,128)(2,1)} %x_ref.3), channel_id=1, source_target_pairs={{0,1},{1,0},{2,3},{3,2},{4,5},{5,4},{6,7},{7,6},{8,9},{9,8},{10,11... | collective-permute-start | bytes 1572872 | tf_op jit(solution)/shard_map/ppermute | solution.py:519
  3.0 1.1 %copy-done.5 = bf16[256,1024]{1,0:T(8,128)(2,1)S(1)} copy-done((bf16[256,1024]{1,0:T(8,128)(2,1)S(1)}, bf16[256,1024]{1,0:T(8,128)(2,1)}, u32[]{:S(2)}) %copy-start.5) | copy-done | bytes 524312
  4.1 1.6 %collective-permute-start.2 = (bf16[16,1024]{1,0:T(8,128)(2,1)S(1)}, bf16[16,1024]{1,0:T(8,128)(2,1)S(1)}, u32[]{:S(2)}, u32[]{:S(2)}) collective-permute-start(bf16[16,1024]{1,0:T(8,128)(2,1)S(1)} %get-tuple-element.42.tail_ref), channel_id=1, source_target_pairs={{0,2},{2,4},{4,6},{6,8},{8,10},{10,12},{12,14},{14,16},{16,18},{18... | collective-permute-start | bytes 98312 | tf_op jit(solution)/shard_map/ppermute | solution.py:519
  5.7 2.3 %collective-permute-start.1 = (bf16[16,1024]{1,0:T(8,128)(2,1)S(1)}, bf16[16,1024]{1,0:T(8,128)(2,1)S(1)}, u32[]{:S(2)}, u32[]{:S(2)}) collective-permute-start(bf16[16,1024]{1,0:T(8,128)(2,1)S(1)} %get-tuple-element.42.tail_ref), channel_id=1, source_target_pairs={{0,1},{1,2},{2,3},{3,4},{4,5},{5,6},{6,7},{7,8},{8,9},{9,10},{10,1... | collective-permute-start | bytes 98312 | tf_op jit(solution)/shard_map/ppermute | solution.py:519
  8.1 0.0 copy-start.3
  8.1 1.2 %copy-done.3 = bf16[1024,512]{1,0:T(8,128)(2,1)S(1)} copy-done((bf16[1024,512]{1,0:T(8,128)(2,1)S(1)}, bf16[1024,512]{1,0:T(8,128)(2,1)}, u32[]{:S(2)}) %copy-start.3) | copy-done | bytes 1048600
  9.3 5.9 %shard_map.92 = (f32[4,128,256]{2,1,0:T(8,128)S(1)}, bf16[4,256,256]{2,1,0:T(8,128)(2,1)S(1)}) custom-call(f32[4]{0:T(128)S(1)} %copy-done.16, bf16[256,1024]{1,0:T(8,128)(2,1)S(1)} %copy-done.6, bf16[1024,512]{1,0:T(8,128)(2,1)S(1)} %copy-done, bf16[1024,512]{1,0:T(8,128)(2,1)S(1)} %copy-done.1, bf16[1024,512]{1,0:T(8,128)(2,1)S(1)} %copy-done.3, ...), custom_call_target="tpu_custom_call" | custom-call | flops 10000000 | bytes 100000 | tf_op jit(solution)/shard_map/pallas_call | solution.py:503
  15.2 0.8 %copy-done.9 = bf16[4,256,256]{2,1,0:T(8,128)(2,1)} copy-done((bf16[4,256,256]{2,1,0:T(8,128)(2,1)}, bf16[4,256,256]{2,1,0:T(8,128)(2,1)S(1)}, u32[]{:S(2)}) %copy-start.9) | copy-done | bytes 524312
  16.0 0.0 collective-permute-done.2.behind_ref
  16.0 0.0 collective-permute-done.1.halo_ref
  16.0 0.0 collective-permute-done.x_ref
  16.0 6.1 %shard_map.93 = (bf16[2,128,256]{2,1,0:T(8,128)(2,1)S(1)}, bf16[2,128,256]{2,1,0:T(8,128)(2,1)S(1)}, f32[4,256]{1,0:T(4,128)S(1)}, bf16[4,784,256]{2,1,0:T(8,128)(2,1)S(1)}) custom-call(s32[1]{0:T(128)} %bitcast.swapped_ref, s32[1]{0:T(128)} %bitcast.1.bit_ref.flags_ref, f32[4]{0:T(128)S(1)} %copy-done.16, bf16[256,1024]{1,0:T(8,128)(2,1)S(1)} %collective-permute-done.x_ref, ...), custom_call_target="tpu_custom_call" | custom-call | flops 10000000 | bytes 100000 | tf_op jit(solution)/shard_map/pallas_call | solution.py:503
  22.1 2.0 %collective-permute-start.3 = (bf16[2,128,256]{2,1,0:T(8,128)(2,1)S(1)}, bf16[2,128,256]{2,1,0:T(8,128)(2,1)S(1)}, u32[]{:S(2)}, u32[]{:S(2)}) collective-permute-start(bf16[2,128,256]{2,1,0:T(8,128)(2,1)S(1)} %get-tuple-element.45), channel_id=1, source_target_pairs={{0,2},{2,0},{4,6},{6,4},{8,10},{10,8},{12,14},{14,12},{16,18},{18,... | collective-permute-start | bytes 393224 | tf_op jit(solution)/shard_map/ppermute | solution.py:519
  24.2 1.0 %collective-permute-done.3.other_ref = bf16[2,128,256]{2,1,0:T(8,128)(2,1)S(1)} collective-permute-done((bf16[2,128,256]{2,1,0:T(8,128)(2,1)S(1)}, bf16[2,128,256]{2,1,0:T(8,128)(2,1)S(1)}, u32[]{:S(2)}, u32[]{:S(2)}) %collective-permute-start.3) | collective-permute-done | bytes 131104 | tf_op jit(solution)/shard_map/ppermute | solution.py:519
  25.1 0.2 shard_map.94.own_ref
  25.3 1.6 %collective-permute-start.4 = (bf16[2,128,256]{2,1,0:T(8,128)(2,1)S(1)}, bf16[2,128,256]{2,1,0:T(8,128)(2,1)S(1)}, u32[]{:S(2)}, u32[]{:S(2)}) collective-permute-start(bf16[2,128,256]{2,1,0:T(8,128)(2,1)S(1)} %shard_map.94.own_ref), channel_id=1, source_target_pairs={{0,4},{2,6},{4,0},{6,2},{8,12},{10,14},{12,8},{14,10},{16,20},{18,... | collective-permute-start | bytes 393224 | tf_op jit(solution)/shard_map/ppermute | solution.py:519
  27.0 1.7 %shard_map.96.reads_ref = bf16[4,256,256]{2,1,0:T(8,128)(2,1)S(1)} custom-call(s32[1]{0:T(128)} %bitcast.swapped_ref, f32[4,256]{1,0:T(4,128)S(1)} %get-tuple-element.50.norm_ref, bf16[4,784,256]{2,1,0:T(8,128)(2,1)S(1)} %get-tuple-element.51.held_ref), custom_call_target="tpu_custom_call" | custom-call | flops 10000000 | bytes 100000 | tf_op jit(solution)/shard_map/pallas_call | solution.py:503
  28.6 1.9 %shard_map.97 = bf16[256,1024]{1,0:T(8,128)(2,1)} custom-call(s32[1]{0:T(128)} %bitcast.1.bit_ref.flags_ref, bf16[512,1024]{1,0:T(8,128)(2,1)} %w_ref.1), custom_call_target="tpu_custom_call" | custom-call | flops 10000000 | bytes 100000 | tf_op jit(solution)/shard_map/pallas_call | solution.py:252
  30.5 0.6 %collective-permute-done.4.other_ref.came_ref = bf16[2,128,256]{2,1,0:T(8,128)(2,1)S(1)} collective-permute-done((bf16[2,128,256]{2,1,0:T(8,128)(2,1)S(1)}, bf16[2,128,256]{2,1,0:T(8,128)(2,1)S(1)}, u32[]{:S(2)}, u32[]{:S(2)}) %collective-permute-start.4) | collective-permute-done | bytes 131104 | tf_op jit(solution)/shard_map/ppermute | solution.py:519
  31.2 1.5 %collective-permute-start.10 = (bf16[256,1024]{1,0:T(8,128)(2,1)}, bf16[256,1024]{1,0:T(8,128)(2,1)S(1)}, u32[]{:S(2)}, u32[]{:S(2)}) collective-permute-start(bf16[256,1024]{1,0:T(8,128)(2,1)} %shard_map.97), channel_id=1, source_target_pairs={{0,1},{1,0},{2,3},{3,2},{4,5},{5,4},{6,7},{7,6},{8,9},{9,8},{10,11... | collective-permute-start | bytes 1572872 | tf_op jit(solution)/shard_map/ppermute | solution.py:519
  32.6 0.2 shard_map.98.own_ref
  32.8 1.6 %collective-permute-start.5 = (bf16[2,128,256]{2,1,0:T(8,128)(2,1)S(1)}, bf16[2,128,256]{2,1,0:T(8,128)(2,1)S(1)}, u32[]{:S(2)}, u32[]{:S(2)}) collective-permute-start(bf16[2,128,256]{2,1,0:T(8,128)(2,1)S(1)} %shard_map.98.own_ref), channel_id=1, source_target_pairs={{0,8},{2,10},{4,12},{6,14},{8,0},{10,2},{12,4},{14,6},{16,24},{18,... | collective-permute-start | bytes 393224 | tf_op jit(solution)/shard_map/ppermute | solution.py:519
  34.4 1.0 %copy-done.10 = bf16[4,256,256]{2,1,0:T(8,128)(2,1)S(1)} copy-done((bf16[4,256,256]{2,1,0:T(8,128)(2,1)S(1)}, bf16[4,256,256]{2,1,0:T(8,128)(2,1)}, u32[]{:S(2)}) %copy-start.10) | copy-done | bytes 524312
  35.5 0.7 %shard_map.100.reads_ref = bf16[4,256,256]{2,1,0:T(8,128)(2,1)S(1)} custom-call(s32[1]{0:T(128)} %bitcast.swapped_ref, bf16[4,784,256]{2,1,0:T(8,128)(2,1)S(1)} %get-tuple-element.51.held_ref, bf16[4,256,256]{2,1,0:T(8,128)(2,1)S(1)} %copy-done.10), custom_call_target="tpu_custom_call" | custom-call | flops 10000000 | bytes 100000 | tf_op jit(solution)/shard_map/pallas_call | solution.py:503
  36.2 0.0 copy-start.15
  36.2 0.2 shard_map.99.path_ref
  36.4 1.4 %collective-permute-done.5.other_ref.came_ref = bf16[2,128,256]{2,1,0:T(8,128)(2,1)S(1)} collective-permute-done((bf16[2,128,256]{2,1,0:T(8,128)(2,1)S(1)}, bf16[2,128,256]{2,1,0:T(8,128)(2,1)S(1)}, u32[]{:S(2)}, u32[]{:S(2)}) %collective-permute-start.5) | collective-permute-done | bytes 131104 | tf_op jit(solution)/shard_map/ppermute | solution.py:519
  37.8 0.2 shard_map.101
  38.0 2.7 %collective-permute-start.6 = (bf16[2,128,128]{2,1,0:T(8,128)(2,1)S(1)}, bf16[2,128,128]{2,1,0:T(8,128)(2,1)S(1)}, u32[]{:S(2)}, u32[]{:S(2)}) collective-permute-start(bf16[2,128,128]{2,1,0:T(8,128)(2,1)S(1)} %shard_map.101), channel_id=1, source_target_pairs={{0,16},{2,18},{4,20},{6,22},{8,24},{10,26},{12,28},{14,30},{16,0},... | collective-permute-start | bytes 196616 | tf_op jit(solution)/shard_map/ppermute | solution.py:519
  40.7 0.2 shard_map.102.path_ref
  40.9 2.4 %collective-permute-done.6.state_ref = bf16[2,128,128]{2,1,0:T(8,128)(2,1)S(1)} collective-permute-done((bf16[2,128,128]{2,1,0:T(8,128)(2,1)S(1)}, bf16[2,128,128]{2,1,0:T(8,128)(2,1)S(1)}, u32[]{:S(2)}, u32[]{:S(2)}) %collective-permute-start.6) | collective-permute-done | bytes 65568 | tf_op jit(solution)/shard_map/ppermute | solution.py:519
  43.2 0.2 shard_map.103
  43.5 1.0 %shard_map.104 = bf16[256,256]{1,0:T(8,128)(2,1)} custom-call(s32[1]{0:T(128)} %bitcast.1.bit_ref.flags_ref, bf16[2,128,128]{2,1,0:T(8,128)(2,1)S(1)} %get-tuple-element.68.state_ref.keep_ref, bf16[4,256,256]{2,1,0:T(8,128)(2,1)S(1)} %shard_map.96.reads_ref, f32[4,1,128]{2,1,0:T(1,128)S(1)} %bitcast.9), custom_call_target="tpu_custom_call" | custom-call | flops 10000000 | bytes 100000 | tf_op jit(solution)/shard_map/pallas_call | solution.py:503
  44.4 0.6 %collective-permute-start.7 = (bf16[256,256]{1,0:T(8,128)(2,1)}, bf16[256,256]{1,0:T(8,128)(2,1)S(1)}, u32[]{:S(2)}, u32[]{:S(2)}) collective-permute-start(bf16[256,256]{1,0:T(8,128)(2,1)} %shard_map.104), channel_id=1, source_target_pairs={{0,1},{1,0},{2,3},{3,2},{4,5},{5,4},{6,7},{7,6},{8,9},{9,8},{10,11... | collective-permute-start | bytes 393224 | tf_op jit(solution)/shard_map/ppermute | solution.py:519
  45.0 0.0 collective-permute-start.8
  45.0 1.3 %collective-permute-done.8.state_ref.came_ref = bf16[2,128,128]{2,1,0:T(8,128)(2,1)S(1)} collective-permute-done((bf16[2,128,128]{2,1,0:T(8,128)(2,1)S(1)}, bf16[2,128,128]{2,1,0:T(8,128)(2,1)S(1)}, u32[]{:S(2)}, u32[]{:S(2)}) %collective-permute-start.8) | collective-permute-done | bytes 65568 | tf_op jit(solution)/shard_map/ppermute | solution.py:519
  46.3 0.3 shard_map.105
  46.6 0.3 copy-done.12
  46.9 1.5 %collective-permute-start.9 = (bf16[256,256]{1,0:T(8,128)(2,1)S(1)}, bf16[256,256]{1,0:T(8,128)(2,1)S(1)}, u32[]{:S(2)}, u32[]{:S(2)}) collective-permute-start(bf16[256,256]{1,0:T(8,128)(2,1)S(1)} %shard_map.105), channel_id=1, source_target_pairs={{0,1},{1,0},{2,3},{3,2},{4,5},{5,4},{6,7},{7,6},{8,9},{9,8},{10,11... | collective-permute-start | bytes 393224 | tf_op jit(solution)/shard_map/ppermute | solution.py:519
  48.3 2.3 %shard_map.106.w_ref = bf16[512,1024]{1,0:T(8,128)(2,1)} custom-call(bf16[512,1024]{1,0:T(8,128)(2,1)} %w_ref.1), custom_call_target="tpu_custom_call" | custom-call | flops 10000000 | bytes 100000 | tf_op jit(solution)/shard_map/pallas_call | solution.py:503
  50.6 0.0 collective-permute-done.7.own_ref
  50.6 0.0 collective-permute-done.10.w_own_ref
  50.6 0.0 collective-permute-start.11
  50.7 1.2 %copy-done.4 = bf16[512,1024]{1,0:T(8,128)(2,1)S(1)} copy-done((bf16[512,1024]{1,0:T(8,128)(2,1)S(1)}, bf16[512,1024]{1,0:T(8,128)(2,1)}, u32[]{:S(2)}) %copy-start.4) | copy-done | bytes 1048600
  51.9 0.7 %shard_map.107.mine_ref = bf16[256,1024]{1,0:T(8,128)(2,1)S(1)} custom-call(s32[1]{0:T(128)} %bitcast.1.bit_ref.flags_ref, bf16[2,128,128]{2,1,0:T(8,128)(2,1)S(1)} %get-tuple-element.68.state_ref.keep_ref, bf16[2,128,128]{2,1,0:T(8,128)(2,1)S(1)} %copy-done.13, bf16[4,256,256]{2,1,0:T(8,128)(2,1)S(1)} %copy-done.8, f32[4,1,128]{2,1,0:T(1,128)S(1)} %bitcast.11, ...), custom_call_target="tpu_custom_call" | custom-call | flops 6000000000 | bytes 100000 | tf_op jit(solution)/shard_map/pallas_call | solution.py:503
  52.6 0.0 collective-permute-done.9.other_ref
  52.6 0.0 collective-permute-done.11.w_other_ref
  52.6 1.3 %shard_map.108 = bf16[256,1024]{1,0:T(8,128)(2,1)} custom-call(bf16[256,256]{1,0:T(8,128)(2,1)S(1)} %collective-permute-done.7.own_ref, bf16[256,256]{1,0:T(8,128)(2,1)S(1)} %collective-permute-done.9.other_ref, bf16[256,1024]{1,0:T(8,128)(2,1)S(1)} %collective-permute-done.10.w_own_ref, bf16[256,1024]{1,0:T(8,128)(2,1)S(1)} %collective-permute-done.11.w_other_ref, ...), custom_call_target="tpu_custom_call" | custom-call | flops 10000000 | bytes 100000 | tf_op jit(solution)/shard_map/pallas_call | solution.py:503
  (28 shorter events, 0.1 us)
Async XLA Ops:
  0.0 8.0 %copy-start.1 = (bf16[1024,512]{1,0:T(8,128)(2,1)S(1)}, bf16[1024,512]{1,0:T(8,128)(2,1)}, u32[]{:S(2)}) copy-start(bf16[1024,512]{1,0:T(8,128)(2,1)} %wk_ref.3) | copy-start | bytes 3145732
  0.0 8.0 %copy-start = (bf16[1024,512]{1,0:T(8,128)(2,1)S(1)}, bf16[1024,512]{1,0:T(8,128)(2,1)}, u32[]{:S(2)}) copy-start(bf16[1024,512]{1,0:T(8,128)(2,1)} %wq_ref.3) | copy-start | bytes 3145732
  0.0 16.0 %collective-permute-start = (bf16[256,1024]{1,0:T(8,128)(2,1)}, bf16[256,1024]{1,0:T(8,128)(2,1)S(1)}, u32[]{:S(2)}, u32[]{:S(2)}) collective-permute-start(bf16[256,1024]{1,0:T(8,128)(2,1)} %x_ref.3), channel_id=1, source_target_pairs={{0,1},{1,0},{2,3},{3,2},{4,5},{5,4},{6,7},{7,6},{8,9},{9,8},{10,11... | collective-permute-start | bytes 1572872 | tf_op jit(solution)/shard_map/ppermute | solution.py:519
  3.0 1.1 %copy-start.5 = (bf16[256,1024]{1,0:T(8,128)(2,1)S(1)}, bf16[256,1024]{1,0:T(8,128)(2,1)}, u32[]{:S(2)}) copy-start(bf16[256,1024]{1,0:T(8,128)(2,1)} %x_ref.3) | copy-start | bytes 1572868
  4.0 4.0 %copy-start.6 = (bf16[256,1024]{1,0:T(8,128)(2,1)S(1)}, bf16[256,1024]{1,0:T(8,128)(2,1)}, u32[]{:S(2)}) copy-start(bf16[256,1024]{1,0:T(8,128)(2,1)} %x_ref.3) | copy-start | bytes 1572868
  4.0 4.0 %copy-start.11 = (f32[3,4,512]{2,1,0:T(4,128)S(1)}, f32[3,4,512]{2,1,0:T(4,128)}, u32[]{:S(2)}) copy-start(f32[3,4,512]{2,1,0:T(4,128)} %conv_ref.3) | copy-start | bytes 73732
  4.1 4.0 %copy-start.14 = (bf16[1024,4]{0,1:T(4,128)(2,1)S(1)}, bf16[1024,4]{0,1:T(4,128)(2,1)}, u32[]{:S(2)}) copy-start(bf16[1024,4]{0,1:T(4,128)(2,1)} %param.13) | copy-start | bytes 24580
  4.1 4.0 %copy-start.16 = (f32[4]{0:T(128)S(1)}, f32[4]{0:T(128)}, u32[]{:S(2)}) copy-start(f32[4]{0:T(128)} %bias_ref.3) | copy-start | bytes 52
  4.1 11.9 %collective-permute-start.2 = (bf16[16,1024]{1,0:T(8,128)(2,1)S(1)}, bf16[16,1024]{1,0:T(8,128)(2,1)S(1)}, u32[]{:S(2)}, u32[]{:S(2)}) collective-permute-start(bf16[16,1024]{1,0:T(8,128)(2,1)S(1)} %get-tuple-element.42.tail_ref), channel_id=1, source_target_pairs={{0,2},{2,4},{4,6},{6,8},{8,10},{10,12},{12,14},{14,16},{16,18},{18... | collective-permute-start | bytes 98312 | tf_op jit(solution)/shard_map/ppermute | solution.py:519
  5.7 10.3 %collective-permute-start.1 = (bf16[16,1024]{1,0:T(8,128)(2,1)S(1)}, bf16[16,1024]{1,0:T(8,128)(2,1)S(1)}, u32[]{:S(2)}, u32[]{:S(2)}) collective-permute-start(bf16[16,1024]{1,0:T(8,128)(2,1)S(1)} %get-tuple-element.42.tail_ref), channel_id=1, source_target_pairs={{0,1},{1,2},{2,3},{3,4},{4,5},{5,6},{6,7},{7,8},{8,9},{9,10},{10,1... | collective-permute-start | bytes 98312 | tf_op jit(solution)/shard_map/ppermute | solution.py:519
  8.1 1.2 %copy-start.3 = (bf16[1024,512]{1,0:T(8,128)(2,1)S(1)}, bf16[1024,512]{1,0:T(8,128)(2,1)}, u32[]{:S(2)}) copy-start(bf16[1024,512]{1,0:T(8,128)(2,1)} %wv_ref.3) | copy-start | bytes 3145732
  9.3 6.7 %copy-start.2 = (bf16[1024,512]{1,0:T(8,128)(2,1)S(1)}, bf16[1024,512]{1,0:T(8,128)(2,1)}, u32[]{:S(2)}) copy-start(bf16[1024,512]{1,0:T(8,128)(2,1)} %wk_ref.3) | copy-start | bytes 3145732
  15.2 0.8 %copy-start.9 = (bf16[4,256,256]{2,1,0:T(8,128)(2,1)}, bf16[4,256,256]{2,1,0:T(8,128)(2,1)S(1)}, u32[]{:S(2)}) copy-start(bf16[4,256,256]{2,1,0:T(8,128)(2,1)S(1)} %get-tuple-element.59.early_ref) | copy-start | bytes 1572868
  22.1 3.0 %collective-permute-start.3 = (bf16[2,128,256]{2,1,0:T(8,128)(2,1)S(1)}, bf16[2,128,256]{2,1,0:T(8,128)(2,1)S(1)}, u32[]{:S(2)}, u32[]{:S(2)}) collective-permute-start(bf16[2,128,256]{2,1,0:T(8,128)(2,1)S(1)} %get-tuple-element.45), channel_id=1, source_target_pairs={{0,2},{2,0},{4,6},{6,4},{8,10},{10,8},{12,14},{14,12},{16,18},{18,... | collective-permute-start | bytes 393224 | tf_op jit(solution)/shard_map/ppermute | solution.py:519
  25.3 5.8 %collective-permute-start.4 = (bf16[2,128,256]{2,1,0:T(8,128)(2,1)S(1)}, bf16[2,128,256]{2,1,0:T(8,128)(2,1)S(1)}, u32[]{:S(2)}, u32[]{:S(2)}) collective-permute-start(bf16[2,128,256]{2,1,0:T(8,128)(2,1)S(1)} %shard_map.94.own_ref), channel_id=1, source_target_pairs={{0,4},{2,6},{4,0},{6,2},{8,12},{10,14},{12,8},{14,10},{16,20},{18,... | collective-permute-start | bytes 393224 | tf_op jit(solution)/shard_map/ppermute | solution.py:519
  31.2 19.5 %collective-permute-start.10 = (bf16[256,1024]{1,0:T(8,128)(2,1)}, bf16[256,1024]{1,0:T(8,128)(2,1)S(1)}, u32[]{:S(2)}, u32[]{:S(2)}) collective-permute-start(bf16[256,1024]{1,0:T(8,128)(2,1)} %shard_map.97), channel_id=1, source_target_pairs={{0,1},{1,0},{2,3},{3,2},{4,5},{5,4},{6,7},{7,6},{8,9},{9,8},{10,11... | collective-permute-start | bytes 1572872 | tf_op jit(solution)/shard_map/ppermute | solution.py:519
  32.8 5.0 %collective-permute-start.5 = (bf16[2,128,256]{2,1,0:T(8,128)(2,1)S(1)}, bf16[2,128,256]{2,1,0:T(8,128)(2,1)S(1)}, u32[]{:S(2)}, u32[]{:S(2)}) collective-permute-start(bf16[2,128,256]{2,1,0:T(8,128)(2,1)S(1)} %shard_map.98.own_ref), channel_id=1, source_target_pairs={{0,8},{2,10},{4,12},{6,14},{8,0},{10,2},{12,4},{14,6},{16,24},{18,... | collective-permute-start | bytes 393224 | tf_op jit(solution)/shard_map/ppermute | solution.py:519
  34.4 1.0 %copy-start.10 = (bf16[4,256,256]{2,1,0:T(8,128)(2,1)S(1)}, bf16[4,256,256]{2,1,0:T(8,128)(2,1)}, u32[]{:S(2)}) copy-start(bf16[4,256,256]{2,1,0:T(8,128)(2,1)} %copy-done.9) | copy-start | bytes 1572868
  36.2 1.8 %copy-start.7 = (bf16[4,256,256]{2,1,0:T(8,128)(2,1)}, bf16[4,256,256]{2,1,0:T(8,128)(2,1)S(1)}, u32[]{:S(2)}) copy-start(bf16[4,256,256]{2,1,0:T(8,128)(2,1)S(1)} %shard_map.100.reads_ref) | copy-start | bytes 1572868
  36.2 7.3 %copy-start.15 = (f32[512]{0:T(512)S(1)}, f32[512]{0:T(512)}, u32[]{:S(2)}) copy-start(f32[512]{0:T(512)} %param.16) | copy-start | bytes 6148
  38.0 5.2 %collective-permute-start.6 = (bf16[2,128,128]{2,1,0:T(8,128)(2,1)S(1)}, bf16[2,128,128]{2,1,0:T(8,128)(2,1)S(1)}, u32[]{:S(2)}, u32[]{:S(2)}) collective-permute-start(bf16[2,128,128]{2,1,0:T(8,128)(2,1)S(1)} %shard_map.101), channel_id=1, source_target_pairs={{0,16},{2,18},{4,20},{6,22},{8,24},{10,26},{12,28},{14,30},{16,0},... | collective-permute-start | bytes 196616 | tf_op jit(solution)/shard_map/ppermute | solution.py:519
  43.5 7.2 %copy-start.8 = (bf16[4,256,256]{2,1,0:T(8,128)(2,1)S(1)}, bf16[4,256,256]{2,1,0:T(8,128)(2,1)}, u32[]{:S(2)}) copy-start(bf16[4,256,256]{2,1,0:T(8,128)(2,1)} %copy-done.7) | copy-start | bytes 1572868
  44.4 6.2 %collective-permute-start.7 = (bf16[256,256]{1,0:T(8,128)(2,1)}, bf16[256,256]{1,0:T(8,128)(2,1)S(1)}, u32[]{:S(2)}, u32[]{:S(2)}) collective-permute-start(bf16[256,256]{1,0:T(8,128)(2,1)} %shard_map.104), channel_id=1, source_target_pairs={{0,1},{1,0},{2,3},{3,2},{4,5},{5,4},{6,7},{7,6},{8,9},{9,8},{10,11... | collective-permute-start | bytes 393224 | tf_op jit(solution)/shard_map/ppermute | solution.py:519
  45.0 1.3 %collective-permute-start.8 = (bf16[2,128,128]{2,1,0:T(8,128)(2,1)S(1)}, bf16[2,128,128]{2,1,0:T(8,128)(2,1)S(1)}, u32[]{:S(2)}, u32[]{:S(2)}) collective-permute-start(bf16[2,128,128]{2,1,0:T(8,128)(2,1)S(1)} %get-tuple-element.70), channel_id=1, source_target_pairs={{0,2},{2,0},{4,6},{6,4},{8,10},{10,8},{12,14},{14,12},{16,18},{18,... | collective-permute-start | bytes 196616 | tf_op jit(solution)/shard_map/ppermute | solution.py:519
  46.3 0.6 %copy-start.12 = (bf16[2,128,128]{2,1,0:T(8,128)(2,1)}, bf16[2,128,128]{2,1,0:T(8,128)(2,1)S(1)}, u32[]{:S(2)}) copy-start(bf16[2,128,128]{2,1,0:T(8,128)(2,1)S(1)} %collective-permute-done.8.state_ref.came_ref) | copy-start | bytes 196612
  46.9 5.8 %collective-permute-start.9 = (bf16[256,256]{1,0:T(8,128)(2,1)S(1)}, bf16[256,256]{1,0:T(8,128)(2,1)S(1)}, u32[]{:S(2)}, u32[]{:S(2)}) collective-permute-start(bf16[256,256]{1,0:T(8,128)(2,1)S(1)} %shard_map.105), channel_id=1, source_target_pairs={{0,1},{1,0},{2,3},{3,2},{4,5},{5,4},{6,7},{7,6},{8,9},{9,8},{10,11... | collective-permute-start | bytes 393224 | tf_op jit(solution)/shard_map/ppermute | solution.py:519
  48.3 2.3 %copy-start.13 = (bf16[2,128,128]{2,1,0:T(8,128)(2,1)S(1)}, bf16[2,128,128]{2,1,0:T(8,128)(2,1)}, u32[]{:S(2)}) copy-start(bf16[2,128,128]{2,1,0:T(8,128)(2,1)} %copy-done.12) | copy-start | bytes 196612
  50.6 2.0 %collective-permute-start.11 = (bf16[256,1024]{1,0:T(8,128)(2,1)S(1)}, bf16[256,1024]{1,0:T(8,128)(2,1)S(1)}, u32[]{:S(2)}, u32[]{:S(2)}) collective-permute-start(bf16[256,1024]{1,0:T(8,128)(2,1)S(1)} %collective-permute-done.10.w_own_ref), channel_id=1, source_target_pairs={{0,2},{2,0},{4,6},{6,4},{8,10},{10,8},{12,14},{14,12},{16,18},{18,... | collective-permute-start | bytes 1572872 | tf_op jit(solution)/shard_map/ppermute | solution.py:519
  50.7 1.2 %copy-start.4 = (bf16[512,1024]{1,0:T(8,128)(2,1)S(1)}, bf16[512,1024]{1,0:T(8,128)(2,1)}, u32[]{:S(2)}) copy-start(bf16[512,1024]{1,0:T(8,128)(2,1)} %shard_map.106.w_ref) | copy-start | bytes 3145732
